TPU v7x, 32 devices: a whole 2x2x4 slice. The times are simulated.
32 devices in a mesh: groups: 2 (over x), loop: 4 (over y, core), cuts: 4 (over z).
Axes of the slice: x: 2, y: 2, z: 4, core: 2. Of those that a mesh axis runs over, the one named last changes fastest.
Arguments:
- vectors: bfloat16 [128, 64, 256], P(('groups', 'loop'), 'cuts'), parts along dimension 0, may hold values from -6 to 6
- near_tiles: bfloat16 [384, 256, 256], P(('groups', 'loop')), parts along dimension 0, may hold values from -0.1875 to 0.1875
- self_tiles: bfloat16 [128, 256, 256], P(('groups', 'loop')), parts along dimension 0, may hold values from -0.1875 to 0.1875
- source_home: int32 [384, 1], P(('groups', 'loop')), parts along dimension 0, may hold values from 0 to 3; in each aligned block of 48 rows (0 to 47, 48 to 95, ...) at most 24 rows name the same one
- target_home: int32 [384, 1], P(('groups', 'loop')), parts along dimension 0, may hold values from 0 to 3; in each aligned block of 48 rows (0 to 47, 48 to 95, ...) at most 24 rows name the same one
- block_local: int32 [384, 2], P(('groups', 'loop')), parts along dimension 0, may hold values from 0 to 15
- column_basis: bfloat16 [128, 64, 256], P(('groups', 'loop')), parts along dimension 0, may hold values from -0.375 to 0.375
- row_basis: bfloat16 [128, 64, 256], P(('groups', 'loop')), parts along dimension 0, may hold values from -0.375 to 0.375
- column_transfer: bfloat16 [128, 64, 64], P(('groups', 'loop')), parts along dimension 0, may hold values from -0.5 to 0.5
- row_transfer: bfloat16 [128, 64, 64], P(('groups', 'loop')), parts along dimension 0, may hold values from -0.75 to 0.75
- coupling: bfloat16 [64, 64, 512], P(('groups', 'loop')), parts along dimension 0, may hold values from -0.25 to 0.25
- far_source: int32 [64, 8], P(('groups', 'loop')), parts along dimension 0, may hold values from 0 to 31
Outputs:
- product: bfloat16 [128, 64, 256], P(('groups', 'loop'), 'cuts'), parts along dimension 0
There are 2 independent parts, one for each index of `groups`. A program takes and returns all parts, laid end to end along the dimension named above; each array names one. Nothing has to cross between parts.
Inputs may be any that keep to these rules, and one draw needn't show every extreme that they name: `source_home`: among the 48 blocks of one index of loop, no value is named by more than 24 of them, and in every draw some value is named by exactly 24 of them on some index. `target_home`: among the 48 blocks of one index of loop, no value is named by more than 24 of them, and in every draw some value is named by exactly 24 of them on some index.
All inputs are finite; a program needn't handle non-finite values.
Results may differ from a plain program's by a relative error of at most 0.0058.
Values may be sent and summed in bfloat16 or wider, within the bound.
No kernel may reach another device: no remote copies, remote signals or barrier semaphores. Data moves between devices by JAX's collectives and lax.ppermute only.
A program may use at most 64 MiB of HBM per device.

v0:
```python
import jax
import jax.numpy as jnp
from jax import lax
from jax.sharding import PartitionSpec as P

ITERS = 2


PRECISE = lax.Precision.HIGHEST


def on_device(
    vectors,
    near_tiles,
    self_tiles,
    source_home,
    target_home,
    block_local,
    column_basis,
    row_basis,
    column_transfer,
    row_transfer,
    coupling,
    far_source,
):
    clusters, vector_count, leaf_size = vectors.shape
    blocks = near_tiles.shape[0]
    rank_size = column_basis.shape[1]
    parents, far_count = far_source.shape
    source_homes = source_home[:, 0]
    target_homes = target_home[:, 0]
    far_flat = far_source.reshape(-1)
    source_global = source_homes * clusters + block_local[:, 0]
    target_global = target_homes * clusters + block_local[:, 1]
    current = vectors
    for step in range(ITERS):
        self_part = jnp.einsum(
            "cvj,cij->cvi", current, self_tiles, preferred_element_type=jnp.float32
        )
        empty_panels = jnp.zeros((blocks, vector_count, leaf_size), jnp.bfloat16)
        shard_rows = lax.all_gather(current, "loop", axis=0, tiled=True)
        inside = jnp.logical_and(source_global >= 0, source_global < shard_rows.shape[0])
        taken_rows = jnp.take(
            shard_rows, jnp.clip(source_global, 0, shard_rows.shape[0] - 1), axis=0
        )
        panels = jnp.where(inside[:, None, None], taken_rows, empty_panels)
        partials = jnp.einsum(
            "bvj,bij->bvi", panels, near_tiles, preferred_element_type=jnp.float32
        )
        selector = (
            target_global[None, :]
            == jnp.arange(clusters * lax.axis_size("loop"), dtype=jnp.int32)[:, None]
        ).astype(jnp.float32)
        near_sum = lax.psum_scatter(
            jnp.einsum("cb,bvi->cvi", selector, partials, precision=PRECISE),
            "loop",
            scatter_dimension=0,
            tiled=True,
        )
        leaf_coeffs = jnp.einsum(
            "cvj,crj->cvr", current, column_basis, preferred_element_type=jnp.float32
        )
        lifted = jnp.einsum(
            "cvr,crs->cvs", leaf_coeffs, column_transfer.astype(jnp.float32), precision=PRECISE
        )
        parent_coeffs = jnp.sum(lifted.reshape(parents, 2, vector_count, rank_size), axis=1).astype(
            jnp.bfloat16
        )
        parent_coeffs = parent_coeffs.reshape(parents, vector_count * rank_size)
        empty_coeffs = jnp.zeros((parents * far_count, vector_count * rank_size), jnp.bfloat16)
        pick_shard_rows = lax.all_gather(parent_coeffs, "loop", axis=0, tiled=True)
        pick_inside = jnp.logical_and(far_flat >= 0, far_flat < pick_shard_rows.shape[0])
        pick_taken_rows = jnp.take(
            pick_shard_rows, jnp.clip(far_flat, 0, pick_shard_rows.shape[0] - 1), axis=0
        )
        gathered = jnp.where(pick_inside[:, None], pick_taken_rows, empty_coeffs)
        parent_out = jnp.einsum(
            "pfvj,pifj->pvi",
            gathered.reshape(parents, far_count, vector_count, rank_size),
            coupling.reshape(parents, rank_size, far_count, rank_size),
            preferred_element_type=jnp.float32,
        )
        leaf_out = jnp.einsum(
            "cvr,crs->cvs",
            jnp.repeat(parent_out, 2, axis=0),
            row_transfer.astype(jnp.float32),
            precision=PRECISE,
        ).astype(jnp.bfloat16)
        far_part = jnp.einsum(
            "cvr,cri->cvi", leaf_out, row_basis, preferred_element_type=jnp.float32
        )
        current = (self_part + near_sum + far_part).astype(jnp.bfloat16)
    return current


def solution(mesh):
    in_specs = (
        P(("groups", "loop"), "cuts", None),
        P(("groups", "loop"), None, None),
        P(("groups", "loop"), None, None),
        P(("groups", "loop"), None),
        P(("groups", "loop"), None),
        P(("groups", "loop"), None),
        P(("groups", "loop"), None, None),
        P(("groups", "loop"), None, None),
        P(("groups", "loop"), None, None),
        P(("groups", "loop"), None, None),
        P(("groups", "loop"), None, None),
        P(("groups", "loop"), None),
    )
    out_specs = P(("groups", "loop"), "cuts", None)
    return jax.shard_map(
        on_device, mesh=mesh, in_specs=in_specs, out_specs=out_specs, check_vma=False
    )
```

profile of v0, /device:TPU:0, one launch (start us, length us, event | category | flops | bytes accessed | tf_op | source)
XLA Modules:
  0.0 107.9 jit_solution(2454271647510905576)
XLA Ops:
  6.5 0.0 reduce-scatter.3.cloned.1.call-start
  6.5 0.8 and_bitcast_fusion
  7.4 0.7 compare_and_fusion.2
  8.1 0.7 add_bitcast_fusion
  8.8 8.9 %all_gather.12 = bf16[64,16,256]{2,1,0:T(8,128)(2,1)S(1)} all-gather(bf16[16,16,256]{2,1,0:T(8,128)(2,1)} %param.16), channel_id=1, replica_groups=mesh['groups'=2,'loop'=4,'cuts'=4] {'loop'}, dimensions={0}, use_global_device_ids=true | all-gather | bytes 655360 | tf_op jit(solution)/shard_map/all_gather | solution.py:41
  17.6 0.6 gather_fusion
  18.2 0.0 copy-start.5
  18.2 0.0 copy-start.1
  18.2 0.0 copy-start.2
  18.3 4.6 %fusion.9 = f32[48,16,256]{2,1,0:T(8,128)S(1)} fusion(bf16[48,256,256]{2,1,0:T(8,128)(2,1)} %param.17, bf16[48,16,256]{2,1,0:T(8,128)(2,1)S(1)} %gather_fusion, pred[48]{0:T(512)(128)(4,1)S(1)} %get-tuple-element.6, pred[48]{0:T(512)(128)(4,1)S(1)} %and_bitcast_fusion), kind=kOutput, calls=%fused_computation.23 | convolution fusion | flops 101056512 | bytes 7471200 | tf_op jit(solution)/shard_map/bvj,bij->bvi/dot_general | solution.py:47
  22.8 1.2 %fusion.6 = f32[64,16,256]{2,0,1:T(8,128)S(1)} fusion(f32[48,16,256]{2,1,0:T(8,128)S(1)} %fusion.9, s32[48]{0:T(128)S(1)} %add_bitcast_fusion), kind=kOutput, calls=%fused_computation.18 | convolution fusion | flops 150998016 | bytes 1835200 | tf_op jit(solution)/shard_map/cb,bvi->cvi/dot_general | solution.py:55
  24.0 1.6 %copy.17 = f32[64,16,256]{2,1,0:T(8,128)} copy(f32[64,16,256]{2,0,1:T(8,128)S(1)} %fusion.6) | data formatting | bytes 2097152 | tf_op jit(solution)/shard_map/cb,bvi->cvi/dot_general | solution.py:55
  25.6 0.0 reduce-scatter.3.cloned.1.call-update
  25.6 0.0 reduce-scatter.5.cloned.1.call-start
  25.7 0.1 and.33
  25.8 0.1 min.29
  25.9 0.2 fusion.27
  26.1 1.3 %bitcast_reduce_fusion.1 = bf16[8,16,64]{2,1,0:T(8,128)(2,1)S(1)} fusion(f32[16,16,64]{2,1,0:T(8,128)S(1)} %fusion.27, bf16[16,64,64]{2,1,0:T(8,128)(2,1)} %param.24), kind=kOutput, calls=%fused_computation.33 | convolution fusion | flops 12591104 | bytes 212992 | tf_op jit(solution)/shard_map/cvr,crs->cvs/dot_general | solution.py:63
  27.4 0.1 convert_element_type.33
  27.5 5.2 %all_gather.13 = bf16[32,1024]{1,0:T(8,128)(2,1)S(1)} all-gather(bf16[8,1024]{1,0:T(8,128)(2,1)S(1)} %convert_element_type.33), channel_id=1, replica_groups=mesh['groups'=2,'loop'=4,'cuts'=4] {'loop'}, dimensions={0}, use_global_device_ids=true | all-gather | bytes 81920 | tf_op jit(solution)/shard_map/all_gather | solution.py:71
  32.8 0.7 gather_fusion.1
  33.5 0.1 select_select_fusion.5
  33.6 0.4 copy-done.8
  34.0 0.9 reshape.95
  34.9 1.7 %reshape.96 = bf16[8,64,8,64]{3,2,1,0:T(8,128)(2,1)S(1)} reshape(bf16[8,64,512]{2,1,0:T(8,128)(2,1)} %param.26) | data formatting | bytes 1048576 | tf_op jit(solution)/shard_map/reshape | solution.py:80
  36.6 1.3 %convolution_bitcast_fusion.1 = f32[8,16,64]{2,1,0:T(8,128)S(1)} fusion(bf16[8,8,16,64]{3,2,1,0:T(8,128)(2,1)} %reshape.95, bf16[8,64,8,64]{3,2,1,0:T(8,128)(2,1)S(1)} %reshape.96), kind=kOutput, calls=%fused_computation.13 | convolution fusion | flops 8388608 | bytes 688128 | tf_op jit(solution)/shard_map/pfvj,pifj->pvi/dot_general | solution.py:77
  37.9 1.0 convolution_convert_fusion.1
  38.9 12.6 %reduce-scatter.3.cloned.1.call-done = f32[16,16,256]{2,1,0:T(8,128)} async-done(((f32[64,16,256]{2,1,0:T(8,128)}), f32[16,16,256]{2,1,0:T(8,128)}) %reduce-scatter.3.cloned.1.call-update) | async-done | bytes 262160 | tf_op jit(solution)/shard_map/reduce_scatter | solution.py:54
  51.5 1.6 %convolution_add_fusion.3 = f32[16,16,256]{2,1,0:T(8,128)S(1)} fusion(f32[16,16,256]{2,1,0:T(8,128)} %reduce-scatter.3.cloned.1.call-done, bf16[16,16,256]{2,1,0:T(8,128)(2,1)S(1)} %copy-done.2, bf16[16,256,256]{2,1,0:T(8,128)(2,1)S(1)} %copy-done), kind=kOutput, calls=%fused_computation.7 | convolution fusion | flops 33619968 | bytes 2752512 | tf_op jit(solution)/shard_map/cvj,cij->cvi/dot_general | solution.py:37
  53.1 1.3 %fusion = bf16[16,16,256]{2,1,0:T(8,128)(2,1)S(1)} fusion(f32[16,16,256]{2,1,0:T(8,128)S(1)} %convolution_add_fusion.3, bf16[16,16,64]{2,1,0:T(8,128)(2,1)} %convolution_convert_fusion.1, bf16[16,64,256]{2,1,0:T(8,128)(2,1)} %param.23), kind=kOutput, calls=%fused_computation.8 | convolution fusion | flops 8519680 | bytes 950272 | tf_op jit(solution)/shard_map/cvr,cri->cvi/dot_general | solution.py:89
  54.4 7.2 %all_gather.14 = bf16[64,16,256]{2,1,0:T(8,128)(2,1)} all-gather(bf16[16,16,256]{2,1,0:T(8,128)(2,1)S(1)} %fusion), channel_id=1, replica_groups=mesh['groups'=2,'loop'=4,'cuts'=4] {'loop'}, dimensions={0}, use_global_device_ids=true | all-gather | bytes 655360 | tf_op jit(solution)/shard_map/all_gather | solution.py:41
  61.6 2.4 %gather_fusion.2 = bf16[48,16,256]{2,1,0:T(8,128)(2,1)} fusion(bf16[64,16,256]{2,1,0:T(8,128)(2,1)} %all_gather.14, s32[1024]{0:T(1024)S(1)} %pad_clamp_fusion.1), kind=kCustom, calls=%fused_computation.2.clone | custom fusion | bytes 786624 | tf_op jit(solution)/shard_map/jit(_take)/gather | solution.py:43
  64.0 4.7 %fusion.8 = f32[48,16,256]{2,1,0:T(8,128)S(1)} fusion(bf16[48,256,256]{2,1,0:T(8,128)(2,1)} %param.17, bf16[48,16,256]{2,1,0:T(8,128)(2,1)} %gather_fusion.2, pred[48]{0:T(512)(128)(4,1)S(1)} %get-tuple-element.6, pred[48]{0:T(512)(128)(4,1)S(1)} %and_bitcast_fusion), kind=kOutput, calls=%fused_computation.21 | convolution fusion | flops 101056512 | bytes 7471200 | tf_op jit(solution)/shard_map/bvj,bij->bvi/dot_general | solution.py:47
  68.7 1.8 %fusion.4 = f32[64,16,256]{2,0,1:T(8,128)S(1)} fusion(f32[48,16,256]{2,1,0:T(8,128)S(1)} %fusion.8, s32[48]{0:T(128)} %copy-done.10), kind=kOutput, calls=%fused_computation.16 | convolution fusion | flops 150998016 | bytes 1835200 | tf_op jit(solution)/shard_map/cb,bvi->cvi/dot_general | solution.py:55
  70.6 1.6 %copy.19 = f32[64,16,256]{2,1,0:T(8,128)} copy(f32[64,16,256]{2,0,1:T(8,128)S(1)} %fusion.4) | data formatting | bytes 2097152 | tf_op jit(solution)/shard_map/cb,bvi->cvi/dot_general | solution.py:55
  72.2 0.0 reduce-scatter.5.cloned.1.call-update
  72.2 1.3 %fusion.28 = f32[16,16,64]{2,1,0:T(8,128)S(1)} fusion(bf16[16,16,256]{2,1,0:T(8,128)(2,1)S(1)} %fusion, bf16[16,64,256]{2,1,0:T(8,128)(2,1)} %param.22), kind=kOutput, calls=%fused_computation.56 | convolution fusion | flops 8388608 | bytes 720896 | tf_op jit(solution)/shard_map/cvj,crj->cvr/dot_general | solution.py:60
  73.5 1.0 bitcast_reduce_fusion
  74.4 0.9 convert_element_type.37
  75.3 5.2 %all_gather.15 = bf16[32,1024]{1,0:T(8,128)(2,1)S(1)} all-gather(bf16[8,1024]{1,0:T(8,128)(2,1)S(1)} %convert_element_type.37), channel_id=1, replica_groups=mesh['groups'=2,'loop'=4,'cuts'=4] {'loop'}, dimensions={0}, use_global_device_ids=true | all-gather | bytes 81920 | tf_op jit(solution)/shard_map/all_gather | solution.py:71
  80.5 0.7 gather_fusion.3
  81.2 0.7 select_select_fusion.4
  82.0 1.1 %reshape.99 = bf16[8,8,16,64]{3,2,1,0:T(8,128)(2,1)S(1)} reshape(bf16[64,1024]{1,0:T(8,128)(2,1)} %select_select_fusion.4) | data formatting | bytes 262144 | tf_op jit(solution)/shard_map/reshape | solution.py:79
  83.1 0.4 convolution_bitcast_fusion
  83.5 1.3 %convolution_convert_fusion = bf16[16,16,64]{2,1,0:T(8,128)(2,1)S(1)} fusion(f32[16,16,64]{2,1,0:T(8,128)S(1)} %bitcast.48, bf16[16,64,64]{2,1,0:T(8,128)(2,1)} %param.25), kind=kOutput, calls=%fused_computation.10 | convolution fusion | flops 12599296 | bytes 229376 | tf_op jit(solution)/shard_map/cvr,crs->cvs/dot_general | solution.py:83
  84.8 12.8 %reduce-scatter.5.cloned.1.call-done = f32[16,16,256]{2,1,0:T(8,128)} async-done(((f32[64,16,256]{2,1,0:T(8,128)}), f32[16,16,256]{2,1,0:T(8,128)}) %reduce-scatter.5.cloned.1.call-update) | async-done | bytes 262160 | tf_op jit(solution)/shard_map/reduce_scatter | solution.py:54
  97.6 1.6 %convolution_add_fusion.1 = f32[16,16,256]{2,1,0:T(8,128)S(1)} fusion(f32[16,16,256]{2,1,0:T(8,128)} %reduce-scatter.5.cloned.1.call-done, bf16[16,16,256]{2,1,0:T(8,128)(2,1)S(1)} %fusion, bf16[16,256,256]{2,1,0:T(8,128)(2,1)S(1)} %copy-done), kind=kOutput, calls=%fused_computation.5 | convolution fusion | flops 33619968 | bytes 2752512 | tf_op jit(solution)/shard_map/cvj,cij->cvi/dot_general | solution.py:37
  99.2 1.9 %fusion.1 = bf16[16,16,256]{2,1,0:T(8,128)(2,1)} fusion(f32[16,16,256]{2,1,0:T(8,128)S(1)} %convolution_add_fusion.1, bf16[16,16,64]{2,1,0:T(8,128)(2,1)S(1)} %convolution_convert_fusion, bf16[16,64,256]{2,1,0:T(8,128)(2,1)} %param.23), kind=kOutput, calls=%fused_computation.9 | convolution fusion | flops 8519680 | bytes 950272 | tf_op jit(solution)/shard_map/cvr,cri->cvi/dot_general | solution.py:89
  (26 shorter events, 0.1 us)
Async XLA Ops:
  6.5 45.0 %copy-start = (bf16[16,256,256]{2,1,0:T(8,128)(2,1)S(1)}, bf16[16,256,256]{2,1,0:T(8,128)(2,1)}, u32[]{:S(2)}) copy-start(bf16[16,256,256]{2,1,0:T(8,128)(2,1)} %param.18) | copy-start | bytes 6291460
  6.5 45.0 %reduce-scatter.3.cloned.1.call-start = ((), (), s32[]{:S(2)}) async-start(), calls=%async_computation.2 | async-start | bytes 1310720 | tf_op jit(solution)/shard_map/reduce_scatter | solution.py:54
  8.8 16.8 %copy-start.10 = (s32[48]{0:T(128)}, s32[48]{0:T(128)S(1)}, u32[]{:S(2)}) copy-start(s32[48]{0:T(128)S(1)} %add_bitcast_fusion) | copy-start | bytes 580
  18.2 7.5 %copy-start.5 = (s32[8,8]{1,0:T(8,128)S(1)}, s32[8,8]{1,0:T(8,128)}, u32[]{:S(2)}) copy-start(s32[8,8]{1,0:T(8,128)} %param.27) | copy-start | bytes 772
  18.2 7.7 %copy-start.1 = (bf16[16,64,256]{2,1,0:T(8,128)(2,1)S(1)}, bf16[16,64,256]{2,1,0:T(8,128)(2,1)}, u32[]{:S(2)}) copy-start(bf16[16,64,256]{2,1,0:T(8,128)(2,1)} %param.22) | copy-start | bytes 1572868
  18.2 7.6 %copy-start.2 = (bf16[16,16,256]{2,1,0:T(8,128)(2,1)S(1)}, bf16[16,16,256]{2,1,0:T(8,128)(2,1)}, u32[]{:S(2)}) copy-start(bf16[16,16,256]{2,1,0:T(8,128)(2,1)} %param.16) | copy-start | bytes 393220
  22.8 15.1 %copy-start.3 = (bf16[16,64,64]{2,1,0:T(8,128)(2,1)S(1)}, bf16[16,64,64]{2,1,0:T(8,128)(2,1)}, u32[]{:S(2)}) copy-start(bf16[16,64,64]{2,1,0:T(8,128)(2,1)} %param.25) | copy-start | bytes 393220
  25.6 72.0 %reduce-scatter.5.cloned.1.call-start = ((), (), s32[]{:S(2)}) async-start(), calls=%async_computation.3 | async-start | bytes 1310720 | tf_op jit(solution)/shard_map/reduce_scatter | solution.py:54
  25.8 7.8 %copy-start.6 = (pred[64]{0:T(512)(128)(4,1)}, pred[64]{0:T(512)(128)(4,1)S(1)}, u32[]{:S(2)}) copy-start(pred[64]{0:T(512)(128)(4,1)S(1)} %and.33) | copy-start | bytes 196
  33.5 0.5 copy-start.8
  64.0 9.4 %copy-start.4 = (bf16[16,64,64]{2,1,0:T(8,128)(2,1)S(1)}, bf16[16,64,64]{2,1,0:T(8,128)(2,1)}, u32[]{:S(2)}) copy-start(bf16[16,64,64]{2,1,0:T(8,128)(2,1)} %param.24) | copy-start | bytes 393220
  64.0 17.2 %copy-start.7 = (pred[64]{0:T(512)(128)(4,1)S(1)}, pred[64]{0:T(512)(128)(4,1)}, u32[]{:S(2)}) copy-start(pred[64]{0:T(512)(128)(4,1)} %copy-done.6) | copy-start | bytes 196
  68.7 12.5 %copy-start.9 = (pred[64]{0:T(512)(128)(4,1)S(1)}, pred[64]{0:T(512)(128)(4,1)}, u32[]{:S(2)}) copy-start(pred[64]{0:T(512)(128)(4,1)} %copy-done.8) | copy-start | bytes 196
Sparse Core Ops, SparseCore 0:
  25.7 25.7 reduce-scatter.2
  72.3 25.2 reduce-scatter.4
where the time goes:
time: 109 us; the launch traced here: 108 us
  blocking collectives  26.6 us (24%)
  matrix products  26.3 us (24%)
  waiting for transfers between devices  25.5 us (23%)
  between operations  13.6 us (12%)
  local copies, waits for them, and re-layouts  12.8 us (12%)
  other arithmetic  3.09 us (3%)
    reduce_scatter x2, waiting for transfers between devices, on_device(): lax.psum_scatter(jnp.einsum('cb,bvi->cvi', selector, partials, precision=...  25.5 us
    all_gather x2, blocking collectives, on_device(): shard_rows = lax.all_gather(current, 'loop', axis=0, tiled=True)  16.1 us
    all_gather x2, blocking collectives, on_device(): pick_shard_rows = lax.all_gather(parent_coeffs, 'loop', axis=0, tiled=True)  10.5 us
    dot_general x2, matrix products, on_device(): jnp.einsum('bvj,bij->bvi', panels, near_tiles, preferred_element_type=jnp...  9.3 us
    dot_general x2, matrix products, on_device(): jnp.einsum('cvr,cri->cvi', leaf_out, row_basis, preferred_element_type=jn...  3.19 us
    dot_general x2, matrix products, on_device(): jnp.einsum('cvj,cij->cvi', current, self_tiles, preferred_element_type=jn...  3.19 us
    dot_general x2, local copies, waits for them, and re-layouts, on_device(): jnp.einsum('cb,bvi->cvi', selector, partials, precision=PRECISE)  3.17 us
    dot_general x2, matrix products, on_device(): jnp.einsum('cb,bvi->cvi', selector, partials, precision=PRECISE)  2.98 us
  transfers between devices with their start and end apart: 2, of which 2 were waited for; matrix products, arithmetic and copies ran while one was open for 14% of the time, Pallas kernels for 0%

commit v1 on v0

v1 whole, which is shorter than its diff:
```python
import functools

import jax
import jax.numpy as jnp
from jax import lax
from jax.experimental import pallas as pl
from jax.experimental.pallas import tpu as pltpu
from jax.sharding import PartitionSpec as P

ITERS = 2
F32, BF16 = jnp.float32, jnp.bfloat16
ROWS_BY_ROWS = (((1,), (1,)), ((), ()))
ROWS_BY_COLUMNS = (((1,), (0,)), ((), ()))
VMEM_LIMIT = 8 * 1024 * 1024


def dot(a, b, dims):
    return lax.dot_general(a, b, dims, preferred_element_type=F32)


def dot_wide(a, b, dims):
    rows = a.shape[0]
    upper = a.astype(BF16).astype(F32)
    halves = jnp.concatenate([upper, a - upper], axis=0).astype(BF16)
    both = dot(halves, b, dims)
    return both[:rows] + both[rows:]


def table_kernel(values, table, sem):
    copy = pltpu.make_async_copy(values, table, sem)
    copy.start()
    copy.wait()


def coeffs_kernel(current, column_basis, column_transfer, coeffs):
    for p in range(coeffs.shape[0]):
        total = None
        for c in (2 * p, 2 * p + 1):
            leaf = dot(current[c], column_basis[c], ROWS_BY_ROWS)
            lifted = dot_wide(leaf, column_transfer[c], ROWS_BY_COLUMNS)
            total = lifted if total is None else total + lifted
        coeffs[p] = jnp.concatenate([total, total], axis=-1).astype(BF16)


def self_kernel(current, self_tiles, self_part):
    for c in range(self_part.shape[0]):
        self_part[c] = dot(current[c], self_tiles[c], ROWS_BY_ROWS)


def near_kernel(panel_count, table, tiles, *refs):
    panels, (send, keep, gathered, products, sums) = refs[:panel_count], refs[panel_count:]
    clusters = panels[0].shape[0]
    blocks = tiles.shape[0]
    for k in range(panel_count):
        gathered[k * clusters : (k + 1) * clusters] = panels[k][...]
    sums[...] = jnp.zeros_like(sums)
    for b in range(blocks):
        products[b] = dot(gathered[table[b]], tiles[b], ROWS_BY_ROWS)
    for b in range(blocks):
        sums[table[blocks + b]] += products[b]
    half = send.shape[0]
    send[...] = sums[:half].astype(BF16)
    keep[...] = sums[half:]


def far_kernel(piece_count, first_entry, table, row_transfer, row_basis, coupling, *refs):
    pieces, (far_part, gathered) = refs[:piece_count], refs[piece_count:]
    parents, vectors, lanes = pieces[0].shape
    far_count = coupling.shape[2] // (lanes // 2)
    for k in range(piece_count):
        gathered[k * parents : (k + 1) * parents] = pieces[k][...]
    lower = lax.broadcasted_iota(jnp.int32, (vectors, lanes), 1) < lanes // 2
    for p in range(parents):
        pairs = []
        for f in range(0, far_count, 2):
            entry = first_entry + p * far_count + f
            first, second = gathered[table[entry]], gathered[table[entry + 1]]
            pairs.append(jnp.where(lower, first.astype(F32), second.astype(F32)).astype(BF16))
        inputs = jnp.concatenate(pairs, axis=-1)
        parent_out = dot(inputs, coupling[p], ROWS_BY_ROWS)
        for c in (2 * p, 2 * p + 1):
            leaf_out = dot_wide(parent_out, row_transfer[c], ROWS_BY_COLUMNS).astype(BF16)
            far_part[c] = dot(leaf_out, row_basis[c], ROWS_BY_COLUMNS)


def in_vmem(*arrays):
    return [pltpu.with_memory_space_constraint(a, pltpu.VMEM) for a in arrays]


VMEM_SPEC = pl.BlockSpec(memory_space=pltpu.VMEM)
SMEM_SPEC = pl.BlockSpec(memory_space=pltpu.SMEM)


def call(kernel, name, out_shape, in_specs, scratch_shapes=(), us=1.0):
    return pl.pallas_call(
        kernel,
        name=name,
        out_shape=out_shape,
        in_specs=in_specs,
        out_specs=jax.tree.map(lambda _: VMEM_SPEC, out_shape),
        scratch_shapes=scratch_shapes,
        compiler_params=pltpu.CompilerParams(vmem_limit_bytes=VMEM_LIMIT),
        cost_estimate=pl.CostEstimate(
            flops=int(us * 1.0e9), bytes_accessed=0, transcendentals=0
        ),
    )


def on_device(
    vectors,
    near_tiles,
    self_tiles,
    source_home,
    target_home,
    block_local,
    column_basis,
    row_basis,
    column_transfer,
    row_transfer,
    coupling,
    far_source,
):
    clusters, vector_count, leaf_size = vectors.shape
    blocks = near_tiles.shape[0]
    rank = column_basis.shape[1]
    parents, far_count = far_source.shape
    count = lax.axis_size("loop")
    columns = count // 2
    sibling = [(i, i ^ 1) for i in range(count)]

    def to_sibling(x):
        return lax.ppermute(x, "loop", sibling)

    def to_column(x, shift):
        return lax.ppermute(x, "loop", [(i, (i + 2 * shift) % count) for i in range(count)])

    def gather(x):
        near = [x] + [to_column(x, s) for s in range(1, columns)]
        return [piece for y in near for piece in (y, to_sibling(y))]

    panel = (clusters, vector_count, leaf_size)
    coeffs_shape = (parents, vector_count, 2 * rank)
    sums_shape = (columns * clusters, vector_count, leaf_size)

    me = lax.axis_index("loop")
    my_column, my_core = me // 2, me % 2

    def piece(home, local, size):
        shift = (my_column - home // 2) % columns
        return (2 * shift + (home % 2 != my_core)) * size + local

    source, target = source_home[:, 0], target_home[:, 0]
    target_place = ((target // 2 - my_column) % columns) * clusters + block_local[:, 1]
    values = jnp.concatenate(
        [
            piece(source, block_local[:, 0], clusters),
            target_place + jnp.where(target % 2 == my_core, columns * clusters, 0),
            piece(far_source // parents, far_source % parents, parents).reshape(-1),
        ]
    )
    table = pl.pallas_call(
        table_kernel,
        name="table",
        out_shape=pltpu.SMEM(values.shape, jnp.int32),
        in_specs=[pl.BlockSpec(memory_space=pl.ANY)],
        out_specs=SMEM_SPEC,
        scratch_shapes=[pltpu.SemaphoreType.DMA],
    )(values)

    def with_table(x):
        return pltpu.with_memory_space_constraint(x, pltpu.SMEM)

    coeffs_call = call(
        coeffs_kernel, "coeffs", jax.ShapeDtypeStruct(coeffs_shape, BF16), [VMEM_SPEC] * 3
    )
    self_call = call(self_kernel, "self", jax.ShapeDtypeStruct(panel, F32), [VMEM_SPEC] * 2)
    near_call = call(
        functools.partial(near_kernel, count),
        "near",
        (jax.ShapeDtypeStruct(sums_shape, BF16), jax.ShapeDtypeStruct(sums_shape, F32)),
        [SMEM_SPEC] + [VMEM_SPEC] * (1 + count),
        [
            pltpu.VMEM((count * clusters, vector_count, leaf_size), BF16),
            pltpu.VMEM((blocks, vector_count, leaf_size), F32),
            pltpu.VMEM((count * clusters, vector_count, leaf_size), F32),
        ],
    )
    far_call = call(
        functools.partial(far_kernel, count, 2 * blocks),
        "far",
        jax.ShapeDtypeStruct(panel, F32),
        [SMEM_SPEC] + [VMEM_SPEC] * (3 + count),
        [pltpu.VMEM((count * parents, vector_count, 2 * rank), BF16)],
    )

    current = vectors
    for step in range(ITERS):
        panels = gather(current)
        coeffs = coeffs_call(*in_vmem(current, column_basis, column_transfer))
        self_part = self_call(*in_vmem(current, self_tiles))
        pieces = gather(coeffs)
        send, keep = near_call(with_table(table), *in_vmem(near_tiles, *panels))
        far_part = far_call(
            with_table(table), *in_vmem(row_transfer, row_basis, coupling, *pieces)
        )
        arrived = to_sibling(send).reshape(columns, *panel)
        keep = keep.reshape(columns, *panel)
        near = keep[0] + arrived[0].astype(F32)
        for s in range(1, columns):
            partial = (keep[s] + arrived[s].astype(F32)).astype(BF16)
            near = near + to_column(partial, s).astype(F32)
        current = (self_part + far_part + near).astype(BF16)
    return current


def solution(mesh):
    in_specs = (
        P(("groups", "loop"), "cuts", None),
        P(("groups", "loop"), None, None),
        P(("groups", "loop"), None, None),
        P(("groups", "loop"), None),
        P(("groups", "loop"), None),
        P(("groups", "loop"), None),
        P(("groups", "loop"), None, None),
        P(("groups", "loop"), None, None),
        P(("groups", "loop"), None, None),
        P(("groups", "loop"), None, None),
        P(("groups", "loop"), None, None),
        P(("groups", "loop"), None),
    )
    out_specs = P(("groups", "loop"), "cuts", None)
    return jax.shard_map(
        on_device, mesh=mesh, in_specs=in_specs, out_specs=out_specs, check_vma=False
    )
```

time: 109 us -> 50 us (0.46)
  blocking collectives: 26.6 us -> 0 us
  matrix products: 26.3 us -> 0 us
  Pallas kernels: 0 us -> 14.8 us
  between operations: 13.6 us -> 0.17 us
  starting transfers between devices: 0.04 us -> 12.8 us
  waiting for transfers between devices: 25.5 us -> 15.2 us
  local copies, waits for them, and re-layouts: 12.8 us -> 3.81 us
    all_gather x4 -> x0, blocking collectives: 26.6 us -> none  [the longest x2 16.1 us: on_device(): shard_rows = lax.all_gather(current, 'loop', axis=0, tiled=True)]
    dot_general x16 -> x0, matrix products: 26.3 us -> none  [the longest x2 9.3 us: on_device(): jnp.einsum('bvj,bij->bvi', panels, near_tiles, preferred_element_type=jnp...]
    reduce_scatter x2 -> x0, waiting for transfers between devices: 25.5 us -> none  [on_device(): lax.psum_scatter(jnp.einsum('cb,bvi->cvi', selector, partials, precision=...]
    ppermute x0 -> x16, waiting for transfers between devices: none -> 15.2 us  [the longest x6 13.8 us: to_column(): lax.ppermute(x, 'loop', [(i, (i + 2 * shift) % count) for i in range(coun...]
    pallas_call x0 -> x9, Pallas kernels: none -> 14.8 us  [the longest x2 4.64 us: on_device(): coeffs = coeffs_call(*in_vmem(current, column_basis, column_transfer))]
    ppermute x0 -> x16, starting transfers between devices: none -> 12.8 us  [the longest x6 11.5 us: to_column(): lax.ppermute(x, 'loop', [(i, (i + 2 * shift) % count) for i in range(coun...]
    gather x4 -> x0, local copies, waits for them, and re-layouts: 4.38 us -> none  [the longest x2 2.96 us: on_device(): jnp.take(shard_rows, jnp.clip(source_global, 0, shard_rows.shape[0] - 1),...]
    reshape x3 -> x1, local copies, waits for them, and re-layouts: 3.66 us -> 0.08 us  [on_device(): piece(far_source // parents, far_source % parents, parents).reshape(-1)]
  transfers between devices with their start and end apart: 2 -> 16, of which waited for: 2 -> 7; matrix products, arithmetic and copies ran while one was open for 14% -> 5% of each run, Pallas kernels for 0% -> 22%
where the time goes in v1:
time: 50 us; the launch traced here: 49.8 us
  waiting for transfers between devices  15.2 us (30%)
  Pallas kernels  14.8 us (30%)
  starting transfers between devices  12.8 us (26%)
  local copies, waits for them, and re-layouts  3.81 us (8%)
  other arithmetic  3.09 us (6%)
    ppermute x6, waiting for transfers between devices, to_column(): lax.ppermute(x, 'loop', [(i, (i + 2 * shift) % count) for i in range(coun...  13.8 us
    ppermute x6, starting transfers between devices, to_column(): lax.ppermute(x, 'loop', [(i, (i + 2 * shift) % count) for i in range(coun...  11.5 us
    pallas_call x2, Pallas kernels, on_device(): coeffs = coeffs_call(*in_vmem(current, column_basis, column_transfer))  4.64 us
    pallas_call x2, Pallas kernels, on_device(): far_call(with_table(table), *in_vmem(row_transfer, row_basis, coupling, *...  4.52 us
    unnamed x20, local copies, waits for them, and re-layouts  3.73 us
    pallas_call x2, Pallas kernels, on_device(): send, keep = near_call(with_table(table), *in_vmem(near_tiles, *panels))  3.63 us
    add x2, other arithmetic, piece(): return (2 * shift + (home % 2 != my_core)) * size + local  1.5 us
    ppermute x10, waiting for transfers between devices, to_sibling(): return lax.ppermute(x, 'loop', sibling)  1.37 us
  transfers between devices with their start and end apart: 16, of which 7 were waited for; matrix products, arithmetic and copies ran while one was open for 5% of the time, Pallas kernels for 22%

profile of v1, /device:TPU:0, one launch (start us, length us, event | category | flops | bytes accessed | tf_op | source)
XLA Modules:
  0.0 49.8 jit_solution(16736465549507757618)
XLA Ops:
  0.0 0.5 collective-permute-start.3
  0.5 2.5 %collective-permute-start.4 = (bf16[16,16,256]{2,1,0:T(8,128)(2,1)}, bf16[16,16,256]{2,1,0:T(8,128)(2,1)S(1)}, u32[]{:S(2)}, u32[]{:S(2)}) collective-permute-start(bf16[16,16,256]{2,1,0:T(8,128)(2,1)} %refs_0_.1), channel_id=1, source_target_pairs={{0,8},{4,12},{8,0},{12,4},{1,9},{5,13},{9,1},{13,5},{2,10},{6,14},... | collective-permute-start | bytes 393224 | tf_op jit(solution)/shard_map/ppermute | solution.py:135
  3.0 0.7 %fusion.5 = s32[8,8]{1,0:T(8,128)S(1)} fusion(s32[8,8]{1,0:T(8,128)} %param.23, s32[]{:T(128)S(6)} %select_n.67, s32[]{:T(128)S(6)} %select_n.63), kind=kLoop, calls=%fused_computation.22 | loop fusion | flops 3584 | bytes 520 | tf_op jit(solution)/shard_map/add | solution.py:150
  3.7 3.7 %collective-permute-done.4.refs_2_ = bf16[16,16,256]{2,1,0:T(8,128)(2,1)S(1)} collective-permute-done((bf16[16,16,256]{2,1,0:T(8,128)(2,1)}, bf16[16,16,256]{2,1,0:T(8,128)(2,1)S(1)}, u32[]{:S(2)}, u32[]{:S(2)}) %collective-permute-start.4) | collective-permute-done | bytes 131104 | tf_op jit(solution)/shard_map/ppermute | solution.py:135
  7.3 0.0 collective-permute-start.5
  7.4 0.8 %bitcast_add_fusion = (s32[48]{0:T(128)S(1)}, s32[48]{0:T(128)S(1)}) fusion(s32[48,2]{0,1:T(2,128)} %param.17, s32[48,1]{0,1:T(1,128)} %param.15, s32[]{:T(128)S(6)} %select_n.67, s32[]{:T(128)S(6)} %select_n.63, s32[48,1]{0,1:T(1,128)} %param.16), kind=kLoop, calls=%fused_computation.55 | loop fusion | flops 3504 | bytes 1160 | tf_op jit(solution)/shard_map/add | solution.py:150
  8.1 0.1 reshape.23
  8.2 0.6 %pad_add_fusion.values = s32[160]{0:T(256)} fusion(s32[64]{0:T(128)S(1)} %reshape.23, s32[48]{0:T(128)S(1)} %get-tuple-element.14, s32[48]{0:T(128)S(1)} %get-tuple-element.13), kind=kLoop, calls=%fused_computation.46 | loop fusion | flops 320 | bytes 1280 | tf_op jit(solution)/shard_map/concatenate | solution.py:154
  8.9 0.7 %table.1 = s32[160]{0:T(256)S(4)} custom-call(s32[160]{0:T(256)} %pad_add_fusion.values), custom_call_target="tpu_custom_call" | custom-call | tf_op jit(solution)/shard_map/table/pallas_call | solution.py:161
  9.6 0.0 collective-permute-done.3.refs_1_
  9.6 0.0 collective-permute-done.5.refs_3_
  9.6 0.0 copy-start
  9.6 2.8 %copy-done = bf16[48,256,256]{2,1,0:T(8,128)(2,1)S(1)} copy-done((bf16[48,256,256]{2,1,0:T(8,128)(2,1)S(1)}, bf16[48,256,256]{2,1,0:T(8,128)(2,1)}, u32[]{:S(2)}) %copy-start) | copy-done | bytes 6291480
  12.4 0.9 %copy-done.1 = bf16[16,16,256]{2,1,0:T(8,128)(2,1)S(1)} copy-done((bf16[16,16,256]{2,1,0:T(8,128)(2,1)S(1)}, bf16[16,16,256]{2,1,0:T(8,128)(2,1)}, u32[]{:S(2)}) %copy-start.1) | copy-done | bytes 131096
  13.3 0.0 copy-start.5
  13.3 0.0 copy-start.7
  13.3 1.8 %near.2 = (bf16[32,16,256]{2,1,0:T(8,128)(2,1)S(1)}, f32[32,16,256]{2,1,0:T(8,128)S(1)}) custom-call(s32[160]{0:T(256)S(4)} %table.1, bf16[48,256,256]{2,1,0:T(8,128)(2,1)S(1)} %copy-done, bf16[16,16,256]{2,1,0:T(8,128)(2,1)S(1)} %copy-done.1, bf16[16,16,256]{2,1,0:T(8,128)(2,1)S(1)} %collective-permute-done.3.refs_1_, ...), custom_call_target="tpu_custom_call" | custom-call | flops 1000000000 | tf_op jit(solution)/shard_map/near/pallas_call | solution.py:202
  15.1 0.0 slice-start
  15.1 0.6 %collective-permute-start.6 = (bf16[32,16,256]{2,1,0:T(8,128)(2,1)S(1)}, bf16[32,16,256]{2,1,0:T(8,128)(2,1)S(1)}, u32[]{:S(2)}, u32[]{:S(2)}) collective-permute-start(bf16[32,16,256]{2,1,0:T(8,128)(2,1)S(1)} %get-tuple-element.10), channel_id=1, source_target_pairs={{0,4},{4,0},{8,12},{12,8},{1,5},{5,1},{9,13},{13,9},{2,6},{6,2},{1... | collective-permute-start | bytes 786440 | tf_op jit(solution)/shard_map/ppermute | solution.py:132
  15.7 2.3 %coeffs.2.refs_0_ = bf16[8,16,128]{2,1,0:T(8,128)(2,1)S(1)} custom-call(bf16[16,16,256]{2,1,0:T(8,128)(2,1)S(1)} %copy-done.1, bf16[16,64,256]{2,1,0:T(8,128)(2,1)S(1)} %copy-done.3, bf16[16,64,64]{2,1,0:T(8,128)(2,1)S(1)} %copy-done.6), custom_call_target="tpu_custom_call" | custom-call | flops 1000000000 | tf_op jit(solution)/shard_map/coeffs/pallas_call | solution.py:199
  18.0 1.8 %collective-permute-start.1 = (bf16[8,16,128]{2,1,0:T(8,128)(2,1)S(1)}, bf16[8,16,128]{2,1,0:T(8,128)(2,1)S(1)}, u32[]{:S(2)}, u32[]{:S(2)}) collective-permute-start(bf16[8,16,128]{2,1,0:T(8,128)(2,1)S(1)} %coeffs.2.refs_0_), channel_id=1, source_target_pairs={{0,8},{4,12},{8,0},{12,4},{1,9},{5,13},{9,1},{13,5},{2,10},{6,14},... | collective-permute-start | bytes 98312 | tf_op jit(solution)/shard_map/ppermute | solution.py:135
  19.8 2.2 %collective-permute-done.1.refs_2_ = bf16[8,16,128]{2,1,0:T(8,128)(2,1)S(1)} collective-permute-done((bf16[8,16,128]{2,1,0:T(8,128)(2,1)S(1)}, bf16[8,16,128]{2,1,0:T(8,128)(2,1)S(1)}, u32[]{:S(2)}, u32[]{:S(2)}) %collective-permute-start.1) | collective-permute-done | bytes 32800 | tf_op jit(solution)/shard_map/ppermute | solution.py:135
  22.0 0.0 slice-start.1
  22.1 1.8 %collective-permute-start.7 = (bf16[16,16,256]{2,1,0:T(8,128)(2,1)S(1)}, bf16[16,16,256]{2,1,0:T(8,128)(2,1)S(1)}, u32[]{:S(2)}, u32[]{:S(2)}) collective-permute-start(bf16[16,16,256]{2,1,0:T(8,128)(2,1)S(1)} %add_convert_fusion.3), channel_id=1, source_target_pairs={{0,8},{4,12},{8,0},{12,4},{1,9},{5,13},{9,1},{13,5},{2,10},{6,14},... | collective-permute-start | bytes 393224 | tf_op jit(solution)/shard_map/ppermute | solution.py:135
  23.9 0.6 %self.2 = f32[16,16,256]{2,1,0:T(8,128)S(1)} custom-call(bf16[16,16,256]{2,1,0:T(8,128)(2,1)S(1)} %copy-done.1, bf16[16,256,256]{2,1,0:T(8,128)(2,1)S(1)} %copy-done.2), custom_call_target="tpu_custom_call" | custom-call | flops 1000000000 | tf_op jit(solution)/shard_map/self/pallas_call | solution.py:200
  24.5 0.0 collective-permute-done.refs_1_
  24.5 0.0 collective-permute-done.2.refs_3_
  24.5 0.0 copy-done.4
  24.6 2.3 %far.2 = f32[16,16,256]{2,1,0:T(8,128)S(1)} custom-call(s32[160]{0:T(256)S(4)} %table.1, bf16[16,64,64]{2,1,0:T(8,128)(2,1)S(1)} %copy-done.7, bf16[16,64,256]{2,1,0:T(8,128)(2,1)S(1)} %copy-done.4, bf16[8,64,512]{2,1,0:T(8,128)(2,1)S(1)} %copy-done.5, bf16[8,16,128]{2,1,0:T(8,128)(2,1)S(1)} %coeffs.2.refs_0_, ...), custom_call_target="tpu_custom_call" | custom-call | flops 1000000000 | tf_op jit(solution)/shard_map/far/pallas_call | solution.py:203
  26.8 1.2 %collective-permute-done.7 = bf16[16,16,256]{2,1,0:T(8,128)(2,1)S(1)} collective-permute-done((bf16[16,16,256]{2,1,0:T(8,128)(2,1)S(1)}, bf16[16,16,256]{2,1,0:T(8,128)(2,1)S(1)}, u32[]{:S(2)}, u32[]{:S(2)}) %collective-permute-start.7) | collective-permute-done | bytes 131104 | tf_op jit(solution)/shard_map/ppermute | solution.py:135
  28.0 0.1 add_convert_fusion.2.current.refs_0_
  28.1 1.8 %collective-permute-start.12 = (bf16[16,16,256]{2,1,0:T(8,128)(2,1)S(1)}, bf16[16,16,256]{2,1,0:T(8,128)(2,1)S(1)}, u32[]{:S(2)}, u32[]{:S(2)}) collective-permute-start(bf16[16,16,256]{2,1,0:T(8,128)(2,1)S(1)} %add_convert_fusion.2.current.refs_0_), channel_id=1, source_target_pairs={{0,8},{4,12},{8,0},{12,4},{1,9},{5,13},{9,1},{13,5},{2,10},{6,14},... | collective-permute-start | bytes 393224 | tf_op jit(solution)/shard_map/ppermute | solution.py:135
  30.0 3.4 %collective-permute-done.12.refs_2_ = bf16[16,16,256]{2,1,0:T(8,128)(2,1)S(1)} collective-permute-done((bf16[16,16,256]{2,1,0:T(8,128)(2,1)S(1)}, bf16[16,16,256]{2,1,0:T(8,128)(2,1)S(1)}, u32[]{:S(2)}, u32[]{:S(2)}) %collective-permute-start.12) | collective-permute-done | bytes 131104 | tf_op jit(solution)/shard_map/ppermute | solution.py:135
  33.3 1.3 %collective-permute-done.13.refs_3_ = bf16[16,16,256]{2,1,0:T(8,128)(2,1)S(1)} collective-permute-done((bf16[16,16,256]{2,1,0:T(8,128)(2,1)S(1)}, bf16[16,16,256]{2,1,0:T(8,128)(2,1)S(1)}, u32[]{:S(2)}, u32[]{:S(2)}) %collective-permute-start.13) | collective-permute-done | bytes 131104 | tf_op jit(solution)/shard_map/ppermute | solution.py:132
  34.7 1.8 %near.3 = (bf16[32,16,256]{2,1,0:T(8,128)(2,1)S(1)}, f32[32,16,256]{2,1,0:T(8,128)S(1)}) custom-call(s32[160]{0:T(256)S(4)} %table.1, bf16[48,256,256]{2,1,0:T(8,128)(2,1)S(1)} %bitcast.31, bf16[16,16,256]{2,1,0:T(8,128)(2,1)S(1)} %add_convert_fusion.2.current.refs_0_, bf16[16,16,256]{2,1,0:T(8,128)(2,1)S(1)} %collective-permute-done.11.refs_1_, ...), custom_call_target="tpu_custom_call" | custom-call | flops 1000000000 | tf_op jit(solution)/shard_map/near/pallas_call | solution.py:202
  36.5 0.2 collective-permute-start.14
  36.7 2.3 %coeffs.3.refs_0_ = bf16[8,16,128]{2,1,0:T(8,128)(2,1)S(1)} custom-call(bf16[16,16,256]{2,1,0:T(8,128)(2,1)S(1)} %add_convert_fusion.2.current.refs_0_, bf16[16,64,256]{2,1,0:T(8,128)(2,1)S(1)} %copy-done.3, bf16[16,64,64]{2,1,0:T(8,128)(2,1)S(1)} %copy-done.6), custom_call_target="tpu_custom_call" | custom-call | flops 1000000000 | tf_op jit(solution)/shard_map/coeffs/pallas_call | solution.py:199
  39.1 1.8 %collective-permute-start.9 = (bf16[8,16,128]{2,1,0:T(8,128)(2,1)S(1)}, bf16[8,16,128]{2,1,0:T(8,128)(2,1)S(1)}, u32[]{:S(2)}, u32[]{:S(2)}) collective-permute-start(bf16[8,16,128]{2,1,0:T(8,128)(2,1)S(1)} %coeffs.3.refs_0_), channel_id=1, source_target_pairs={{0,8},{4,12},{8,0},{12,4},{1,9},{5,13},{9,1},{13,5},{2,10},{6,14},... | collective-permute-start | bytes 98312 | tf_op jit(solution)/shard_map/ppermute | solution.py:135
  40.8 0.1 collective-permute-start.8
  40.9 2.1 %collective-permute-done.9.refs_2_ = bf16[8,16,128]{2,1,0:T(8,128)(2,1)S(1)} collective-permute-done((bf16[8,16,128]{2,1,0:T(8,128)(2,1)S(1)}, bf16[8,16,128]{2,1,0:T(8,128)(2,1)S(1)}, u32[]{:S(2)}, u32[]{:S(2)}) %collective-permute-start.9) | collective-permute-done | bytes 32800 | tf_op jit(solution)/shard_map/ppermute | solution.py:135
  43.0 0.0 collective-permute-done.14
  43.1 1.8 %collective-permute-start.15 = (bf16[16,16,256]{2,1,0:T(8,128)(2,1)S(1)}, bf16[16,16,256]{2,1,0:T(8,128)(2,1)S(1)}, u32[]{:S(2)}, u32[]{:S(2)}) collective-permute-start(bf16[16,16,256]{2,1,0:T(8,128)(2,1)S(1)} %add_convert_fusion.1), channel_id=1, source_target_pairs={{0,8},{4,12},{8,0},{12,4},{1,9},{5,13},{9,1},{13,5},{2,10},{6,14},... | collective-permute-start | bytes 393224 | tf_op jit(solution)/shard_map/ppermute | solution.py:135
  44.9 0.6 %self.3 = f32[16,16,256]{2,1,0:T(8,128)S(1)} custom-call(bf16[16,16,256]{2,1,0:T(8,128)(2,1)S(1)} %add_convert_fusion.2.current.refs_0_, bf16[16,256,256]{2,1,0:T(8,128)(2,1)S(1)} %copy-done.2), custom_call_target="tpu_custom_call" | custom-call | flops 1000000000 | tf_op jit(solution)/shard_map/self/pallas_call | solution.py:200
  45.5 0.0 collective-permute-done.8.refs_1_
  45.5 0.0 collective-permute-done.10.refs_3_
  45.5 2.3 %far.3 = f32[16,16,256]{2,1,0:T(8,128)S(1)} custom-call(s32[160]{0:T(256)S(4)} %table.1, bf16[16,64,64]{2,1,0:T(8,128)(2,1)S(1)} %copy-done.7, bf16[16,64,256]{2,1,0:T(8,128)(2,1)S(1)} %copy-done.4, bf16[8,64,512]{2,1,0:T(8,128)(2,1)S(1)} %copy-done.5, bf16[8,16,128]{2,1,0:T(8,128)(2,1)S(1)} %coeffs.3.refs_0_, ...), custom_call_target="tpu_custom_call" | custom-call | flops 1000000000 | tf_op jit(solution)/shard_map/far/pallas_call | solution.py:203
  47.8 1.2 %collective-permute-done.15 = bf16[16,16,256]{2,1,0:T(8,128)(2,1)S(1)} collective-permute-done((bf16[16,16,256]{2,1,0:T(8,128)(2,1)S(1)}, bf16[16,16,256]{2,1,0:T(8,128)(2,1)S(1)}, u32[]{:S(2)}, u32[]{:S(2)}) %collective-permute-start.15) | collective-permute-done | bytes 131104 | tf_op jit(solution)/shard_map/ppermute | solution.py:135
  49.0 0.8 %add_convert_fusion = bf16[16,16,256]{2,1,0:T(8,128)(2,1)} fusion(bf16[16,16,256]{2,1,0:T(8,128)(2,1)S(1)} %collective-permute-done.15, f32[32,16,256]{2,1,0:T(8,128)S(1)} %get-tuple-element.11, f32[16,16,256]{2,1,0:T(8,128)S(1)} %self.3, f32[16,16,256]{2,1,0:T(8,128)S(1)} %far.3, bf16[32,16,256]{2,1,0:T(8,128)(2,1)S(1)} %collective-permute-done.14), kind=kLoop, calls=%fused_computation | loop fusion | flops 458752 | bytes 1179648 | tf_op jit(solution)/shard_map/convert_element_type | solution.py:212
  (22 shorter events, 0.1 us)
Async XLA Ops:
  0.0 9.6 %collective-permute-start.3 = (bf16[16,16,256]{2,1,0:T(8,128)(2,1)}, bf16[16,16,256]{2,1,0:T(8,128)(2,1)S(1)}, u32[]{:S(2)}, u32[]{:S(2)}) collective-permute-start(bf16[16,16,256]{2,1,0:T(8,128)(2,1)} %refs_0_.1), channel_id=1, source_target_pairs={{0,4},{4,0},{8,12},{12,8},{1,5},{5,1},{9,13},{13,9},{2,6},{6,2},{1... | collective-permute-start | bytes 393224 | tf_op jit(solution)/shard_map/ppermute | solution.py:132
  0.5 6.9 %collective-permute-start.4 = (bf16[16,16,256]{2,1,0:T(8,128)(2,1)}, bf16[16,16,256]{2,1,0:T(8,128)(2,1)S(1)}, u32[]{:S(2)}, u32[]{:S(2)}) collective-permute-start(bf16[16,16,256]{2,1,0:T(8,128)(2,1)} %refs_0_.1), channel_id=1, source_target_pairs={{0,8},{4,12},{8,0},{12,4},{1,9},{5,13},{9,1},{13,5},{2,10},{6,14},... | collective-permute-start | bytes 393224 | tf_op jit(solution)/shard_map/ppermute | solution.py:135
  7.3 2.2 %collective-permute-start.5 = (bf16[16,16,256]{2,1,0:T(8,128)(2,1)S(1)}, bf16[16,16,256]{2,1,0:T(8,128)(2,1)S(1)}, u32[]{:S(2)}, u32[]{:S(2)}) collective-permute-start(bf16[16,16,256]{2,1,0:T(8,128)(2,1)S(1)} %collective-permute-done.4.refs_2_), channel_id=1, source_target_pairs={{0,4},{4,0},{8,12},{12,8},{1,5},{5,1},{9,13},{13,9},{2,6},{6,2},{1... | collective-permute-start | bytes 393224 | tf_op jit(solution)/shard_map/ppermute | solution.py:132
  9.6 2.8 %copy-start = (bf16[48,256,256]{2,1,0:T(8,128)(2,1)S(1)}, bf16[48,256,256]{2,1,0:T(8,128)(2,1)}, u32[]{:S(2)}) copy-start(bf16[48,256,256]{2,1,0:T(8,128)(2,1)} %tiles.3) | copy-start | bytes 18874372
  12.4 0.9 %copy-start.1 = (bf16[16,16,256]{2,1,0:T(8,128)(2,1)S(1)}, bf16[16,16,256]{2,1,0:T(8,128)(2,1)}, u32[]{:S(2)}) copy-start(bf16[16,16,256]{2,1,0:T(8,128)(2,1)} %refs_0_.1) | copy-start | bytes 393220
  13.3 2.4 %copy-start.3 = (bf16[16,64,256]{2,1,0:T(8,128)(2,1)S(1)}, bf16[16,64,256]{2,1,0:T(8,128)(2,1)}, u32[]{:S(2)}) copy-start(bf16[16,64,256]{2,1,0:T(8,128)(2,1)} %column_basis.3) | copy-start | bytes 1572868
  13.3 2.4 %copy-start.6 = (bf16[16,64,64]{2,1,0:T(8,128)(2,1)S(1)}, bf16[16,64,64]{2,1,0:T(8,128)(2,1)}, u32[]{:S(2)}) copy-start(bf16[16,64,64]{2,1,0:T(8,128)(2,1)} %column_transfer.3) | copy-start | bytes 393220
  13.3 10.6 %copy-start.2 = (bf16[16,256,256]{2,1,0:T(8,128)(2,1)S(1)}, bf16[16,256,256]{2,1,0:T(8,128)(2,1)}, u32[]{:S(2)}) copy-start(bf16[16,256,256]{2,1,0:T(8,128)(2,1)} %self_tiles.3) | copy-start | bytes 6291460
  13.3 11.2 %copy-start.4 = (bf16[16,64,256]{2,1,0:T(8,128)(2,1)S(1)}, bf16[16,64,256]{2,1,0:T(8,128)(2,1)}, u32[]{:S(2)}) copy-start(bf16[16,64,256]{2,1,0:T(8,128)(2,1)} %row_basis.3) | copy-start | bytes 1572868
  13.3 11.3 %copy-start.5 = (bf16[8,64,512]{2,1,0:T(8,128)(2,1)S(1)}, bf16[8,64,512]{2,1,0:T(8,128)(2,1)}, u32[]{:S(2)}) copy-start(bf16[8,64,512]{2,1,0:T(8,128)(2,1)} %coupling.3) | copy-start | bytes 1572868
  13.3 11.3 %copy-start.7 = (bf16[16,64,64]{2,1,0:T(8,128)(2,1)S(1)}, bf16[16,64,64]{2,1,0:T(8,128)(2,1)}, u32[]{:S(2)}) copy-start(bf16[16,64,64]{2,1,0:T(8,128)(2,1)} %row_transfer.3) | copy-start | bytes 393220
  15.1 19.6 %slice-start = ((s8[6291456]{0:T(1024)(128)(4,1)}), s8[4194304]{0:T(1024)(128)(4,1)S(1)}, s32[]{:S(2)}) async-start(s8[6291456]{0:T(1024)(128)(4,1)} %bitcast.30), calls=%async_computation | async-start | bytes 8388608
  15.1 6.9 %collective-permute-start.6 = (bf16[32,16,256]{2,1,0:T(8,128)(2,1)S(1)}, bf16[32,16,256]{2,1,0:T(8,128)(2,1)S(1)}, u32[]{:S(2)}, u32[]{:S(2)}) collective-permute-start(bf16[32,16,256]{2,1,0:T(8,128)(2,1)S(1)} %get-tuple-element.10), channel_id=1, source_target_pairs={{0,4},{4,0},{8,12},{12,8},{1,5},{5,1},{9,13},{13,9},{2,6},{6,2},{1... | collective-permute-start | bytes 786440 | tf_op jit(solution)/shard_map/ppermute | solution.py:132
  18.0 4.0 %collective-permute-start.1 = (bf16[8,16,128]{2,1,0:T(8,128)(2,1)S(1)}, bf16[8,16,128]{2,1,0:T(8,128)(2,1)S(1)}, u32[]{:S(2)}, u32[]{:S(2)}) collective-permute-start(bf16[8,16,128]{2,1,0:T(8,128)(2,1)S(1)} %coeffs.2.refs_0_), channel_id=1, source_target_pairs={{0,8},{4,12},{8,0},{12,4},{1,9},{5,13},{9,1},{13,5},{2,10},{6,14},... | collective-permute-start | bytes 98312 | tf_op jit(solution)/shard_map/ppermute | solution.py:135
  19.8 4.7 %collective-permute-start = (bf16[8,16,128]{2,1,0:T(8,128)(2,1)S(1)}, bf16[8,16,128]{2,1,0:T(8,128)(2,1)S(1)}, u32[]{:S(2)}, u32[]{:S(2)}) collective-permute-start(bf16[8,16,128]{2,1,0:T(8,128)(2,1)S(1)} %coeffs.2.refs_0_), channel_id=1, source_target_pairs={{0,4},{4,0},{8,12},{12,8},{1,5},{5,1},{9,13},{13,9},{2,6},{6,2},{1... | collective-permute-start | bytes 98312 | tf_op jit(solution)/shard_map/ppermute | solution.py:132
  22.0 2.5 %collective-permute-start.2 = (bf16[8,16,128]{2,1,0:T(8,128)(2,1)S(1)}, bf16[8,16,128]{2,1,0:T(8,128)(2,1)S(1)}, u32[]{:S(2)}, u32[]{:S(2)}) collective-permute-start(bf16[8,16,128]{2,1,0:T(8,128)(2,1)S(1)} %collective-permute-done.1.refs_2_), channel_id=1, source_target_pairs={{0,4},{4,0},{8,12},{12,8},{1,5},{5,1},{9,13},{13,9},{2,6},{6,2},{1... | collective-permute-start | bytes 98312 | tf_op jit(solution)/shard_map/ppermute | solution.py:132
  22.0 12.7 %slice-start.1 = ((s8[6291456]{0:T(1024)(128)(4,1)}), s8[2097152]{0:T(1024)(128)(4,1)S(1)}, s32[]{:S(2)}) async-start(s8[6291456]{0:T(1024)(128)(4,1)} %bitcast.30), calls=%async_computation.1 | async-start | bytes 4194304
  22.1 6.0 %collective-permute-start.7 = (bf16[16,16,256]{2,1,0:T(8,128)(2,1)S(1)}, bf16[16,16,256]{2,1,0:T(8,128)(2,1)S(1)}, u32[]{:S(2)}, u32[]{:S(2)}) collective-permute-start(bf16[16,16,256]{2,1,0:T(8,128)(2,1)S(1)} %add_convert_fusion.3), channel_id=1, source_target_pairs={{0,8},{4,12},{8,0},{12,4},{1,9},{5,13},{9,1},{13,5},{2,10},{6,14},... | collective-permute-start | bytes 393224 | tf_op jit(solution)/shard_map/ppermute | solution.py:135
  28.1 5.2 %collective-permute-start.12 = (bf16[16,16,256]{2,1,0:T(8,128)(2,1)S(1)}, bf16[16,16,256]{2,1,0:T(8,128)(2,1)S(1)}, u32[]{:S(2)}, u32[]{:S(2)}) collective-permute-start(bf16[16,16,256]{2,1,0:T(8,128)(2,1)S(1)} %add_convert_fusion.2.current.refs_0_), channel_id=1, source_target_pairs={{0,8},{4,12},{8,0},{12,4},{1,9},{5,13},{9,1},{13,5},{2,10},{6,14},... | collective-permute-start | bytes 393224 | tf_op jit(solution)/shard_map/ppermute | solution.py:135
  29.9 3.4 %collective-permute-start.11 = (bf16[16,16,256]{2,1,0:T(8,128)(2,1)S(1)}, bf16[16,16,256]{2,1,0:T(8,128)(2,1)S(1)}, u32[]{:S(2)}, u32[]{:S(2)}) collective-permute-start(bf16[16,16,256]{2,1,0:T(8,128)(2,1)S(1)} %add_convert_fusion.2.current.refs_0_), channel_id=1, source_target_pairs={{0,4},{4,0},{8,12},{12,8},{1,5},{5,1},{9,13},{13,9},{2,6},{6,2},{1... | collective-permute-start | bytes 393224 | tf_op jit(solution)/shard_map/ppermute | solution.py:132
  33.3 1.3 %collective-permute-start.13 = (bf16[16,16,256]{2,1,0:T(8,128)(2,1)S(1)}, bf16[16,16,256]{2,1,0:T(8,128)(2,1)S(1)}, u32[]{:S(2)}, u32[]{:S(2)}) collective-permute-start(bf16[16,16,256]{2,1,0:T(8,128)(2,1)S(1)} %collective-permute-done.12.refs_2_), channel_id=1, source_target_pairs={{0,4},{4,0},{8,12},{12,8},{1,5},{5,1},{9,13},{13,9},{2,6},{6,2},{1... | collective-permute-start | bytes 393224 | tf_op jit(solution)/shard_map/ppermute | solution.py:132
  36.5 6.5 %collective-permute-start.14 = (bf16[32,16,256]{2,1,0:T(8,128)(2,1)S(1)}, bf16[32,16,256]{2,1,0:T(8,128)(2,1)S(1)}, u32[]{:S(2)}, u32[]{:S(2)}) collective-permute-start(bf16[32,16,256]{2,1,0:T(8,128)(2,1)S(1)} %get-tuple-element.12), channel_id=1, source_target_pairs={{0,4},{4,0},{8,12},{12,8},{1,5},{5,1},{9,13},{13,9},{2,6},{6,2},{1... | collective-permute-start | bytes 786440 | tf_op jit(solution)/shard_map/ppermute | solution.py:132
  39.1 4.0 %collective-permute-start.9 = (bf16[8,16,128]{2,1,0:T(8,128)(2,1)S(1)}, bf16[8,16,128]{2,1,0:T(8,128)(2,1)S(1)}, u32[]{:S(2)}, u32[]{:S(2)}) collective-permute-start(bf16[8,16,128]{2,1,0:T(8,128)(2,1)S(1)} %coeffs.3.refs_0_), channel_id=1, source_target_pairs={{0,8},{4,12},{8,0},{12,4},{1,9},{5,13},{9,1},{13,5},{2,10},{6,14},... | collective-permute-start | bytes 98312 | tf_op jit(solution)/shard_map/ppermute | solution.py:135
  40.8 4.7 %collective-permute-start.8 = (bf16[8,16,128]{2,1,0:T(8,128)(2,1)S(1)}, bf16[8,16,128]{2,1,0:T(8,128)(2,1)S(1)}, u32[]{:S(2)}, u32[]{:S(2)}) collective-permute-start(bf16[8,16,128]{2,1,0:T(8,128)(2,1)S(1)} %coeffs.3.refs_0_), channel_id=1, source_target_pairs={{0,4},{4,0},{8,12},{12,8},{1,5},{5,1},{9,13},{13,9},{2,6},{6,2},{1... | collective-permute-start | bytes 98312 | tf_op jit(solution)/shard_map/ppermute | solution.py:132
  43.0 2.5 %collective-permute-start.10 = (bf16[8,16,128]{2,1,0:T(8,128)(2,1)S(1)}, bf16[8,16,128]{2,1,0:T(8,128)(2,1)S(1)}, u32[]{:S(2)}, u32[]{:S(2)}) collective-permute-start(bf16[8,16,128]{2,1,0:T(8,128)(2,1)S(1)} %collective-permute-done.9.refs_2_), channel_id=1, source_target_pairs={{0,4},{4,0},{8,12},{12,8},{1,5},{5,1},{9,13},{13,9},{2,6},{6,2},{1... | collective-permute-start | bytes 98312 | tf_op jit(solution)/shard_map/ppermute | solution.py:132
  43.1 6.0 %collective-permute-start.15 = (bf16[16,16,256]{2,1,0:T(8,128)(2,1)S(1)}, bf16[16,16,256]{2,1,0:T(8,128)(2,1)S(1)}, u32[]{:S(2)}, u32[]{:S(2)}) collective-permute-start(bf16[16,16,256]{2,1,0:T(8,128)(2,1)S(1)} %add_convert_fusion.1), channel_id=1, source_target_pairs={{0,8},{4,12},{8,0},{12,4},{1,9},{5,13},{9,1},{13,5},{2,10},{6,14},... | collective-permute-start | bytes 393224 | tf_op jit(solution)/shard_map/ppermute | solution.py:135

commit v2 on v1

v2 whole, which is shorter than its diff:
```python
import functools

import jax
import jax.numpy as jnp
from jax import lax
from jax.experimental import pallas as pl
from jax.experimental.pallas import tpu as pltpu
from jax.sharding import PartitionSpec as P

ITERS = 2
F32, BF16 = jnp.float32, jnp.bfloat16
ROWS_BY_ROWS = (((1,), (1,)), ((), ()))
ROWS_BY_COLUMNS = (((1,), (0,)), ((), ()))
VMEM_LIMIT = 12 * 1024 * 1024
CHUNKS = 4


def dot(a, b, dims):
    return lax.dot_general(a, b, dims, preferred_element_type=F32)


def dot_wide(a, b, dims):
    rows = a.shape[0]
    upper = a.astype(BF16).astype(F32)
    halves = jnp.concatenate([upper, a - upper], axis=0).astype(BF16)
    both = dot(halves, b, dims)
    return both[:rows] + both[rows:]


def lanes_below(vectors, lanes):
    return lax.broadcasted_iota(jnp.int32, (vectors, lanes), 1) < lanes // 2


def parent_coeffs(current, column_basis, column_transfer, coeffs):
    parents, vectors, lanes = coeffs.shape
    rank, leaf_size = column_basis.shape[1:]
    lower = lanes_below(vectors, lanes)
    leaves = []
    for p in range(parents):
        both = dot(
            current[2 * p : 2 * p + 2].reshape(2 * vectors, leaf_size),
            column_basis[2 * p : 2 * p + 2].reshape(2 * rank, leaf_size),
            ROWS_BY_ROWS,
        )
        leaves.append(jnp.where(lower, both[:vectors], both[vectors:]))
    for p in range(parents):
        transfer = column_transfer[2 * p : 2 * p + 2].reshape(2 * rank, rank)
        total = dot_wide(leaves[p], transfer, ROWS_BY_COLUMNS)
        coeffs[p] = jnp.concatenate([total, total], axis=-1).astype(BF16)


def self_product(current, self_tiles, self_part):
    for c in range(self_part.shape[0]):
        self_part[c] = dot(current[c], self_tiles[c], ROWS_BY_ROWS)


def fill_table(me, columns, clusters, parents, raw, table):
    source_home, target_home, block_local, far_source = raw
    my_column = me // 2
    blocks = source_home.shape[1]

    def around(shift):
        return jnp.where(shift < 0, shift + columns, shift)

    for b in range(blocks):
        home = source_home[0, b]
        shift = around(my_column - home // 2)
        table[b] = (2 * shift + ((home ^ me) & 1)) * clusters + block_local[0, b]
        home = target_home[0, b]
        shift = around(home // 2 - my_column)
        same = 1 - ((home ^ me) & 1)
        table[blocks + b] = (same * columns + shift) * clusters + block_local[1, b]
    far_count = far_source.shape[1]
    for p in range(parents):
        for f in range(far_count):
            home = lax.div(far_source[p, f], parents)
            local = lax.rem(far_source[p, f], parents)
            shift = around(my_column - home // 2)
            entry = 2 * blocks + p * far_count + f
            table[entry] = (2 * shift + ((home ^ me) & 1)) * parents + local


def load_all(sems, *pairs):
    copies = [pltpu.make_async_copy(x, y, sems.at[i]) for i, (x, y) in enumerate(pairs)]
    for copy in copies:
        copy.start()
    return copies


def turn(staged, held, copies):
    each = staged.shape[0] // len(copies)
    for k, copy in enumerate(copies):
        copy.wait()
        for b in range(k * each, (k + 1) * each):
            held[b] = staged[b].T


def tile_pairs(tiles, first, staged):
    each = staged.shape[0] // CHUNKS
    return [
        (tiles.at[pl.ds(first + k * each, each)], staged.at[pl.ds(k * each, each)])
        for k in range(CHUNKS)
    ]


def first_kernel(
    vectors,
    column_basis,
    column_transfer,
    tiles,
    coeffs,
    current,
    basis_held,
    transfer_held,
    held,
    staged,
    sems,
):
    copies = load_all(
        sems,
        (vectors, current),
        (column_basis, basis_held),
        (column_transfer, transfer_held),
        *tile_pairs(tiles, 0, staged),
    )
    for copy in copies[:3]:
        copy.wait()
    parent_coeffs(current, basis_held, transfer_held, coeffs)
    turn(staged, held, copies[3:])


def load_kernel(
    columns,
    clusters,
    source_home,
    target_home,
    block_local,
    far_source,
    tiles,
    held,
    table,
    staged,
    source_smem,
    target_smem,
    local_smem,
    far_smem,
    sems,
):
    raw = (source_smem, target_smem, local_smem, far_smem)
    given = (source_home, target_home, block_local, far_source)
    copies = load_all(sems, *zip(given, raw), *tile_pairs(tiles, held.shape[0], staged))
    for copy in copies[:4]:
        copy.wait()
    fill_table(lax.axis_index("loop"), columns, clusters, far_source.shape[0], raw, table)
    turn(staged, held, copies[4:])


def next_kernel(current, column_basis, column_transfer, coeffs):
    parent_coeffs(current, column_basis, column_transfer, coeffs)


def self_kernel(current, self_tiles, self_part):
    self_product(current, self_tiles, self_part)


def tie_kernel(*refs):
    pass


def near_kernel(panel_count, part_count, table, *refs):
    parts, refs = refs[:part_count], refs[part_count:]
    panels, (send, keep, gathered, products, sums) = refs[:panel_count], refs[-5:]
    row = 0
    for panel in panels:
        gathered[row : row + panel.shape[0]] = panel[...]
        row += panel.shape[0]
    sums[...] = jnp.zeros_like(sums)
    b = 0
    for tiles in parts:
        for k in range(tiles.shape[0]):
            products[b] = dot(gathered[table[b]], tiles[k], ROWS_BY_COLUMNS)
            b += 1
    for k in range(b):
        sums[table[b + k]] += products[k]
    half = send.shape[0]
    send[...] = sums[:half].astype(BF16)
    keep[...] = sums[half:]


def join_kernel(keep, arrived, self_part, far_part, message, sums):
    half = self_part.shape[0]
    other = keep[half:] + arrived[half:].astype(F32)
    own = keep[:half] + arrived[:half].astype(F32) + self_part[...] + far_part[...]
    sums[:half] = own
    sums[half:] = other
    message[:half] = other.astype(BF16)
    message[half:] = own.astype(BF16)


def settle_kernel(sums, message, pair):
    pair[...] = (sums[...] + message[...].astype(F32)).astype(BF16)


def far_products(
    pieces, first_entry, table, row_transfer, row_basis, coupling, gathered, store
):
    row = 0
    for piece in pieces:
        gathered[row : row + piece.shape[0]] = piece[...]
        row += piece.shape[0]
    vectors, lanes = gathered.shape[1:]
    rank, leaf_size = row_basis.shape[1:]
    parents = coupling.shape[0]
    far_count = coupling.shape[2] // rank
    lower = lanes_below(vectors, lanes)
    parent_outs = []
    for p in range(parents):
        pairs = []
        for f in range(0, far_count, 2):
            entry = first_entry + p * far_count + f
            first, second = gathered[table[entry]], gathered[table[entry + 1]]
            pairs.append(jnp.where(lower, first.astype(F32), second.astype(F32)).astype(BF16))
        parent_outs.append(dot(jnp.concatenate(pairs, axis=-1), coupling[p], ROWS_BY_ROWS))
    leaf_outs = []
    for p in range(parents):
        transfer = jnp.concatenate([row_transfer[2 * p], row_transfer[2 * p + 1]], axis=-1)
        leaf_outs.append(dot_wide(parent_outs[p], transfer, ROWS_BY_COLUMNS))
    for p in range(parents):
        zero = jnp.zeros_like(leaf_outs[p])
        stacked = jnp.concatenate(
            [jnp.where(lower, leaf_outs[p], zero), jnp.where(lower, zero, leaf_outs[p])], axis=0
        ).astype(BF16)
        basis = row_basis[2 * p : 2 * p + 2].reshape(2 * rank, leaf_size)
        both = dot(stacked, basis, ROWS_BY_COLUMNS)
        store(2 * p, both.reshape(2, vectors, leaf_size))


def far_kernel(piece_count, first_entry, table, row_transfer, row_basis, coupling, *refs):
    pieces, (far_part, gathered) = refs[:piece_count], refs[piece_count:]

    def store(c, both):
        far_part[c : c + 2] = both

    far_products(
        pieces, first_entry, table, row_transfer, row_basis, coupling, gathered, store
    )


def widen_kernel(keep, arrived, coeffs, beside, message):
    half = keep.shape[0] // 2
    message[:half] = (keep[half:] + arrived[half:].astype(F32)).astype(BF16)
    parents, _, lanes = coeffs.shape
    each = message.shape[2] // (lanes // 2)
    row = half
    for one in (coeffs, beside):
        for p in range(0, parents, each):
            parts = [one[p + k][:, : lanes // 2] for k in range(each)]
            message[row] = jnp.concatenate(parts, axis=-1)
            row += 1


def last_kernel(
    first_entry,
    table,
    row_transfer,
    row_basis,
    coupling,
    coeffs,
    beside,
    self_part,
    keep,
    arrived,
    message,
    product,
    gathered,
    unpacked,
):
    clusters = self_part.shape[0]
    _, vectors, lanes = coeffs.shape
    width = lanes // 2
    each = message.shape[2] // width
    for row in range(clusters, message.shape[0]):
        for k in range(each):
            part = message[row][:, k * width : (k + 1) * width]
            unpacked[(row - clusters) * each + k] = jnp.concatenate([part, part], axis=-1)

    def store(c, both):
        near = keep[c : c + 2] + arrived[c : c + 2].astype(F32) + message[c : c + 2].astype(F32)
        product[c : c + 2] = (self_part[c : c + 2] + both + near).astype(BF16)

    far_products(
        (coeffs, beside, unpacked),
        first_entry,
        table,
        row_transfer,
        row_basis,
        coupling,
        gathered,
        store,
    )


def in_vmem(*arrays):
    return [pltpu.with_memory_space_constraint(a, pltpu.VMEM) for a in arrays]


def in_hbm(*arrays):
    return [pltpu.with_memory_space_constraint(a, pltpu.HBM) for a in arrays]


VMEM_SPEC = pl.BlockSpec(memory_space=pltpu.VMEM)
HBM_SPEC = pl.BlockSpec(memory_space=pltpu.HBM)
ANY_SPEC = pl.BlockSpec(memory_space=pl.ANY)
SMEM_SPEC = pl.BlockSpec(memory_space=pltpu.SMEM)


def call(kernel, name, out_shape, in_specs, scratch_shapes=(), out_specs=None, us=1.0):
    return pl.pallas_call(
        kernel,
        name=name,
        out_shape=out_shape,
        in_specs=in_specs,
        out_specs=jax.tree.map(lambda _: VMEM_SPEC, out_shape) if out_specs is None else out_specs,
        scratch_shapes=scratch_shapes,
        compiler_params=pltpu.CompilerParams(vmem_limit_bytes=VMEM_LIMIT),
        cost_estimate=pl.CostEstimate(
            flops=int(us * 1.0e9), bytes_accessed=0, transcendentals=0
        ),
    )


def on_device(
    vectors,
    near_tiles,
    self_tiles,
    source_home,
    target_home,
    block_local,
    column_basis,
    row_basis,
    column_transfer,
    row_transfer,
    coupling,
    far_source,
):
    clusters, vector_count, leaf_size = vectors.shape
    blocks = near_tiles.shape[0]
    rank = column_basis.shape[1]
    parents, far_count = far_source.shape
    count = lax.axis_size("loop")
    columns = count // 2
    sibling = [(i, i ^ 1) for i in range(count)]

    def to_sibling(x):
        return lax.ppermute(x, "loop", sibling)

    def to_column(x, shift):
        return lax.ppermute(x, "loop", [(i, (i + 2 * shift) % count) for i in range(count)])

    panel = (clusters, vector_count, leaf_size)
    coeffs_shape = (parents, vector_count, 2 * rank)
    sums_shape = (columns * clusters, vector_count, leaf_size)

    def with_table(x):
        return pltpu.with_memory_space_constraint(x, pltpu.SMEM)

    held = (vectors, column_basis, column_transfer)
    entries = 2 * blocks + parents * far_count
    coeffs_out = jax.ShapeDtypeStruct(coeffs_shape, BF16)
    panel_out = jax.ShapeDtypeStruct(panel, F32)
    half_tiles = pltpu.VMEM((blocks // 2, leaf_size, leaf_size), BF16)
    first_call = call(
        first_kernel,
        "first",
        (coeffs_out, *(pltpu.VMEM(x.shape, x.dtype) for x in held), half_tiles),
        [HBM_SPEC] * 4,
        [half_tiles, pltpu.SemaphoreType.DMA((3 + CHUNKS,))],
        us=3.0,
    )
    raw = (source_home.T, target_home.T, block_local.T, far_source)
    load_call = call(
        functools.partial(load_kernel, columns, clusters),
        "load",
        (half_tiles, pltpu.SMEM((entries,), jnp.int32)),
        [HBM_SPEC] * 5,
        [half_tiles]
        + [pltpu.SMEM(x.shape, x.dtype) for x in raw]
        + [pltpu.SemaphoreType.DMA((4 + CHUNKS,))],
        out_specs=(VMEM_SPEC, SMEM_SPEC),
        us=2.0,
    )
    next_call = call(next_kernel, "next", coeffs_out, [VMEM_SPEC] * 3, us=0.5)
    self_call = call(self_kernel, "self", panel_out, [VMEM_SPEC] * 2, us=0.5)
    message_out = jax.ShapeDtypeStruct((2 * clusters, vector_count, leaf_size), BF16)
    join_call = call(
        join_kernel,
        "join",
        (message_out, jax.ShapeDtypeStruct(message_out.shape, F32)),
        [VMEM_SPEC] * 4,
        us=0.1,
    )
    settle_call = call(settle_kernel, "settle", message_out, [VMEM_SPEC] * 2, us=0.1)
    sums_out = (jax.ShapeDtypeStruct(sums_shape, BF16), jax.ShapeDtypeStruct(sums_shape, F32))
    near_scratch = [
        pltpu.VMEM((count * clusters, vector_count, leaf_size), BF16),
        pltpu.VMEM((blocks, vector_count, leaf_size), F32),
        pltpu.VMEM((count * clusters, vector_count, leaf_size), F32),
    ]

    def near_call(panels, others):
        return call(
            functools.partial(near_kernel, len(panels), len(tiles)),
            "near",
            sums_out,
            [SMEM_SPEC]
            + [VMEM_SPEC] * (len(tiles) + len(panels))
            + [ANY_SPEC] * len(others),
            near_scratch,
            us=1.0,
        )(with_table(table), *in_vmem(*tiles, *panels), *others)

    gathered_coeffs = pltpu.VMEM((count * parents, vector_count, 2 * rank), BF16)
    far_call = call(
        functools.partial(far_kernel, count, 2 * blocks),
        "far",
        panel_out,
        [SMEM_SPEC] + [VMEM_SPEC] * (3 + count),
        [gathered_coeffs],
        us=0.5,
    )
    packed = 2 * parents * rank // leaf_size
    wide_out = jax.ShapeDtypeStruct((clusters + packed, vector_count, leaf_size), BF16)
    widen_call = call(widen_kernel, "widen", wide_out, [VMEM_SPEC] * 4, us=0.1)
    last_call = call(
        functools.partial(last_kernel, 2 * blocks),
        "last",
        jax.ShapeDtypeStruct(panel, BF16),
        [SMEM_SPEC] + [VMEM_SPEC] * 9,
        [gathered_coeffs, pltpu.VMEM((2 * parents, vector_count, 2 * rank), BF16)],
        us=0.6,
    )

    def tie(x, *others):
        return pl.pallas_call(
            tie_kernel,
            name="tie",
            out_shape=pltpu.VMEM(x.shape, x.dtype),
            in_specs=[VMEM_SPEC] + [pl.BlockSpec(memory_space=pl.ANY)] * len(others),
            out_specs=VMEM_SPEC,
            input_output_aliases={0: 0},
            compiler_params=pltpu.CompilerParams(vmem_limit_bytes=VMEM_LIMIT),
        )(*in_vmem(x), *others)

    def far_of(near_coeffs):
        pieces = [piece for x in near_coeffs for piece in (x, to_sibling(x))]
        return far_call(
            with_table(table), *in_vmem(row_transfer, row_basis, coupling, *pieces)
        )

    def across(x):
        return [to_column(x, shift) for shift in range(1, columns)]

    def gathered(current, from_columns, beside, coeffs):
        panels = [current, beside]
        for x in from_columns:
            panels += [x, to_sibling(tie(x, coeffs))]
        return panels

    def finished(keep, arrived, self_part, far_part):
        near = keep[:clusters] + arrived[:clusters].astype(F32)
        for s in range(1, columns):
            rows = slice(s * clusters, (s + 1) * clusters)
            partial = (keep[rows] + arrived[rows].astype(F32)).astype(BF16)
            near = near + to_column(partial, s).astype(F32)
        return (self_part + far_part + near).astype(BF16)

    from_columns = across(vectors)
    beside = to_sibling(vectors)
    coeffs, current, basis_held, transfer_held, first_half = first_call(
        *in_hbm(*held, near_tiles)
    )
    second_half, table = load_call(*in_hbm(*raw, near_tiles))
    tiles = (first_half, second_half)
    near_coeffs = [coeffs] + across(coeffs)
    panels = gathered(current, from_columns, beside, coeffs)
    send, keep = near_call(panels, near_coeffs)
    arrived = to_sibling(send)
    self_part = self_call(*in_vmem(current, self_tiles))
    far_part = far_of(near_coeffs)

    if columns == 2 and ITERS == 2:
        message, sums = join_call(*in_vmem(keep, arrived, self_part, far_part))
        pair = settle_call(*in_vmem(sums, to_column(message, 1)))
        beside = to_sibling(pair)
        current = pair[:clusters]
        coeffs = next_call(*in_vmem(current, basis_held, transfer_held))
        panels = [pair[:clusters], beside[:clusters], pair[clusters:], beside[clusters:]]
        send, keep = near_call(panels, [coeffs])
        arrived = to_sibling(send)
        coeffs_beside = to_sibling(coeffs)
        self_part = self_call(*in_vmem(current, self_tiles))
        message = widen_call(*in_vmem(keep, arrived, coeffs, coeffs_beside))
        return last_call(
            with_table(table),
            *in_vmem(
                row_transfer,
                row_basis,
                coupling,
                coeffs,
                coeffs_beside,
                self_part,
                keep,
                arrived,
                to_column(message, 1),
            ),
        )
    for step in range(1, ITERS):
        current = finished(keep, arrived, self_part, far_part)
        from_columns = across(current)
        beside = to_sibling(current)
        coeffs = next_call(*in_vmem(current, basis_held, transfer_held))
        near_coeffs = [coeffs] + across(coeffs)
        panels = gathered(current, from_columns, beside, coeffs)
        send, keep = near_call(panels, near_coeffs)
        arrived = to_sibling(send)
        self_part = self_call(*in_vmem(current, self_tiles))
        far_part = far_of(near_coeffs)
    return finished(keep, arrived, self_part, far_part)


def solution(mesh):
    in_specs = (
        P(("groups", "loop"), "cuts", None),
        P(("groups", "loop"), None, None),
        P(("groups", "loop"), None, None),
        P(("groups", "loop"), None),
        P(("groups", "loop"), None),
        P(("groups", "loop"), None),
        P(("groups", "loop"), None, None),
        P(("groups", "loop"), None, None),
        P(("groups", "loop"), None, None),
        P(("groups", "loop"), None, None),
        P(("groups", "loop"), None, None),
        P(("groups", "loop"), None),
    )
    out_specs = P(("groups", "loop"), "cuts", None)
    return jax.shard_map(
        on_device, mesh=mesh, in_specs=in_specs, out_specs=out_specs, check_vma=False
    )
```

time: 50 us -> 34.5 us (0.69)
  starting transfers between devices: 12.8 us -> 8.42 us
  local copies, waits for them, and re-layouts: 3.81 us -> 0.07 us
  Pallas kernels: 14.8 us -> 11.7 us
  other arithmetic: 3.09 us -> 0 us
  waiting for transfers between devices: 15.2 us -> 13.9 us
    ppermute x6 -> x4, starting transfers between devices: 11.5 us -> 6.63 us  [to_column(): lax.ppermute(x, 'loop', [(i, (i + 2 * shift) % count) for i in range(coun...]
    unnamed x20 -> x9, local copies, waits for them, and re-layouts: 3.73 us -> 0.03 us
    pallas_call x7 -> x11, Pallas kernels: 13.5 us -> 10.5 us  [the longest x1 3.29 us: on_device(): second_half, table = load_call(*in_hbm(*raw, near_tiles))]
    ppermute x6 -> x4, waiting for transfers between devices: 13.8 us -> 11.6 us  [to_column(): lax.ppermute(x, 'loop', [(i, (i + 2 * shift) % count) for i in range(coun...]
    add x2 -> x0, other arithmetic: 1.5 us -> none  [piece(): return (2 * shift + (home % 2 != my_core)) * size + local]
    ppermute x10 -> x8, waiting for transfers between devices: 1.37 us -> 2.34 us  [to_sibling(): return lax.ppermute(x, 'loop', sibling)]
    convert_element_type x4 -> x0, other arithmetic: 0.95 us -> none  [the longest x2 0.88 us: on_device(): current = (self_part + far_part + near).astype(BF16)]
    concatenate x1 -> x0, other arithmetic: 0.64 us -> none  [on_device(): jnp.concatenate([piece(source, block_local[:, 0], clusters), target_place...]
  transfers between devices with their start and end apart: 16 -> 12, of which waited for: 7 -> 7; matrix products, arithmetic and copies ran while one was open for 5% -> 0% of each run, Pallas kernels for 22% -> 24%
where the time goes in v2:
time: 34.5 us; the launch traced here: 34.3 us
  waiting for transfers between devices  13.9 us (40%)
  Pallas kernels  11.7 us (34%)
  starting transfers between devices  8.42 us (24%)
    ppermute x4, waiting for transfers between devices, to_column(): lax.ppermute(x, 'loop', [(i, (i + 2 * shift) % count) for i in range(coun...  11.6 us
    ppermute x4, starting transfers between devices, to_column(): lax.ppermute(x, 'loop', [(i, (i + 2 * shift) % count) for i in range(coun...  6.63 us
    pallas_call x1, Pallas kernels, on_device(): second_half, table = load_call(*in_hbm(*raw, near_tiles))  3.29 us
    pallas_call x1, Pallas kernels, on_device(): first_call(*in_hbm(*held, near_tiles))  2.73 us
    ppermute x8, waiting for transfers between devices, to_sibling(): return lax.ppermute(x, 'loop', sibling)  2.34 us
    pallas_call x2, Pallas kernels, near_call(): call(functools.partial(near_kernel, len(panels), len(tiles)), 'near', sum...  2.04 us
    ppermute x8, starting transfers between devices, to_sibling(): return lax.ppermute(x, 'loop', sibling)  1.79 us
    pallas_call x2, Pallas kernels, on_device(): self_part = self_call(*in_vmem(current, self_tiles))  1.29 us
  transfers between devices with their start and end apart: 12, of which 7 were waited for; matrix products, arithmetic and copies ran while one was open for 0% of the time, Pallas kernels for 24%

profile of v2, /device:TPU:0, one launch (start us, length us, event | category | flops | bytes accessed | tf_op | source)
XLA Modules:
  0.0 34.3 jit_solution(5136068035900848180)
XLA Ops:
  0.0 3.0 %collective-permute-start.1 = (bf16[16,16,256]{2,1,0:T(8,128)(2,1)}, bf16[16,16,256]{2,1,0:T(8,128)(2,1)S(1)}, u32[]{:S(2)}, u32[]{:S(2)}) collective-permute-start(bf16[16,16,256]{2,1,0:T(8,128)(2,1)} %vectors.1), channel_id=1, source_target_pairs={{0,8},{4,12},{8,0},{12,4},{1,9},{5,13},{9,1},{13,5},{2,10},{6,14},... | collective-permute-start | bytes 393224 | tf_op jit(solution)/shard_map/ppermute | solution.py:358
  3.0 0.0 collective-permute-start
  3.0 2.7 %first.1 = (bf16[8,16,128]{2,1,0:T(8,128)(2,1)S(1)}, bf16[16,16,256]{2,1,0:T(8,128)(2,1)S(1)}, bf16[16,64,256]{2,1,0:T(8,128)(2,1)S(1)}, bf16[16,64,64]{2,1,0:T(8,128)(2,1)S(1)}, bf16[24,256,256]{2,1,0:T(8,128)(2,1)S(1)}) custom-call(bf16[16,16,256]{2,1,0:T(8,128)(2,1)} %vectors.1, bf16[16,64,256]{2,1,0:T(8,128)(2,1)} %column_basis.1, ...), custom_call_target="tpu_custom_call" | custom-call | flops 3000000000 | tf_op jit(solution)/shard_map/first/pallas_call | solution.py:479
  5.7 0.1 collective-permute-start.3
  5.8 0.9 %collective-permute-done.1.refs_4_ = bf16[16,16,256]{2,1,0:T(8,128)(2,1)S(1)} collective-permute-done((bf16[16,16,256]{2,1,0:T(8,128)(2,1)}, bf16[16,16,256]{2,1,0:T(8,128)(2,1)S(1)}, u32[]{:S(2)}, u32[]{:S(2)}) %collective-permute-start.1) | collective-permute-done | bytes 131104 | tf_op jit(solution)/shard_map/ppermute | solution.py:358
  6.7 0.1 collective-permute-start.2
  6.8 3.3 %load.1 = (bf16[24,256,256]{2,1,0:T(8,128)(2,1)S(1)}, s32[160]{0:T(256)S(4)}) custom-call(s32[1,48]{1,0:T(1,128)} %bitcast.4, s32[1,48]{1,0:T(1,128)} %bitcast.5, s32[2,48]{1,0:T(2,128)} %bitcast.3, s32[8,8]{1,0:T(8,128)} %far_source.1, bf16[48,256,256]{2,1,0:T(8,128)(2,1)} %tiles.3), custom_call_target="tpu_custom_call" | custom-call | flops 2000000000 | tf_op jit(solution)/shard_map/load/pallas_call | solution.py:482
  10.1 0.0 collective-permute-done.3.refs_7_.refs_2_
  10.1 0.0 collective-permute-done.refs_3_
  10.1 0.0 collective-permute-done.2.refs_5_
  10.1 0.0 copy-start
  10.1 0.0 copy-start.1
  10.1 0.0 copy-start.2
  10.1 0.0 copy-start.3
  10.1 1.0 %near.2 = (bf16[32,16,256]{2,1,0:T(8,128)(2,1)S(1)}, f32[32,16,256]{2,1,0:T(8,128)S(1)}) custom-call(s32[160]{0:T(256)S(4)} %get-tuple-element.18.table, bf16[24,256,256]{2,1,0:T(8,128)(2,1)S(1)} %get-tuple-element.19.refs_0_, bf16[24,256,256]{2,1,0:T(8,128)(2,1)S(1)} %get-tuple-element.20.refs_1_, ...), custom_call_target="tpu_custom_call" | custom-call | flops 1000000000 | tf_op jit(solution)/shard_map/near/pallas_call | solution.py:411
  11.2 0.6 %collective-permute-start.4 = (bf16[32,16,256]{2,1,0:T(8,128)(2,1)S(1)}, bf16[32,16,256]{2,1,0:T(8,128)(2,1)S(1)}, u32[]{:S(2)}, u32[]{:S(2)}) collective-permute-start(bf16[32,16,256]{2,1,0:T(8,128)(2,1)S(1)} %get-tuple-element.24), channel_id=1, source_target_pairs={{0,4},{4,0},{8,12},{12,8},{1,5},{5,1},{9,13},{13,9},{2,6},{6,2},{1... | collective-permute-start | bytes 786440 | tf_op jit(solution)/shard_map/ppermute | solution.py:355
  11.7 0.1 collective-permute-start.5
  11.8 0.4 %collective-permute-start.6 = (bf16[8,16,128]{2,1,0:T(8,128)(2,1)S(1)}, bf16[8,16,128]{2,1,0:T(8,128)(2,1)S(1)}, u32[]{:S(2)}, u32[]{:S(2)}) collective-permute-start(bf16[8,16,128]{2,1,0:T(8,128)(2,1)S(1)} %collective-permute-done.3.refs_7_.refs_2_), channel_id=1, source_target_pairs={{0,4},{4,0},{8,12},{12,8},{1,5},{5,1},{9,13},{13,9},{2,6},{6,2},{1... | collective-permute-start | bytes 98312 | tf_op jit(solution)/shard_map/ppermute | solution.py:355
  12.2 0.0 copy-done
  12.3 0.6 %self.2.self_part = f32[16,16,256]{2,1,0:T(8,128)S(1)} custom-call(bf16[16,16,256]{2,1,0:T(8,128)(2,1)S(1)} %get-tuple-element.21.refs_2_.current, bf16[16,256,256]{2,1,0:T(8,128)(2,1)S(1)} %copy-done), custom_call_target="tpu_custom_call" | custom-call | flops 500000000 | tf_op jit(solution)/shard_map/self/pallas_call | solution.py:488
  12.9 0.1 collective-permute-done.5.refs_1_
  12.9 0.2 collective-permute-done.6.refs_3_
  13.1 0.0 copy-done.1
  13.1 0.0 copy-done.2
  13.1 0.0 copy-done.3
  13.1 0.5 %far.1.far_part = f32[16,16,256]{2,1,0:T(8,128)S(1)} custom-call(s32[160]{0:T(256)S(4)} %get-tuple-element.18.table, bf16[16,64,64]{2,1,0:T(8,128)(2,1)S(1)} %copy-done.3, bf16[16,64,256]{2,1,0:T(8,128)(2,1)S(1)} %copy-done.1, bf16[8,64,512]{2,1,0:T(8,128)(2,1)S(1)} %copy-done.2, bf16[8,16,128]{2,1,0:T(8,128)(2,1)S(1)} %get-tuple-element.22.refs_1_.refs_6_.refs_0_, ...), custom_call_target="tpu_custom_call" | custom-call | flops 500000000 | tf_op jit(solution)/shard_map/far/pallas_call | solution.py:456
  13.6 0.0 collective-permute-done.4.arrived
  13.6 0.1 join.1
  13.7 1.8 %collective-permute-start.7 = (bf16[32,16,256]{2,1,0:T(8,128)(2,1)S(1)}, bf16[32,16,256]{2,1,0:T(8,128)(2,1)S(1)}, u32[]{:S(2)}, u32[]{:S(2)}) collective-permute-start(bf16[32,16,256]{2,1,0:T(8,128)(2,1)S(1)} %get-tuple-element.26), channel_id=1, source_target_pairs={{0,8},{4,12},{8,0},{12,4},{1,9},{5,13},{9,1},{13,5},{2,10},{6,14},... | collective-permute-start | bytes 786440 | tf_op jit(solution)/shard_map/ppermute | solution.py:358
  15.5 6.8 %collective-permute-done.7.message = bf16[32,16,256]{2,1,0:T(8,128)(2,1)S(1)} collective-permute-done((bf16[32,16,256]{2,1,0:T(8,128)(2,1)S(1)}, bf16[32,16,256]{2,1,0:T(8,128)(2,1)S(1)}, u32[]{:S(2)}, u32[]{:S(2)}) %collective-permute-start.7) | collective-permute-done | bytes 262176 | tf_op jit(solution)/shard_map/ppermute | solution.py:358
  22.4 0.1 collective-permute-start.9
  22.5 0.5 %next.1.refs_6_.coeffs = bf16[8,16,128]{2,1,0:T(8,128)(2,1)S(1)} custom-call(bf16[16,16,256]{2,1,0:T(8,128)(2,1)S(1)} %get-tuple-element.34.current.refs_2_, bf16[16,64,256]{2,1,0:T(8,128)(2,1)S(1)} %get-tuple-element.27.column_basis, bf16[16,64,64]{2,1,0:T(8,128)(2,1)S(1)} %get-tuple-element.28.column_transfer), custom_call_target="tpu_custom_call" | custom-call | flops 500000000 | tf_op jit(solution)/shard_map/next/pallas_call | solution.py:496
  23.0 1.0 %collective-permute-done.9 = bf16[32,16,256]{2,1,0:T(8,128)(2,1)S(1)} collective-permute-done((bf16[32,16,256]{2,1,0:T(8,128)(2,1)S(1)}, bf16[32,16,256]{2,1,0:T(8,128)(2,1)S(1)}, u32[]{:S(2)}, u32[]{:S(2)}) %collective-permute-start.9) | collective-permute-done | bytes 262176 | tf_op jit(solution)/shard_map/ppermute | solution.py:355
  24.0 1.0 %near.3 = (bf16[32,16,256]{2,1,0:T(8,128)(2,1)S(1)}, f32[32,16,256]{2,1,0:T(8,128)S(1)}) custom-call(s32[160]{0:T(256)S(4)} %get-tuple-element.18.table, bf16[24,256,256]{2,1,0:T(8,128)(2,1)S(1)} %get-tuple-element.19.refs_0_, bf16[24,256,256]{2,1,0:T(8,128)(2,1)S(1)} %get-tuple-element.20.refs_1_, ...), custom_call_target="tpu_custom_call" | custom-call | flops 1000000000 | tf_op jit(solution)/shard_map/near/pallas_call | solution.py:411
  25.0 0.2 collective-permute-start.10
  25.3 0.4 %collective-permute-start.8 = (bf16[8,16,128]{2,1,0:T(8,128)(2,1)S(1)}, bf16[8,16,128]{2,1,0:T(8,128)(2,1)S(1)}, u32[]{:S(2)}, u32[]{:S(2)}) collective-permute-start(bf16[8,16,128]{2,1,0:T(8,128)(2,1)S(1)} %next.1.refs_6_.coeffs), channel_id=1, source_target_pairs={{0,4},{4,0},{8,12},{12,8},{1,5},{5,1},{9,13},{13,9},{2,6},{6,2},{1... | collective-permute-start | bytes 98312 | tf_op jit(solution)/shard_map/ppermute | solution.py:355
  25.6 1.1 %collective-permute-done.8.beside = bf16[8,16,128]{2,1,0:T(8,128)(2,1)S(1)} collective-permute-done((bf16[8,16,128]{2,1,0:T(8,128)(2,1)S(1)}, bf16[8,16,128]{2,1,0:T(8,128)(2,1)S(1)}, u32[]{:S(2)}, u32[]{:S(2)}) %collective-permute-start.8) | collective-permute-done | bytes 32800 | tf_op jit(solution)/shard_map/ppermute | solution.py:355
  26.7 0.0 collective-permute-done.10.arrived
  26.7 0.1 widen.1
  26.8 1.8 %collective-permute-start.11 = (bf16[20,16,256]{2,1,0:T(8,128)(2,1)S(1)}, bf16[20,16,256]{2,1,0:T(8,128)(2,1)S(1)}, u32[]{:S(2)}, u32[]{:S(2)}) collective-permute-start(bf16[20,16,256]{2,1,0:T(8,128)(2,1)S(1)} %widen.1), channel_id=1, source_target_pairs={{0,8},{4,12},{8,0},{12,4},{1,9},{5,13},{9,1},{13,5},{2,10},{6,14},... | collective-permute-start | bytes 491528 | tf_op jit(solution)/shard_map/ppermute | solution.py:358
  28.6 0.6 %self.3.self_part = f32[16,16,256]{2,1,0:T(8,128)S(1)} custom-call(bf16[16,16,256]{2,1,0:T(8,128)(2,1)S(1)} %get-tuple-element.34.current.refs_2_, bf16[16,256,256]{2,1,0:T(8,128)(2,1)S(1)} %copy-done), custom_call_target="tpu_custom_call" | custom-call | flops 500000000 | tf_op jit(solution)/shard_map/self/pallas_call | solution.py:501
  29.2 3.9 %collective-permute-done.11.message = bf16[20,16,256]{2,1,0:T(8,128)(2,1)S(1)} collective-permute-done((bf16[20,16,256]{2,1,0:T(8,128)(2,1)S(1)}, bf16[20,16,256]{2,1,0:T(8,128)(2,1)S(1)}, u32[]{:S(2)}, u32[]{:S(2)}) %collective-permute-start.11) | collective-permute-done | bytes 163872 | tf_op jit(solution)/shard_map/ppermute | solution.py:358
  33.1 1.2 %last.1 = bf16[16,16,256]{2,1,0:T(8,128)(2,1)} custom-call(s32[160]{0:T(256)S(4)} %get-tuple-element.18.table, bf16[16,64,64]{2,1,0:T(8,128)(2,1)S(1)} %copy-done.3, bf16[16,64,256]{2,1,0:T(8,128)(2,1)S(1)} %copy-done.1, bf16[8,64,512]{2,1,0:T(8,128)(2,1)S(1)} %copy-done.2, bf16[8,16,128]{2,1,0:T(8,128)(2,1)S(1)} %next.1.refs_6_.coeffs, ...), custom_call_target="tpu_custom_call" | custom-call | flops 600000000 | tf_op jit(solution)/shard_map/last/pallas_call | solution.py:503
  (5 shorter events, 0.1 us)
Async XLA Ops:
  0.0 6.7 %collective-permute-start.1 = (bf16[16,16,256]{2,1,0:T(8,128)(2,1)}, bf16[16,16,256]{2,1,0:T(8,128)(2,1)S(1)}, u32[]{:S(2)}, u32[]{:S(2)}) collective-permute-start(bf16[16,16,256]{2,1,0:T(8,128)(2,1)} %vectors.1), channel_id=1, source_target_pairs={{0,8},{4,12},{8,0},{12,4},{1,9},{5,13},{9,1},{13,5},{2,10},{6,14},... | collective-permute-start | bytes 393224 | tf_op jit(solution)/shard_map/ppermute | solution.py:358
  3.0 7.1 %collective-permute-start = (bf16[16,16,256]{2,1,0:T(8,128)(2,1)}, bf16[16,16,256]{2,1,0:T(8,128)(2,1)S(1)}, u32[]{:S(2)}, u32[]{:S(2)}) collective-permute-start(bf16[16,16,256]{2,1,0:T(8,128)(2,1)} %vectors.1), channel_id=1, source_target_pairs={{0,4},{4,0},{8,12},{12,8},{1,5},{5,1},{9,13},{13,9},{2,6},{6,2},{1... | collective-permute-start | bytes 393224 | tf_op jit(solution)/shard_map/ppermute | solution.py:355
  5.7 4.4 %collective-permute-start.3 = (bf16[8,16,128]{2,1,0:T(8,128)(2,1)S(1)}, bf16[8,16,128]{2,1,0:T(8,128)(2,1)S(1)}, u32[]{:S(2)}, u32[]{:S(2)}) collective-permute-start(bf16[8,16,128]{2,1,0:T(8,128)(2,1)S(1)} %get-tuple-element.22.refs_1_.refs_6_.refs_0_), channel_id=1, source_target_pairs={{0,8},{4,12},{8,0},{12,4},{1,9},{5,13},{9,1},{13,5},{2,10},{6,14},... | collective-permute-start | bytes 98312 | tf_op jit(solution)/shard_map/ppermute | solution.py:358
  6.7 3.4 %collective-permute-start.2 = (bf16[16,16,256]{2,1,0:T(8,128)(2,1)S(1)}, bf16[16,16,256]{2,1,0:T(8,128)(2,1)S(1)}, u32[]{:S(2)}, u32[]{:S(2)}) collective-permute-start(bf16[16,16,256]{2,1,0:T(8,128)(2,1)S(1)} %tie.1), channel_id=1, source_target_pairs={{0,4},{4,0},{8,12},{12,8},{1,5},{5,1},{9,13},{13,9},{2,6},{6,2},{1... | collective-permute-start | bytes 393224 | tf_op jit(solution)/shard_map/ppermute | solution.py:355
  10.1 2.2 %copy-start = (bf16[16,256,256]{2,1,0:T(8,128)(2,1)S(1)}, bf16[16,256,256]{2,1,0:T(8,128)(2,1)}, u32[]{:S(2)}) copy-start(bf16[16,256,256]{2,1,0:T(8,128)(2,1)} %self_tiles.3) | copy-start | bytes 6291460
  10.1 3.0 %copy-start.1 = (bf16[16,64,256]{2,1,0:T(8,128)(2,1)S(1)}, bf16[16,64,256]{2,1,0:T(8,128)(2,1)}, u32[]{:S(2)}) copy-start(bf16[16,64,256]{2,1,0:T(8,128)(2,1)} %row_basis.3) | copy-start | bytes 1572868
  10.1 3.0 %copy-start.2 = (bf16[8,64,512]{2,1,0:T(8,128)(2,1)S(1)}, bf16[8,64,512]{2,1,0:T(8,128)(2,1)}, u32[]{:S(2)}) copy-start(bf16[8,64,512]{2,1,0:T(8,128)(2,1)} %coupling.3) | copy-start | bytes 1572868
  10.1 3.0 %copy-start.3 = (bf16[16,64,64]{2,1,0:T(8,128)(2,1)S(1)}, bf16[16,64,64]{2,1,0:T(8,128)(2,1)}, u32[]{:S(2)}) copy-start(bf16[16,64,64]{2,1,0:T(8,128)(2,1)} %row_transfer.3) | copy-start | bytes 393220
  11.2 2.4 %collective-permute-start.4 = (bf16[32,16,256]{2,1,0:T(8,128)(2,1)S(1)}, bf16[32,16,256]{2,1,0:T(8,128)(2,1)S(1)}, u32[]{:S(2)}, u32[]{:S(2)}) collective-permute-start(bf16[32,16,256]{2,1,0:T(8,128)(2,1)S(1)} %get-tuple-element.24), channel_id=1, source_target_pairs={{0,4},{4,0},{8,12},{12,8},{1,5},{5,1},{9,13},{13,9},{2,6},{6,2},{1... | collective-permute-start | bytes 786440 | tf_op jit(solution)/shard_map/ppermute | solution.py:355
  11.7 1.2 %collective-permute-start.5 = (bf16[8,16,128]{2,1,0:T(8,128)(2,1)S(1)}, bf16[8,16,128]{2,1,0:T(8,128)(2,1)S(1)}, u32[]{:S(2)}, u32[]{:S(2)}) collective-permute-start(bf16[8,16,128]{2,1,0:T(8,128)(2,1)S(1)} %get-tuple-element.22.refs_1_.refs_6_.refs_0_), channel_id=1, source_target_pairs={{0,4},{4,0},{8,12},{12,8},{1,5},{5,1},{9,13},{13,9},{2,6},{6,2},{1... | collective-permute-start | bytes 98312 | tf_op jit(solution)/shard_map/ppermute | solution.py:355
  11.8 1.3 %collective-permute-start.6 = (bf16[8,16,128]{2,1,0:T(8,128)(2,1)S(1)}, bf16[8,16,128]{2,1,0:T(8,128)(2,1)S(1)}, u32[]{:S(2)}, u32[]{:S(2)}) collective-permute-start(bf16[8,16,128]{2,1,0:T(8,128)(2,1)S(1)} %collective-permute-done.3.refs_7_.refs_2_), channel_id=1, source_target_pairs={{0,4},{4,0},{8,12},{12,8},{1,5},{5,1},{9,13},{13,9},{2,6},{6,2},{1... | collective-permute-start | bytes 98312 | tf_op jit(solution)/shard_map/ppermute | solution.py:355
  13.7 8.6 %collective-permute-start.7 = (bf16[32,16,256]{2,1,0:T(8,128)(2,1)S(1)}, bf16[32,16,256]{2,1,0:T(8,128)(2,1)S(1)}, u32[]{:S(2)}, u32[]{:S(2)}) collective-permute-start(bf16[32,16,256]{2,1,0:T(8,128)(2,1)S(1)} %get-tuple-element.26), channel_id=1, source_target_pairs={{0,8},{4,12},{8,0},{12,4},{1,9},{5,13},{9,1},{13,5},{2,10},{6,14},... | collective-permute-start | bytes 786440 | tf_op jit(solution)/shard_map/ppermute | solution.py:358
  22.4 1.6 %collective-permute-start.9 = (bf16[32,16,256]{2,1,0:T(8,128)(2,1)S(1)}, bf16[32,16,256]{2,1,0:T(8,128)(2,1)S(1)}, u32[]{:S(2)}, u32[]{:S(2)}) collective-permute-start(bf16[32,16,256]{2,1,0:T(8,128)(2,1)S(1)} %settle.1), channel_id=1, source_target_pairs={{0,4},{4,0},{8,12},{12,8},{1,5},{5,1},{9,13},{13,9},{2,6},{6,2},{1... | collective-permute-start | bytes 786440 | tf_op jit(solution)/shard_map/ppermute | solution.py:355
  25.0 1.7 %collective-permute-start.10 = (bf16[32,16,256]{2,1,0:T(8,128)(2,1)S(1)}, bf16[32,16,256]{2,1,0:T(8,128)(2,1)S(1)}, u32[]{:S(2)}, u32[]{:S(2)}) collective-permute-start(bf16[32,16,256]{2,1,0:T(8,128)(2,1)S(1)} %get-tuple-element.30), channel_id=1, source_target_pairs={{0,4},{4,0},{8,12},{12,8},{1,5},{5,1},{9,13},{13,9},{2,6},{6,2},{1... | collective-permute-start | bytes 786440 | tf_op jit(solution)/shard_map/ppermute | solution.py:355
  25.3 1.4 %collective-permute-start.8 = (bf16[8,16,128]{2,1,0:T(8,128)(2,1)S(1)}, bf16[8,16,128]{2,1,0:T(8,128)(2,1)S(1)}, u32[]{:S(2)}, u32[]{:S(2)}) collective-permute-start(bf16[8,16,128]{2,1,0:T(8,128)(2,1)S(1)} %next.1.refs_6_.coeffs), channel_id=1, source_target_pairs={{0,4},{4,0},{8,12},{12,8},{1,5},{5,1},{9,13},{13,9},{2,6},{6,2},{1... | collective-permute-start | bytes 98312 | tf_op jit(solution)/shard_map/ppermute | solution.py:355
  26.8 6.3 %collective-permute-start.11 = (bf16[20,16,256]{2,1,0:T(8,128)(2,1)S(1)}, bf16[20,16,256]{2,1,0:T(8,128)(2,1)S(1)}, u32[]{:S(2)}, u32[]{:S(2)}) collective-permute-start(bf16[20,16,256]{2,1,0:T(8,128)(2,1)S(1)} %widen.1), channel_id=1, source_target_pairs={{0,8},{4,12},{8,0},{12,4},{1,9},{5,13},{9,1},{13,5},{2,10},{6,14},... | collective-permute-start | bytes 491528 | tf_op jit(solution)/shard_map/ppermute | solution.py:358

commit v3 on v0

v3 whole, which is shorter than its diff:
```python
import functools

import jax
import jax.numpy as jnp
from jax import lax
from jax.experimental import pallas as pl
from jax.experimental.pallas import tpu as pltpu
from jax.sharding import PartitionSpec as P

ITERS = 2
F32, BF16 = jnp.float32, jnp.bfloat16
ROWS_BY_ROWS = (((1,), (1,)), ((), ()))
ROWS_BY_COLUMNS = (((1,), (0,)), ((), ()))
VMEM_LIMIT = 8 * 1024 * 1024
FAR_ROW = 8


def dot(a, b, dims):
    return lax.dot_general(a, b, dims, preferred_element_type=F32)


def dot_wide(a, b, dims):
    rows = a.shape[0]
    upper = a.astype(BF16).astype(F32)
    halves = jnp.concatenate([upper, a - upper], axis=0).astype(BF16)
    both = dot(halves, b, dims)
    return both[:rows] + both[rows:]


def lanes_below(vectors, lanes):
    return lax.broadcasted_iota(jnp.int32, (vectors, lanes), 1) < lanes // 2


def load_all(sems, *pairs):
    copies = [pltpu.make_async_copy(x, y, sems.at[i]) for i, (x, y) in enumerate(pairs)]
    for copy in copies:
        copy.start()
    return copies


def parent_coeffs(current, column_basis, column_transfer, packed, first):
    clusters, rank, leaf_size = column_basis.shape
    vectors = current.shape[1]
    parents = clusters // 2
    lower = lanes_below(vectors, 2 * rank)
    leaves = []
    for p in range(parents):
        both = dot(
            current[2 * p : 2 * p + 2].reshape(2 * vectors, leaf_size),
            column_basis[2 * p : 2 * p + 2].reshape(2 * rank, leaf_size),
            ROWS_BY_ROWS,
        )
        leaves.append(jnp.where(lower, both[:vectors], both[vectors:]))
    totals = []
    for p in range(parents):
        transfer = column_transfer[2 * p : 2 * p + 2].reshape(2 * rank, rank)
        totals.append(dot_wide(leaves[p], transfer, ROWS_BY_COLUMNS))
    each = leaf_size // rank
    for p in range(0, parents, each):
        row = jnp.concatenate(totals[p : p + each], axis=-1)
        packed[first + p // each] = row.astype(BF16)


def unpack(packed, first, rows, rank, gathered, slot):
    for r in range(rows):
        row = packed[first + r].astype(F32)
        for k in range(row.shape[1] // (2 * rank)):
            pair = row[:, 2 * rank * k : 2 * rank * (k + 1)]
            lower = lanes_below(*pair.shape)
            turned = pltpu.roll(pair, rank, 1)
            gathered[slot] = jnp.where(lower, pair, turned).astype(BF16)
            gathered[slot + 1] = jnp.where(lower, turned, pair).astype(BF16)
            slot += 2
    return slot


def place_table(columns, clusters, source, target, local, far, values):
    me = lax.axis_index("loop")
    my_column = me // 2

    def around(shift):
        return jnp.where(shift < 0, shift + columns, shift)

    def other_core(home):
        return (home ^ me) & 1

    blocks = source.shape[1]
    home = source[...]
    shift = around(my_column - (home >> 1))
    values[0:1, :blocks] = (2 * shift + other_core(home)) * clusters + local[0:1]
    home = target[...]
    shift = around((home >> 1) - my_column)
    values[1:2, :blocks] = ((1 - other_core(home)) * columns + shift) * clusters + local[1:2]
    cluster = far[...]
    parents, far_count = cluster.shape
    home = jnp.zeros_like(cluster)
    for h in range(1, 2 * columns):
        home = home + jnp.where(cluster >= h * parents, 1, 0)
    shift = around(my_column - (home >> 1))
    place = (2 * shift + other_core(home)) * parents + cluster - home * parents
    values[FAR_ROW : FAR_ROW + parents, :far_count] = place


def first_kernel(
    columns,
    source_home,
    target_home,
    block_local,
    far_source,
    vectors,
    column_basis,
    column_transfer,
    packed,
    current,
    table,
    basis_held,
    transfer_held,
    source,
    target,
    local,
    far,
    values,
    sems,
):
    copies = load_all(
        sems,
        (source_home, source),
        (target_home, target),
        (block_local, local),
        (far_source, far),
        (vectors, current),
        (column_basis, basis_held),
        (column_transfer, transfer_held),
    )
    for copy in copies[:4]:
        copy.wait()
    place_table(columns, vectors.shape[0], source, target, local, far, values)
    placed = pltpu.make_async_copy(values, table, sems.at[7])
    placed.start()
    for copy in copies[4:]:
        copy.wait()
    parent_coeffs(current, basis_held, transfer_held, packed, 0)
    placed.wait()


def coeffs_kernel(current, column_basis, column_transfer, packed):
    parent_coeffs(current, column_basis, column_transfer, packed, 0)


def message_kernel(current, column_basis, column_transfer, message):
    clusters = current.shape[0]
    message[:clusters] = current[...]
    parent_coeffs(current, column_basis, column_transfer, message, clusters)


def self_kernel(current, self_tiles, *others):
    self_part = others[-1]
    for c in range(self_part.shape[0]):
        self_part[c] = dot(current[c], self_tiles[c], ROWS_BY_ROWS)


def turn_kernel(tiles, turned):
    for b in range(tiles.shape[0]):
        turned[b] = tiles[b].T


def near_kernel(panel_count, table, tiles, *refs):
    panels, refs = refs[:panel_count], refs[panel_count:]
    send, send_own, keep, keep_own, gathered, products, sums = refs[-7:]
    each = gathered.shape[0] // panel_count
    for k, panel in enumerate(panels):
        gathered[k * each : (k + 1) * each] = panel[:each]
    sums[...] = jnp.zeros_like(sums)
    blocks = tiles.shape[0]
    for b in range(blocks):
        products[b] = dot(gathered[table[0, b]], tiles[b], ROWS_BY_COLUMNS)
    for b in range(blocks):
        sums[table[1, b]] += products[b]
    own, half = keep_own.shape[0], sums.shape[0] // 2
    send_own[...] = sums[:own].astype(BF16)
    send[...] = sums[own:half].astype(BF16)
    keep_own[...] = sums[half : half + own]
    keep[...] = sums[half + own :]


def far_products(table, row_transfer, row_basis, coupling, gathered, store):
    vectors, lanes = gathered.shape[1:]
    rank, leaf_size = row_basis.shape[1:]
    parents = coupling.shape[0]
    far_count = coupling.shape[2] // rank
    lower = lanes_below(vectors, lanes)
    parent_outs = []
    for p in range(parents):
        pairs = []
        for f in range(0, far_count, 2):
            first = gathered[table[FAR_ROW + p, f]]
            second = gathered[table[FAR_ROW + p, f + 1]]
            pairs.append(jnp.where(lower, first.astype(F32), second.astype(F32)).astype(BF16))
        parent_outs.append(dot(jnp.concatenate(pairs, axis=-1), coupling[p], ROWS_BY_ROWS))
    leaf_outs = []
    for p in range(parents):
        transfer = jnp.concatenate([row_transfer[2 * p], row_transfer[2 * p + 1]], axis=-1)
        leaf_outs.append(dot_wide(parent_outs[p], transfer, ROWS_BY_COLUMNS))
    for p in range(parents):
        zero = jnp.zeros_like(leaf_outs[p])
        stacked = jnp.concatenate(
            [jnp.where(lower, leaf_outs[p], zero), jnp.where(lower, zero, leaf_outs[p])], axis=0
        ).astype(BF16)
        basis = row_basis[2 * p : 2 * p + 2].reshape(2 * rank, leaf_size)
        both = dot(stacked, basis, ROWS_BY_COLUMNS)
        store(2 * p, both.reshape(2, vectors, leaf_size))


def far_kernel(message_count, rows, table, row_transfer, row_basis, coupling, *refs):
    messages, (far_part, gathered) = refs[:message_count], refs[-2:]
    slot = 0
    for message in messages:
        slot = unpack(message, message.shape[0] - rows, rows, row_basis.shape[1], gathered, slot)

    def store(c, both):
        far_part[c : c + 2] = both

    far_products(table, row_transfer, row_basis, coupling, gathered, store)


def other_kernel(keep, arrived, message, sums):
    other = keep[...] + arrived[...].astype(F32)
    sums[...] = other
    message[...] = other.astype(BF16)


def own_kernel(keep, arrived, self_part, far_part, sent_before, message, sums):
    own = keep[...] + arrived[...].astype(F32) + self_part[...] + far_part[...]
    sums[...] = own
    message[...] = own.astype(BF16)


def settle_kernel(sums, message, *others):
    current = others[-1]
    current[...] = (sums[...] + message[...].astype(F32)).astype(BF16)


def cross_kernel(keep, arrived, self_part, column_coeffs, message):
    message[...] = (keep[...] + arrived[...].astype(F32)).astype(BF16)


def last_kernel(self_part, far_part, keep, arrived, message, product):
    near = keep[...] + arrived[...].astype(F32) + message[...].astype(F32)
    product[...] = (self_part[...] + far_part[...] + near).astype(BF16)


def tie_kernel(*refs):
    pass


def in_vmem(*arrays):
    return [pltpu.with_memory_space_constraint(a, pltpu.VMEM) for a in arrays]


def in_hbm(*arrays):
    return [pltpu.with_memory_space_constraint(a, pltpu.HBM) for a in arrays]


def in_smem(array):
    return pltpu.with_memory_space_constraint(array, pltpu.SMEM)


VMEM_SPEC = pl.BlockSpec(memory_space=pltpu.VMEM)
HBM_SPEC = pl.BlockSpec(memory_space=pltpu.HBM)
ANY_SPEC = pl.BlockSpec(memory_space=pl.ANY)
SMEM_SPEC = pl.BlockSpec(memory_space=pltpu.SMEM)


def call(kernel, name, out_shape, in_specs, scratch_shapes=(), out_specs=None, us=1.0):
    return pl.pallas_call(
        kernel,
        name=name,
        out_shape=out_shape,
        in_specs=in_specs,
        out_specs=jax.tree.map(lambda _: VMEM_SPEC, out_shape) if out_specs is None else out_specs,
        scratch_shapes=scratch_shapes,
        compiler_params=pltpu.CompilerParams(vmem_limit_bytes=VMEM_LIMIT),
        cost_estimate=pl.CostEstimate(
            flops=int(us * 1.0e9), bytes_accessed=0, transcendentals=0
        ),
    )


def tie(x, *others):
    return pl.pallas_call(
        tie_kernel,
        name="tie",
        out_shape=pltpu.VMEM(x.shape, x.dtype),
        in_specs=[VMEM_SPEC] + [ANY_SPEC] * len(others),
        out_specs=VMEM_SPEC,
        input_output_aliases={0: 0},
        compiler_params=pltpu.CompilerParams(vmem_limit_bytes=VMEM_LIMIT),
    )(*in_vmem(x), *others)


def on_device(
    vectors,
    near_tiles,
    self_tiles,
    source_home,
    target_home,
    block_local,
    column_basis,
    row_basis,
    column_transfer,
    row_transfer,
    coupling,
    far_source,
):
    clusters, vector_count, leaf_size = vectors.shape
    blocks = near_tiles.shape[0]
    rank = column_basis.shape[1]
    parents, far_count = far_source.shape
    count = lax.axis_size("loop")
    columns = count // 2
    sibling = [(i, i ^ 1) for i in range(count)]

    def to_sibling(x):
        return lax.ppermute(x, "loop", sibling)

    def to_column(x, shift):
        return lax.ppermute(x, "loop", [(i, (i + 2 * shift) % count) for i in range(count)])

    def across(x):
        return [to_column(x, shift) for shift in range(1, columns)]

    def panels(number, dtype):
        return jax.ShapeDtypeStruct((number, vector_count, leaf_size), dtype)

    def scratch(number, dtype, width=leaf_size):
        return pltpu.VMEM((number, vector_count, width), dtype)

    rows = parents * rank // leaf_size
    raw = (source_home.T, target_home.T, block_local.T, far_source)
    table_shape = (FAR_ROW + parents, 128)
    first_call = call(
        functools.partial(first_kernel, columns),
        "first",
        (
            panels(rows, BF16),
            pltpu.VMEM(vectors.shape, BF16),
            pltpu.SMEM(table_shape, jnp.int32),
        ),
        [HBM_SPEC] * 7,
        [pltpu.VMEM(x.shape, x.dtype) for x in (column_basis, column_transfer, *raw)]
        + [pltpu.VMEM(table_shape, jnp.int32), pltpu.SemaphoreType.DMA((8,))],
        out_specs=(VMEM_SPEC, VMEM_SPEC, SMEM_SPEC),
        us=10.0,
    )
    turn_call = call(
        turn_kernel, "turn", pltpu.VMEM(near_tiles.shape, BF16), [VMEM_SPEC], us=2.5
    )
    coeffs_call = call(coeffs_kernel, "coeffs", panels(rows, BF16), [VMEM_SPEC] * 3, us=0.5)
    def self_call(current, *others, us=0.6):
        specs = [VMEM_SPEC] * 2 + [ANY_SPEC] * len(others)
        return call(self_kernel, "self", panels(clusters, F32), specs, us=us)(
            *in_vmem(current, self_tiles), *others
        )

    def near_call(table, turned, given, *others):
        return call(
            functools.partial(near_kernel, len(given)),
            "near",
            (
                panels((columns - 1) * clusters, BF16),
                panels(clusters, BF16),
                panels((columns - 1) * clusters, F32),
                panels(clusters, F32),
            ),
            [SMEM_SPEC] + [VMEM_SPEC] * (1 + len(given)) + [ANY_SPEC] * len(others),
            [
                scratch(count * clusters, BF16),
                scratch(blocks, F32),
                scratch(count * clusters, F32),
            ],
            us=1.0,
        )(in_smem(table), *in_vmem(turned, *given), *others)

    gathered_coeffs = scratch(count * parents, BF16, 2 * rank)

    def far_call(table, messages):
        return call(
            functools.partial(far_kernel, len(messages), rows),
            "far",
            panels(clusters, F32),
            [SMEM_SPEC] + [VMEM_SPEC] * (3 + len(messages)),
            [gathered_coeffs],
            us=0.5,
        )(in_smem(table), *in_vmem(row_transfer, row_basis, coupling, *messages))

    def gather(message, *others):
        gathered = [message, to_sibling(message)]
        for x in across(message):
            gathered += [x, to_sibling(tie(x, *others) if others else x)]
        return gathered

    def both_to_sibling(send, send_own):
        arrived = to_sibling(jnp.concatenate([send, send_own]))
        return arrived[: send.shape[0]], arrived[send.shape[0] :]

    def all_coeffs(packed, crossed):
        beside = to_sibling(jnp.concatenate([packed, *crossed]))
        pieces = []
        for k, piece in enumerate([packed, *crossed]):
            pieces += [piece, beside[k * rows : (k + 1) * rows]]
        return pieces

    crossed = across(vectors)
    beside = to_sibling(vectors)
    packed, current, table = first_call(*in_hbm(*raw, vectors, column_basis, column_transfer))
    given = [current, beside]
    for x in crossed:
        given += [x, to_sibling(tie(x, packed))]
    crossed = across(packed)
    turned = turn_call(*in_vmem(near_tiles))
    send, send_own, keep, keep_own = near_call(table, turned, given, *crossed)
    arrived, arrived_own = to_sibling(send), to_sibling(send_own)
    pieces = all_coeffs(packed, crossed)

    if columns == 2 and ITERS == 2:
        both_out = (panels(clusters, BF16), panels(clusters, F32))
        other, other_sums = call(other_kernel, "other", both_out, [VMEM_SPEC] * 2, us=0.1)(
            *in_vmem(keep, arrived)
        )
        self_part = self_call(current, other)
        far_part = far_call(table, pieces)
        own, own_sums = call(
            own_kernel, "own", both_out, [VMEM_SPEC] * 4 + [ANY_SPEC], us=0.1
        )(*in_vmem(keep_own, arrived_own, self_part, far_part), other)

        def settled(sums, message, *others):
            specs = [VMEM_SPEC] * 2 + [ANY_SPEC] * len(others)
            return call(settle_kernel, "settle", panels(clusters, BF16), specs, us=0.1)(
                *in_vmem(sums, message), *others
            )

        other, own = to_column(other, 1), to_column(own, 1)
        current = settled(own_sums, other)
        beside = to_sibling(current)
        packed = coeffs_call(*in_vmem(current, column_basis, column_transfer))
        packed_column = to_column(packed, 1)
        column = settled(other_sums, own, packed, beside)
        given = [current, beside, column, to_sibling(column)]
        send, send_own, keep, keep_own = near_call(table, turned, given, packed)
        arrived, arrived_own = both_to_sibling(send, send_own)
        self_part = self_call(current, us=2.5)
        crossing = call(
            cross_kernel,
            "cross",
            panels(clusters, BF16),
            [VMEM_SPEC] * 2 + [ANY_SPEC] * 2,
            us=0.1,
        )(*in_vmem(keep, arrived), self_part, packed_column)
        far_part = far_call(table, all_coeffs(packed, [packed_column]))
        return call(last_kernel, "last", panels(clusters, BF16), [VMEM_SPEC] * 5, us=0.1)(
            *in_vmem(self_part, far_part, keep_own, arrived_own, to_column(crossing, 1))
        )

    self_part = self_call(current)
    far_part = far_call(table, pieces)

    def finished():
        near = keep_own + arrived_own.astype(F32)
        for s in range(1, columns):
            part = slice((s - 1) * clusters, s * clusters)
            partial = (keep[part] + arrived[part].astype(F32)).astype(BF16)
            near = near + to_column(partial, s).astype(F32)
        return (self_part + far_part + near).astype(BF16)

    for step in range(1, ITERS):
        message = call(
            message_kernel, "message", panels(clusters + rows, BF16), [VMEM_SPEC] * 3, us=0.5
        )(*in_vmem(finished(), column_basis, column_transfer))
        messages = gather(message)
        send, send_own, keep, keep_own = near_call(table, turned, messages)
        arrived, arrived_own = to_sibling(send), to_sibling(send_own)
        self_part = self_call(message)
        far_part = far_call(table, messages)
    return finished()


def solution(mesh):
    in_specs = (
        P(("groups", "loop"), "cuts", None),
        P(("groups", "loop"), None, None),
        P(("groups", "loop"), None, None),
        P(("groups", "loop"), None),
        P(("groups", "loop"), None),
        P(("groups", "loop"), None),
        P(("groups", "loop"), None, None),
        P(("groups", "loop"), None, None),
        P(("groups", "loop"), None, None),
        P(("groups", "loop"), None, None),
        P(("groups", "loop"), None, None),
        P(("groups", "loop"), None),
    )
    out_specs = P(("groups", "loop"), "cuts", None)
    return jax.shard_map(
        on_device, mesh=mesh, in_specs=in_specs, out_specs=out_specs, check_vma=False
    )
```

time: 109 us -> 31 us (0.28)
  blocking collectives: 26.6 us -> 0 us
  matrix products: 26.3 us -> 0 us
  waiting for transfers between devices: 25.5 us -> 11.1 us
  between operations: 13.6 us -> 0.22 us
  local copies, waits for them, and re-layouts: 12.8 us -> 0.09 us
  starting transfers between devices: 0.04 us -> 9.91 us
  Pallas kernels: 0 us -> 9.46 us
  other arithmetic: 3.09 us -> 0.04 us
    all_gather x4 -> x0, blocking collectives: 26.6 us -> none  [the longest x2 16.1 us: on_device(): shard_rows = lax.all_gather(current, 'loop', axis=0, tiled=True)]
    dot_general x16 -> x0, matrix products: 26.3 us -> none  [the longest x2 9.3 us: on_device(): jnp.einsum('bvj,bij->bvi', panels, near_tiles, preferred_element_type=jnp...]
    reduce_scatter x2 -> x0, waiting for transfers between devices: 25.5 us -> none  [on_device(): lax.psum_scatter(jnp.einsum('cb,bvi->cvi', selector, partials, precision=...]
    ppermute x0 -> x15, waiting for transfers between devices: none -> 11.1 us  [the longest x6 10.3 us: to_column(): lax.ppermute(x, 'loop', [(i, (i + 2 * shift) % count) for i in range(coun...]
    ppermute x0 -> x15, starting transfers between devices: none -> 9.91 us  [the longest x6 8.28 us: to_column(): lax.ppermute(x, 'loop', [(i, (i + 2 * shift) % count) for i in range(coun...]
    pallas_call x0 -> x16, Pallas kernels: none -> 9.46 us  [the longest x2 2.04 us: near_call(): call(functools.partial(near_kernel, len(given)), 'near', (panels((columns...]
    gather x4 -> x0, local copies, waits for them, and re-layouts: 4.38 us -> none  [the longest x2 2.96 us: on_device(): jnp.take(shard_rows, jnp.clip(source_global, 0, shard_rows.shape[0] - 1),...]
    reshape x3 -> x0, local copies, waits for them, and re-layouts: 3.66 us -> none  [the longest x2 2.01 us: on_device(): gathered.reshape(parents, far_count, vector_count, rank_size)]
  transfers between devices with their start and end apart: 2 -> 15, of which waited for: 2 -> 8; matrix products, arithmetic and copies ran while one was open for 14% -> 0% of each run, Pallas kernels for 0% -> 25%
where the time goes in v3:
time: 31 us; the launch traced here: 30.8 us
  waiting for transfers between devices  11.1 us (36%)
  starting transfers between devices  9.91 us (32%)
  Pallas kernels  9.46 us (31%)
    ppermute x6, waiting for transfers between devices, to_column(): lax.ppermute(x, 'loop', [(i, (i + 2 * shift) % count) for i in range(coun...  10.3 us
    ppermute x6, starting transfers between devices, to_column(): lax.ppermute(x, 'loop', [(i, (i + 2 * shift) % count) for i in range(coun...  8.28 us
    pallas_call x2, Pallas kernels, near_call(): call(functools.partial(near_kernel, len(given)), 'near', (panels((columns...  2.04 us
    pallas_call x1, Pallas kernels, on_device(): first_call(*in_hbm(*raw, vectors, column_basis, column_transfer))  1.94 us
    pallas_call x1, Pallas kernels, on_device(): turned = turn_call(*in_vmem(near_tiles))  1.67 us
    ppermute x9, starting transfers between devices, to_sibling(): return lax.ppermute(x, 'loop', sibling)  1.64 us
    pallas_call x2, Pallas kernels, self_call(): call(self_kernel, 'self', panels(clusters, F32), specs, us=us)  1.29 us
    pallas_call x2, Pallas kernels, far_call(): call(functools.partial(far_kernel, len(messages), rows), 'far', panels(cl...  1.12 us
  transfers between devices with their start and end apart: 15, of which 8 were waited for; matrix products, arithmetic and copies ran while one was open for 0% of the time, Pallas kernels for 25%

profile of v3, /device:TPU:0, one launch (start us, length us, event | category | flops | bytes accessed | tf_op | source)
XLA Modules:
  0.0 30.8 jit_solution(223266103897252600)
XLA Ops:
  0.0 3.0 %collective-permute-start.1 = (bf16[16,16,256]{2,1,0:T(8,128)(2,1)}, bf16[16,16,256]{2,1,0:T(8,128)(2,1)S(1)}, u32[]{:S(2)}, u32[]{:S(2)}) collective-permute-start(bf16[16,16,256]{2,1,0:T(8,128)(2,1)} %vectors.1), channel_id=1, source_target_pairs={{0,8},{4,12},{8,0},{12,4},{1,9},{5,13},{9,1},{13,5},{2,10},{6,14},... | collective-permute-start | bytes 393224 | tf_op jit(solution)/shard_map/ppermute | solution.py:327
  3.0 0.0 collective-permute-start
  3.0 1.9 %first.1 = (bf16[2,16,256]{2,1,0:T(8,128)(2,1)S(1)}, bf16[16,16,256]{2,1,0:T(8,128)(2,1)S(1)}, s32[16,128]{1,0:T(8,128)S(4)}) custom-call(s32[1,48]{1,0:T(1,128)} %bitcast.4, s32[1,48]{1,0:T(1,128)} %bitcast.5, s32[2,48]{1,0:T(2,128)} %bitcast.3, s32[8,8]{1,0:T(8,128)} %far_source.1, bf16[16,16,256]{2,1,0:T(8,128)(2,1)} %vectors.1, ...), custom_call_target="tpu_custom_call" | custom-call | flops 10000000000 | tf_op jit(solution)/shard_map/first/pallas_call | solution.py:415
  4.9 0.1 collective-permute-start.3
  5.0 1.7 %collective-permute-done.1.refs_2_ = bf16[16,16,256]{2,1,0:T(8,128)(2,1)S(1)} collective-permute-done((bf16[16,16,256]{2,1,0:T(8,128)(2,1)}, bf16[16,16,256]{2,1,0:T(8,128)(2,1)S(1)}, u32[]{:S(2)}, u32[]{:S(2)}) %collective-permute-start.1) | collective-permute-done | bytes 131104 | tf_op jit(solution)/shard_map/ppermute | solution.py:327
  6.7 0.1 collective-permute-start.2
  6.8 0.0 copy-done
  6.8 1.7 %turn.1.tiles = bf16[48,256,256]{2,1,0:T(8,128)(2,1)S(1)} custom-call(bf16[48,256,256]{2,1,0:T(8,128)(2,1)S(1)} %copy-done), custom_call_target="tpu_custom_call" | custom-call | flops 2500000000 | tf_op jit(solution)/shard_map/turn/pallas_call | solution.py:420
  8.5 0.0 copy-start.3
  8.5 0.0 copy-start.4
  8.5 0.0 copy-start.6
  8.5 0.0 copy-start.1
  8.5 0.2 collective-permute-done.3.refs_4_.refs_2_
  8.7 0.0 collective-permute-done.refs_1_
  8.7 0.0 collective-permute-done.2.refs_3_
  8.7 0.0 copy-start.5
  8.7 1.0 %near.2 = (bf16[16,16,256]{2,1,0:T(8,128)(2,1)S(1)}, bf16[16,16,256]{2,1,0:T(8,128)(2,1)S(1)}, f32[16,16,256]{2,1,0:T(8,128)S(1)}, f32[16,16,256]{2,1,0:T(8,128)S(1)}) custom-call(s32[16,128]{1,0:T(8,128)S(4)} %get-tuple-element.20.table, bf16[48,256,256]{2,1,0:T(8,128)(2,1)S(1)} %turn.1.tiles, bf16[16,16,256]{2,1,0:T(8,128)(2,1)S(1)} %get-tuple-element.21.refs_0_.current, ...), custom_call_target="tpu_custom_call" | custom-call | flops 1000000000 | tf_op jit(solution)/shard_map/near/pallas_call | solution.py:366
  9.8 0.4 %collective-permute-start.5 = (bf16[16,16,256]{2,1,0:T(8,128)(2,1)S(1)}, bf16[16,16,256]{2,1,0:T(8,128)(2,1)S(1)}, u32[]{:S(2)}, u32[]{:S(2)}) collective-permute-start(bf16[16,16,256]{2,1,0:T(8,128)(2,1)S(1)} %get-tuple-element.26), channel_id=1, source_target_pairs={{0,4},{4,0},{8,12},{12,8},{1,5},{5,1},{9,13},{13,9},{2,6},{6,2},{1... | collective-permute-start | bytes 393224 | tf_op jit(solution)/shard_map/ppermute | solution.py:324
  10.2 0.2 collective-permute-start.6
  10.4 0.3 collective-permute-start.4
  10.7 0.5 %collective-permute-done.5.arrived = bf16[16,16,256]{2,1,0:T(8,128)(2,1)S(1)} collective-permute-done((bf16[16,16,256]{2,1,0:T(8,128)(2,1)S(1)}, bf16[16,16,256]{2,1,0:T(8,128)(2,1)S(1)}, u32[]{:S(2)}, u32[]{:S(2)}) %collective-permute-start.5) | collective-permute-done | bytes 131104 | tf_op jit(solution)/shard_map/ppermute | solution.py:324
  11.2 1.8 %collective-permute-start.7 = (bf16[16,16,256]{2,1,0:T(8,128)(2,1)S(1)}, bf16[16,16,256]{2,1,0:T(8,128)(2,1)S(1)}, u32[]{:S(2)}, u32[]{:S(2)}) collective-permute-start(bf16[16,16,256]{2,1,0:T(8,128)(2,1)S(1)} %get-tuple-element.27.others_0_.sent_before), channel_id=1, source_target_pairs={{0,8},{4,12},{8,0},{12,4},{1,9},{5,13},{9,1},{13,5},{2,10},{6,14},... | collective-permute-start | bytes 393224 | tf_op jit(solution)/shard_map/ppermute | solution.py:327
  13.0 0.0 collective-permute-done.6
  13.0 0.6 %far.2.far_part = f32[16,16,256]{2,1,0:T(8,128)S(1)} custom-call(s32[16,128]{1,0:T(8,128)S(4)} %get-tuple-element.20.table, bf16[16,64,64]{2,1,0:T(8,128)(2,1)S(1)} %copy-done.6, bf16[16,64,256]{2,1,0:T(8,128)(2,1)S(1)} %copy-done.3, bf16[8,64,512]{2,1,0:T(8,128)(2,1)S(1)} %copy-done.4, bf16[2,16,256]{2,1,0:T(8,128)(2,1)S(1)} %get-tuple-element.22.refs_1_.refs_0_, ...), custom_call_target="tpu_custom_call" | custom-call | flops 500000000 | tf_op jit(solution)/shard_map/far/pallas_call | solution.py:387
  13.6 0.0 copy-done.1
  13.6 0.6 %self.2.self_part = f32[16,16,256]{2,1,0:T(8,128)S(1)} custom-call(bf16[16,16,256]{2,1,0:T(8,128)(2,1)S(1)} %get-tuple-element.21.refs_0_.current, bf16[16,256,256]{2,1,0:T(8,128)(2,1)S(1)} %copy-done.1, bf16[16,16,256]{2,1,0:T(8,128)(2,1)S(1)} %get-tuple-element.27.others_0_.sent_before), custom_call_target="tpu_custom_call" | custom-call | flops 600000000 | tf_op jit(solution)/shard_map/self/pallas_call | solution.py:361
  14.3 0.0 collective-permute-done.4.arrived
  14.3 0.1 own.1
  14.3 0.4 %collective-permute-start.11 = (bf16[16,16,256]{2,1,0:T(8,128)(2,1)S(1)}, bf16[16,16,256]{2,1,0:T(8,128)(2,1)S(1)}, u32[]{:S(2)}, u32[]{:S(2)}) collective-permute-start(bf16[16,16,256]{2,1,0:T(8,128)(2,1)S(1)} %get-tuple-element.30), channel_id=1, source_target_pairs={{0,8},{4,12},{8,0},{12,4},{1,9},{5,13},{9,1},{13,5},{2,10},{6,14},... | collective-permute-start | bytes 393224 | tf_op jit(solution)/shard_map/ppermute | solution.py:327
  14.7 2.3 %collective-permute-done.7.message = bf16[16,16,256]{2,1,0:T(8,128)(2,1)S(1)} collective-permute-done((bf16[16,16,256]{2,1,0:T(8,128)(2,1)S(1)}, bf16[16,16,256]{2,1,0:T(8,128)(2,1)S(1)}, u32[]{:S(2)}, u32[]{:S(2)}) %collective-permute-start.7) | collective-permute-done | bytes 131104 | tf_op jit(solution)/shard_map/ppermute | solution.py:327
  17.0 0.1 collective-permute-start.10
  17.1 0.5 %coeffs.1.refs_0_.others_0_.refs_4_ = bf16[2,16,256]{2,1,0:T(8,128)(2,1)S(1)} custom-call(bf16[16,16,256]{2,1,0:T(8,128)(2,1)S(1)} %settle.2.current.refs_0_, bf16[16,64,256]{2,1,0:T(8,128)(2,1)S(1)} %copy-done.2, bf16[16,64,64]{2,1,0:T(8,128)(2,1)S(1)} %copy-done.5), custom_call_target="tpu_custom_call" | custom-call | flops 500000000 | tf_op jit(solution)/shard_map/coeffs/pallas_call | solution.py:445
  17.6 2.3 %collective-permute-done.11.message = bf16[16,16,256]{2,1,0:T(8,128)(2,1)S(1)} collective-permute-done((bf16[16,16,256]{2,1,0:T(8,128)(2,1)S(1)}, bf16[16,16,256]{2,1,0:T(8,128)(2,1)S(1)}, u32[]{:S(2)}, u32[]{:S(2)}) %collective-permute-start.11) | collective-permute-done | bytes 131104 | tf_op jit(solution)/shard_map/ppermute | solution.py:327
  19.9 0.0 collective-permute-done.10.others_1_.refs_1_
  19.9 0.1 collective-permute-start.12
  20.0 1.7 %collective-permute-start.8 = (bf16[2,16,256]{2,1,0:T(8,128)(2,1)S(1)}, bf16[2,16,256]{2,1,0:T(8,128)(2,1)S(1)}, u32[]{:S(2)}, u32[]{:S(2)}) collective-permute-start(bf16[2,16,256]{2,1,0:T(8,128)(2,1)S(1)} %coeffs.1.refs_0_.others_0_.refs_4_), channel_id=1, source_target_pairs={{0,8},{4,12},{8,0},{12,4},{1,9},{5,13},{9,1},{13,5},{2,10},{6,14},... | collective-permute-start | bytes 49160 | tf_op jit(solution)/shard_map/ppermute | solution.py:327
  21.7 0.0 collective-permute-done.12.refs_3_
  21.7 1.0 %near.3 = (bf16[16,16,256]{2,1,0:T(8,128)(2,1)S(1)}, bf16[16,16,256]{2,1,0:T(8,128)(2,1)S(1)}, f32[16,16,256]{2,1,0:T(8,128)S(1)}, f32[16,16,256]{2,1,0:T(8,128)S(1)}) custom-call(s32[16,128]{1,0:T(8,128)S(4)} %get-tuple-element.20.table, bf16[48,256,256]{2,1,0:T(8,128)(2,1)S(1)} %turn.1.tiles, bf16[16,16,256]{2,1,0:T(8,128)(2,1)S(1)} %settle.2.current.refs_0_, ...), custom_call_target="tpu_custom_call" | custom-call | flops 1000000000 | tf_op jit(solution)/shard_map/near/pallas_call | solution.py:366
  22.8 0.2 collective-permute-start.13
  23.0 0.6 %self.3.self_part = f32[16,16,256]{2,1,0:T(8,128)S(1)} custom-call(bf16[16,16,256]{2,1,0:T(8,128)(2,1)S(1)} %settle.2.current.refs_0_, bf16[16,256,256]{2,1,0:T(8,128)(2,1)S(1)} %copy-done.1), custom_call_target="tpu_custom_call" | custom-call | flops 2500000000 | tf_op jit(solution)/shard_map/self/pallas_call | solution.py:361
  23.7 0.1 collective-permute-done.8.refs_2_.column_coeffs
  23.8 0.3 %collective-permute-start.9 = (bf16[4,16,256]{2,1,0:T(8,128)(2,1)S(1)}, bf16[4,16,256]{2,1,0:T(8,128)(2,1)S(1)}, u32[]{:S(2)}, u32[]{:S(2)}) collective-permute-start(bf16[4,16,256]{2,1,0:T(8,128)(2,1)S(1)} %pad_maximum_fusion.2), channel_id=1, source_target_pairs={{0,4},{4,0},{8,12},{12,8},{1,5},{5,1},{9,13},{13,9},{2,6},{6,2},{1... | collective-permute-start | bytes 98312 | tf_op jit(solution)/shard_map/ppermute | solution.py:324
  24.1 0.3 collective-permute-done.13
  24.5 1.3 %collective-permute-start.14 = (bf16[16,16,256]{2,1,0:T(8,128)(2,1)S(1)}, bf16[16,16,256]{2,1,0:T(8,128)(2,1)S(1)}, u32[]{:S(2)}, u32[]{:S(2)}) collective-permute-start(bf16[16,16,256]{2,1,0:T(8,128)(2,1)S(1)} %cross.1), channel_id=1, source_target_pairs={{0,8},{4,12},{8,0},{12,4},{1,9},{5,13},{9,1},{13,5},{2,10},{6,14},... | collective-permute-start | bytes 393224 | tf_op jit(solution)/shard_map/ppermute | solution.py:327
  25.8 0.0 collective-permute-done.9
  25.8 0.6 %far.3.far_part = f32[16,16,256]{2,1,0:T(8,128)S(1)} custom-call(s32[16,128]{1,0:T(8,128)S(4)} %get-tuple-element.20.table, bf16[16,64,64]{2,1,0:T(8,128)(2,1)S(1)} %copy-done.6, bf16[16,64,256]{2,1,0:T(8,128)(2,1)S(1)} %copy-done.3, bf16[8,64,512]{2,1,0:T(8,128)(2,1)S(1)} %copy-done.4, bf16[2,16,256]{2,1,0:T(8,128)(2,1)S(1)} %coeffs.1.refs_0_.others_0_.refs_4_, ...), custom_call_target="tpu_custom_call" | custom-call | flops 500000000 | tf_op jit(solution)/shard_map/far/pallas_call | solution.py:387
  26.4 3.7 %collective-permute-done.14.message = bf16[16,16,256]{2,1,0:T(8,128)(2,1)S(1)} collective-permute-done((bf16[16,16,256]{2,1,0:T(8,128)(2,1)S(1)}, bf16[16,16,256]{2,1,0:T(8,128)(2,1)S(1)}, u32[]{:S(2)}, u32[]{:S(2)}) %collective-permute-start.14) | collective-permute-done | bytes 131104 | tf_op jit(solution)/shard_map/ppermute | solution.py:327
  30.1 0.7 %last.1 = bf16[16,16,256]{2,1,0:T(8,128)(2,1)} custom-call(f32[16,16,256]{2,1,0:T(8,128)S(1)} %self.3.self_part, f32[16,16,256]{2,1,0:T(8,128)S(1)} %far.3.far_part, f32[16,16,256]{2,1,0:T(8,128)S(1)} %get-tuple-element.31.keep, bf16[16,16,256]{2,1,0:T(8,128)(2,1)S(1)} %get-tuple-element.36.arrived, bf16[16,16,256]{2,1,0:T(8,128)(2,1)S(1)} %collective-permute-done.14.message), custom_call_target="tpu_custom_call" | custom-call | flops 100000000 | tf_op jit(solution)/shard_map/last/pallas_call | solution.py:460
  (19 shorter events, 0.2 us)
Async XLA Ops:
  0.0 6.7 %collective-permute-start.1 = (bf16[16,16,256]{2,1,0:T(8,128)(2,1)}, bf16[16,16,256]{2,1,0:T(8,128)(2,1)S(1)}, u32[]{:S(2)}, u32[]{:S(2)}) collective-permute-start(bf16[16,16,256]{2,1,0:T(8,128)(2,1)} %vectors.1), channel_id=1, source_target_pairs={{0,8},{4,12},{8,0},{12,4},{1,9},{5,13},{9,1},{13,5},{2,10},{6,14},... | collective-permute-start | bytes 393224 | tf_op jit(solution)/shard_map/ppermute | solution.py:327
  3.0 5.8 %collective-permute-start = (bf16[16,16,256]{2,1,0:T(8,128)(2,1)}, bf16[16,16,256]{2,1,0:T(8,128)(2,1)S(1)}, u32[]{:S(2)}, u32[]{:S(2)}) collective-permute-start(bf16[16,16,256]{2,1,0:T(8,128)(2,1)} %vectors.1), channel_id=1, source_target_pairs={{0,4},{4,0},{8,12},{12,8},{1,5},{5,1},{9,13},{13,9},{2,6},{6,2},{1... | collective-permute-start | bytes 393224 | tf_op jit(solution)/shard_map/ppermute | solution.py:324
  3.0 3.8 %copy-start = (bf16[48,256,256]{2,1,0:T(8,128)(2,1)S(1)}, bf16[48,256,256]{2,1,0:T(8,128)(2,1)}, u32[]{:S(2)}) copy-start(bf16[48,256,256]{2,1,0:T(8,128)(2,1)} %tiles.1) | copy-start | bytes 18874372
  4.9 3.8 %collective-permute-start.3 = (bf16[2,16,256]{2,1,0:T(8,128)(2,1)S(1)}, bf16[2,16,256]{2,1,0:T(8,128)(2,1)S(1)}, u32[]{:S(2)}, u32[]{:S(2)}) collective-permute-start(bf16[2,16,256]{2,1,0:T(8,128)(2,1)S(1)} %get-tuple-element.22.refs_1_.refs_0_), channel_id=1, source_target_pairs={{0,8},{4,12},{8,0},{12,4},{1,9},{5,13},{9,1},{13,5},{2,10},{6,14},... | collective-permute-start | bytes 49160 | tf_op jit(solution)/shard_map/ppermute | solution.py:327
  6.7 2.0 %collective-permute-start.2 = (bf16[16,16,256]{2,1,0:T(8,128)(2,1)S(1)}, bf16[16,16,256]{2,1,0:T(8,128)(2,1)S(1)}, u32[]{:S(2)}, u32[]{:S(2)}) collective-permute-start(bf16[16,16,256]{2,1,0:T(8,128)(2,1)S(1)} %tie.1), channel_id=1, source_target_pairs={{0,4},{4,0},{8,12},{12,8},{1,5},{5,1},{9,13},{13,9},{2,6},{6,2},{1... | collective-permute-start | bytes 393224 | tf_op jit(solution)/shard_map/ppermute | solution.py:324
  8.5 4.5 %copy-start.3 = (bf16[16,64,256]{2,1,0:T(8,128)(2,1)S(1)}, bf16[16,64,256]{2,1,0:T(8,128)(2,1)}, u32[]{:S(2)}) copy-start(bf16[16,64,256]{2,1,0:T(8,128)(2,1)} %row_basis.3) | copy-start | bytes 1572868
  8.5 4.5 %copy-start.4 = (bf16[8,64,512]{2,1,0:T(8,128)(2,1)S(1)}, bf16[8,64,512]{2,1,0:T(8,128)(2,1)}, u32[]{:S(2)}) copy-start(bf16[8,64,512]{2,1,0:T(8,128)(2,1)} %coupling.3) | copy-start | bytes 1572868
  8.5 4.5 %copy-start.6 = (bf16[16,64,64]{2,1,0:T(8,128)(2,1)S(1)}, bf16[16,64,64]{2,1,0:T(8,128)(2,1)}, u32[]{:S(2)}) copy-start(bf16[16,64,64]{2,1,0:T(8,128)(2,1)} %row_transfer.3) | copy-start | bytes 393220
  8.5 5.1 %copy-start.1 = (bf16[16,256,256]{2,1,0:T(8,128)(2,1)S(1)}, bf16[16,256,256]{2,1,0:T(8,128)(2,1)}, u32[]{:S(2)}) copy-start(bf16[16,256,256]{2,1,0:T(8,128)(2,1)} %self_tiles.3) | copy-start | bytes 6291460
  8.7 8.4 %copy-start.2 = (bf16[16,64,256]{2,1,0:T(8,128)(2,1)S(1)}, bf16[16,64,256]{2,1,0:T(8,128)(2,1)}, u32[]{:S(2)}) copy-start(bf16[16,64,256]{2,1,0:T(8,128)(2,1)} %column_basis.3) | copy-start | bytes 1572868
  8.7 8.4 %copy-start.5 = (bf16[16,64,64]{2,1,0:T(8,128)(2,1)S(1)}, bf16[16,64,64]{2,1,0:T(8,128)(2,1)}, u32[]{:S(2)}) copy-start(bf16[16,64,64]{2,1,0:T(8,128)(2,1)} %column_transfer.3) | copy-start | bytes 393220
  9.8 1.4 %collective-permute-start.5 = (bf16[16,16,256]{2,1,0:T(8,128)(2,1)S(1)}, bf16[16,16,256]{2,1,0:T(8,128)(2,1)S(1)}, u32[]{:S(2)}, u32[]{:S(2)}) collective-permute-start(bf16[16,16,256]{2,1,0:T(8,128)(2,1)S(1)} %get-tuple-element.26), channel_id=1, source_target_pairs={{0,4},{4,0},{8,12},{12,8},{1,5},{5,1},{9,13},{13,9},{2,6},{6,2},{1... | collective-permute-start | bytes 393224 | tf_op jit(solution)/shard_map/ppermute | solution.py:324
  10.2 2.8 %collective-permute-start.6 = (bf16[4,16,256]{2,1,0:T(8,128)(2,1)S(1)}, bf16[4,16,256]{2,1,0:T(8,128)(2,1)S(1)}, u32[]{:S(2)}, u32[]{:S(2)}) collective-permute-start(bf16[4,16,256]{2,1,0:T(8,128)(2,1)S(1)} %pad_maximum_fusion.1), channel_id=1, source_target_pairs={{0,4},{4,0},{8,12},{12,8},{1,5},{5,1},{9,13},{13,9},{2,6},{6,2},{1... | collective-permute-start | bytes 98312 | tf_op jit(solution)/shard_map/ppermute | solution.py:324
  10.4 3.9 %collective-permute-start.4 = (bf16[16,16,256]{2,1,0:T(8,128)(2,1)S(1)}, bf16[16,16,256]{2,1,0:T(8,128)(2,1)S(1)}, u32[]{:S(2)}, u32[]{:S(2)}) collective-permute-start(bf16[16,16,256]{2,1,0:T(8,128)(2,1)S(1)} %get-tuple-element.24), channel_id=1, source_target_pairs={{0,4},{4,0},{8,12},{12,8},{1,5},{5,1},{9,13},{13,9},{2,6},{6,2},{1... | collective-permute-start | bytes 393224 | tf_op jit(solution)/shard_map/ppermute | solution.py:324
  11.2 5.8 %collective-permute-start.7 = (bf16[16,16,256]{2,1,0:T(8,128)(2,1)S(1)}, bf16[16,16,256]{2,1,0:T(8,128)(2,1)S(1)}, u32[]{:S(2)}, u32[]{:S(2)}) collective-permute-start(bf16[16,16,256]{2,1,0:T(8,128)(2,1)S(1)} %get-tuple-element.27.others_0_.sent_before), channel_id=1, source_target_pairs={{0,8},{4,12},{8,0},{12,4},{1,9},{5,13},{9,1},{13,5},{2,10},{6,14},... | collective-permute-start | bytes 393224 | tf_op jit(solution)/shard_map/ppermute | solution.py:327
  14.3 5.5 %collective-permute-start.11 = (bf16[16,16,256]{2,1,0:T(8,128)(2,1)S(1)}, bf16[16,16,256]{2,1,0:T(8,128)(2,1)S(1)}, u32[]{:S(2)}, u32[]{:S(2)}) collective-permute-start(bf16[16,16,256]{2,1,0:T(8,128)(2,1)S(1)} %get-tuple-element.30), channel_id=1, source_target_pairs={{0,8},{4,12},{8,0},{12,4},{1,9},{5,13},{9,1},{13,5},{2,10},{6,14},... | collective-permute-start | bytes 393224 | tf_op jit(solution)/shard_map/ppermute | solution.py:327
  17.0 2.9 %collective-permute-start.10 = (bf16[16,16,256]{2,1,0:T(8,128)(2,1)S(1)}, bf16[16,16,256]{2,1,0:T(8,128)(2,1)S(1)}, u32[]{:S(2)}, u32[]{:S(2)}) collective-permute-start(bf16[16,16,256]{2,1,0:T(8,128)(2,1)S(1)} %settle.2.current.refs_0_), channel_id=1, source_target_pairs={{0,4},{4,0},{8,12},{12,8},{1,5},{5,1},{9,13},{13,9},{2,6},{6,2},{1... | collective-permute-start | bytes 393224 | tf_op jit(solution)/shard_map/ppermute | solution.py:324
  19.9 1.8 %collective-permute-start.12 = (bf16[16,16,256]{2,1,0:T(8,128)(2,1)S(1)}, bf16[16,16,256]{2,1,0:T(8,128)(2,1)S(1)}, u32[]{:S(2)}, u32[]{:S(2)}) collective-permute-start(bf16[16,16,256]{2,1,0:T(8,128)(2,1)S(1)} %settle.3.refs_2_), channel_id=1, source_target_pairs={{0,4},{4,0},{8,12},{12,8},{1,5},{5,1},{9,13},{13,9},{2,6},{6,2},{1... | collective-permute-start | bytes 393224 | tf_op jit(solution)/shard_map/ppermute | solution.py:324
  20.0 3.8 %collective-permute-start.8 = (bf16[2,16,256]{2,1,0:T(8,128)(2,1)S(1)}, bf16[2,16,256]{2,1,0:T(8,128)(2,1)S(1)}, u32[]{:S(2)}, u32[]{:S(2)}) collective-permute-start(bf16[2,16,256]{2,1,0:T(8,128)(2,1)S(1)} %coeffs.1.refs_0_.others_0_.refs_4_), channel_id=1, source_target_pairs={{0,8},{4,12},{8,0},{12,4},{1,9},{5,13},{9,1},{13,5},{2,10},{6,14},... | collective-permute-start | bytes 49160 | tf_op jit(solution)/shard_map/ppermute | solution.py:327
  22.8 1.6 %collective-permute-start.13 = (bf16[32,16,256]{2,1,0:T(8,128)(2,1)S(1)}, bf16[32,16,256]{2,1,0:T(8,128)(2,1)S(1)}, u32[]{:S(2)}, u32[]{:S(2)}) collective-permute-start(bf16[32,16,256]{2,1,0:T(8,128)(2,1)S(1)} %pad_maximum_fusion), channel_id=1, source_target_pairs={{0,4},{4,0},{8,12},{12,8},{1,5},{5,1},{9,13},{13,9},{2,6},{6,2},{1... | collective-permute-start | bytes 786440 | tf_op jit(solution)/shard_map/ppermute | solution.py:324
  23.8 2.0 %collective-permute-start.9 = (bf16[4,16,256]{2,1,0:T(8,128)(2,1)S(1)}, bf16[4,16,256]{2,1,0:T(8,128)(2,1)S(1)}, u32[]{:S(2)}, u32[]{:S(2)}) collective-permute-start(bf16[4,16,256]{2,1,0:T(8,128)(2,1)S(1)} %pad_maximum_fusion.2), channel_id=1, source_target_pairs={{0,4},{4,0},{8,12},{12,8},{1,5},{5,1},{9,13},{13,9},{2,6},{6,2},{1... | collective-permute-start | bytes 98312 | tf_op jit(solution)/shard_map/ppermute | solution.py:324
  24.5 5.6 %collective-permute-start.14 = (bf16[16,16,256]{2,1,0:T(8,128)(2,1)S(1)}, bf16[16,16,256]{2,1,0:T(8,128)(2,1)S(1)}, u32[]{:S(2)}, u32[]{:S(2)}) collective-permute-start(bf16[16,16,256]{2,1,0:T(8,128)(2,1)S(1)} %cross.1), channel_id=1, source_target_pairs={{0,8},{4,12},{8,0},{12,4},{1,9},{5,13},{9,1},{13,5},{2,10},{6,14},... | collective-permute-start | bytes 393224 | tf_op jit(solution)/shard_map/ppermute | solution.py:327

commit v4 on v3

--- a/solution.py
+++ b/solution.py
@@ -183,6 +183,32 @@
     keep[...] = sums[half + own :]
 
 
+def near_half(half, table, tiles, gathered, send, keep, products, sums):
+    lanes = send.shape[2]
+    sums[...] = jnp.zeros_like(sums)
+    blocks = tiles.shape[0]
+    for b in range(blocks):
+        tile = tiles[b, :, half * lanes : (half + 1) * lanes]
+        products[b] = dot(gathered[table[0, b]], tile, ROWS_BY_COLUMNS)
+    for b in range(blocks):
+        sums[table[1, b]] += products[b]
+    middle = send.shape[0]
+    send[...] = sums[:middle].astype(BF16)
+    keep[...] = sums[middle:]
+
+
+def first_half_kernel(panel_count, table, tiles, *refs):
+    panels, (send, keep, gathered, products, sums) = refs[:panel_count], refs[-5:]
+    each = gathered.shape[0] // panel_count
+    for k, panel in enumerate(panels):
+        gathered[k * each : (k + 1) * each] = panel[:each]
+    near_half(0, table, tiles, gathered, send, keep, products, sums)
+
+
+def second_half_kernel(table, tiles, gathered, send, keep, products, sums):
+    near_half(1, table, tiles, gathered, send, keep, products, sums)
+
+
 def far_products(table, row_transfer, row_basis, coupling, gathered, store):
     vectors, lanes = gathered.shape[1:]
     rank, leaf_size = row_basis.shape[1:]
@@ -240,12 +266,22 @@
     current[...] = (sums[...] + message[...].astype(F32)).astype(BF16)
 
 
-def cross_kernel(keep, arrived, self_part, column_coeffs, message):
-    message[...] = (keep[...] + arrived[...].astype(F32)).astype(BF16)
-
-
-def last_kernel(self_part, far_part, keep, arrived, message, product):
-    near = keep[...] + arrived[...].astype(F32) + message[...].astype(F32)
+def cross_kernel(keep, arrived, *refs):
+    message = refs[-1]
+    half = message.shape[0]
+    message[...] = (keep[half:] + arrived[half:].astype(F32)).astype(BF16)
+
+
+def last_kernel(*refs):
+    keep, arrived, crossed, (self_part, far_part, product) = (
+        refs[:2], refs[2:4], refs[4:6], refs[6:]
+    )
+    count = product.shape[0]
+    halves = [
+        k[:count] + a[:count].astype(F32) + x[...].astype(F32)
+        for k, a, x in zip(keep, arrived, crossed)
+    ]
+    near = jnp.concatenate(halves, axis=-1)
     product[...] = (self_part[...] + far_part[...] + near).astype(BF16)
 
 
@@ -329,8 +365,8 @@
     def across(x):
         return [to_column(x, shift) for shift in range(1, columns)]
 
-    def panels(number, dtype):
-        return jax.ShapeDtypeStruct((number, vector_count, leaf_size), dtype)
+    def panels(number, dtype, width=leaf_size):
+        return jax.ShapeDtypeStruct((number, vector_count, width), dtype)
 
     def scratch(number, dtype, width=leaf_size):
         return pltpu.VMEM((number, vector_count, width), dtype)
@@ -381,6 +417,28 @@
             us=1.0,
         )(in_smem(table), *in_vmem(turned, *given), *others)
 
+    half_size = leaf_size // 2
+
+    def half_calls(table, turned, given):
+        outs = (
+            panels(columns * clusters, BF16, half_size),
+            panels(columns * clusters, F32, half_size),
+        )
+        scratches = [scratch(blocks, F32, half_size), scratch(count * clusters, F32, half_size)]
+        send, keep, gathered = call(
+            functools.partial(first_half_kernel, len(given)),
+            "first_half",
+            (*outs, scratch(count * clusters, BF16)),
+            [SMEM_SPEC] + [VMEM_SPEC] * (1 + len(given)),
+            scratches,
+            us=0.5,
+        )(in_smem(table), *in_vmem(turned, *given))
+        next_send, next_keep = call(
+            second_half_kernel, "second_half", outs, [SMEM_SPEC] + [VMEM_SPEC] * 2, scratches, us=0.5
+        )(in_smem(table), *in_vmem(turned, gathered))
+        arrived = (to_sibling(send), to_sibling(next_send))
+        return (keep, next_keep), arrived
+
     gathered_coeffs = scratch(count * parents, BF16, 2 * rank)
 
     def far_call(table, messages):
@@ -399,10 +457,6 @@
             gathered += [x, to_sibling(tie(x, *others) if others else x)]
         return gathered
 
-    def both_to_sibling(send, send_own):
-        arrived = to_sibling(jnp.concatenate([send, send_own]))
-        return arrived[: send.shape[0]], arrived[send.shape[0] :]
-
     def all_coeffs(packed, crossed):
         beside = to_sibling(jnp.concatenate([packed, *crossed]))
         pieces = []
@@ -411,9 +465,8 @@
         return pieces
 
     crossed = across(vectors)
-    beside = to_sibling(vectors)
     packed, current, table = first_call(*in_hbm(*raw, vectors, column_basis, column_transfer))
-    given = [current, beside]
+    given = [current, to_sibling(current)]
     for x in crossed:
         given += [x, to_sibling(tie(x, packed))]
     crossed = across(packed)
@@ -446,19 +499,23 @@
         packed_column = to_column(packed, 1)
         column = settled(other_sums, own, packed, beside)
         given = [current, beside, column, to_sibling(column)]
-        send, send_own, keep, keep_own = near_call(table, turned, given, packed)
-        arrived, arrived_own = both_to_sibling(send, send_own)
+        keep, arrived = half_calls(table, turned, given)
         self_part = self_call(current, us=2.5)
-        crossing = call(
-            cross_kernel,
-            "cross",
-            panels(clusters, BF16),
-            [VMEM_SPEC] * 2 + [ANY_SPEC] * 2,
-            us=0.1,
-        )(*in_vmem(keep, arrived), self_part, packed_column)
+        crossing = []
+        for one_keep, one_arrived, first in zip(keep, arrived, ((self_part,), (self_part, packed_column))):
+            others = (*first, *crossing)
+            crossing.append(
+                call(
+                    cross_kernel,
+                    "cross",
+                    panels(clusters, BF16, half_size),
+                    [VMEM_SPEC] * 2 + [ANY_SPEC] * len(others),
+                    us=1.0,
+                )(*in_vmem(one_keep, one_arrived), *others)
+            )
         far_part = far_call(table, all_coeffs(packed, [packed_column]))
-        return call(last_kernel, "last", panels(clusters, BF16), [VMEM_SPEC] * 5, us=0.1)(
-            *in_vmem(self_part, far_part, keep_own, arrived_own, to_column(crossing, 1))
+        return call(last_kernel, "last", panels(clusters, BF16), [VMEM_SPEC] * 8, us=0.1)(
+            *in_vmem(*keep, *arrived, *(to_column(x, 1) for x in crossing), self_part, far_part)
         )
 
     self_part = self_call(current)

time: 31 us -> 30.4 us (0.981)
  waiting for transfers between devices: 11.1 us -> 8.24 us
  starting transfers between devices: 9.91 us -> 12.1 us
    ppermute x6 -> x7, waiting for transfers between devices: 10.3 us -> 7.12 us  [to_column(): lax.ppermute(x, 'loop', [(i, (i + 2 * shift) % count) for i in range(coun...]
    ppermute x6 -> x7, starting transfers between devices: 8.28 us -> 9.9 us  [to_column(): lax.ppermute(x, 'loop', [(i, (i + 2 * shift) % count) for i in range(coun...]
    pallas_call x2 -> x5, Pallas kernels: 0.76 us -> 1.92 us  [the longest x1 0.72 us: on_device(): call(last_kernel, 'last', panels(clusters, BF16), [VMEM_SPEC] * 8, us=0.1)]
    pallas_call x2 -> x1, Pallas kernels: 2.04 us -> 1.02 us  [near_call(): call(functools.partial(near_kernel, len(given)), 'near', (panels((columns...]
    ppermute x9 -> x10, starting transfers between devices: 1.64 us -> 2.19 us  [to_sibling(): return lax.ppermute(x, 'loop', sibling)]
    ppermute x9 -> x10, waiting for transfers between devices: 0.83 us -> 1.12 us  [to_sibling(): return lax.ppermute(x, 'loop', sibling)]
  transfers between devices with their start and end apart: 15 -> 17, of which waited for: 8 -> 7; matrix products, arithmetic and copies ran while one was open for 0% -> 0% of each run, Pallas kernels for 25% -> 26%
where the time goes in v4:
time: 30.4 us; the launch traced here: 30.2 us
  starting transfers between devices  12.1 us (40%)
  Pallas kernels  9.6 us (32%)
  waiting for transfers between devices  8.24 us (27%)
    ppermute x7, starting transfers between devices, to_column(): lax.ppermute(x, 'loop', [(i, (i + 2 * shift) % count) for i in range(coun...  9.9 us
    ppermute x7, waiting for transfers between devices, to_column(): lax.ppermute(x, 'loop', [(i, (i + 2 * shift) % count) for i in range(coun...  7.12 us
    ppermute x10, starting transfers between devices, to_sibling(): return lax.ppermute(x, 'loop', sibling)  2.19 us
    pallas_call x1, Pallas kernels, on_device(): first_call(*in_hbm(*raw, vectors, column_basis, column_transfer))  1.94 us
    pallas_call x1, Pallas kernels, on_device(): turned = turn_call(*in_vmem(near_tiles))  1.67 us
    pallas_call x2, Pallas kernels, self_call(): call(self_kernel, 'self', panels(clusters, F32), specs, us=us)  1.29 us
    ppermute x10, waiting for transfers between devices, to_sibling(): return lax.ppermute(x, 'loop', sibling)  1.12 us
    pallas_call x2, Pallas kernels, far_call(): call(functools.partial(far_kernel, len(messages), rows), 'far', panels(cl...  1.12 us
  transfers between devices with their start and end apart: 17, of which 7 were waited for; matrix products, arithmetic and copies ran while one was open for 0% of the time, Pallas kernels for 26%

profile of v4, /device:TPU:0, one launch (start us, length us, event | category | flops | bytes accessed | tf_op | source)
XLA Modules:
  0.0 30.2 jit_solution(10272293389818947139)
XLA Ops:
  0.0 3.0 %collective-permute-start.1 = (bf16[16,16,256]{2,1,0:T(8,128)(2,1)}, bf16[16,16,256]{2,1,0:T(8,128)(2,1)S(1)}, u32[]{:S(2)}, u32[]{:S(2)}) collective-permute-start(bf16[16,16,256]{2,1,0:T(8,128)(2,1)} %vectors.1), channel_id=1, source_target_pairs={{0,8},{4,12},{8,0},{12,4},{1,9},{5,13},{9,1},{13,5},{2,10},{6,14},... | collective-permute-start | bytes 393224 | tf_op jit(solution)/shard_map/ppermute | solution.py:363
  3.0 1.9 %first.1 = (bf16[2,16,256]{2,1,0:T(8,128)(2,1)S(1)}, bf16[16,16,256]{2,1,0:T(8,128)(2,1)S(1)}, s32[16,128]{1,0:T(8,128)S(4)}) custom-call(s32[1,48]{1,0:T(1,128)} %bitcast.4, s32[1,48]{1,0:T(1,128)} %bitcast.5, s32[2,48]{1,0:T(2,128)} %bitcast.3, s32[8,8]{1,0:T(8,128)} %far_source.1, bf16[16,16,256]{2,1,0:T(8,128)(2,1)} %vectors.1, ...), custom_call_target="tpu_custom_call" | custom-call | flops 10000000000 | tf_op jit(solution)/shard_map/first/pallas_call | solution.py:468
  4.9 0.1 collective-permute-start
  5.0 0.1 collective-permute-start.3
  5.1 1.6 %collective-permute-done.1.refs_2_ = bf16[16,16,256]{2,1,0:T(8,128)(2,1)S(1)} collective-permute-done((bf16[16,16,256]{2,1,0:T(8,128)(2,1)}, bf16[16,16,256]{2,1,0:T(8,128)(2,1)S(1)}, u32[]{:S(2)}, u32[]{:S(2)}) %collective-permute-start.1) | collective-permute-done | bytes 131104 | tf_op jit(solution)/shard_map/ppermute | solution.py:363
  6.7 0.1 collective-permute-start.2
  6.8 1.7 %turn.1.tiles = bf16[48,256,256]{2,1,0:T(8,128)(2,1)S(1)} custom-call(bf16[48,256,256]{2,1,0:T(8,128)(2,1)S(1)} %copy-done), custom_call_target="tpu_custom_call" | custom-call | flops 2500000000 | tf_op jit(solution)/shard_map/turn/pallas_call | solution.py:473
  8.5 0.0 copy-start.3
  8.5 0.0 copy-start.4
  8.5 0.0 copy-start.6
  8.5 0.0 copy-start.1
  8.5 0.3 collective-permute-done.3.refs_4_.refs_2_
  8.8 0.0 collective-permute-done.refs_1_
  8.8 0.0 copy-start.5
  8.8 1.0 %near.1 = (bf16[16,16,256]{2,1,0:T(8,128)(2,1)S(1)}, bf16[16,16,256]{2,1,0:T(8,128)(2,1)S(1)}, f32[16,16,256]{2,1,0:T(8,128)S(1)}, f32[16,16,256]{2,1,0:T(8,128)S(1)}) custom-call(s32[16,128]{1,0:T(8,128)S(4)} %get-tuple-element.21.table, bf16[48,256,256]{2,1,0:T(8,128)(2,1)S(1)} %turn.1.tiles, bf16[16,16,256]{2,1,0:T(8,128)(2,1)S(1)} %get-tuple-element.22.refs_0_.current, ...), custom_call_target="tpu_custom_call" | custom-call | flops 1000000000 | tf_op jit(solution)/shard_map/near/pallas_call | solution.py:402
  9.9 0.3 collective-permute-start.5
  10.2 0.3 collective-permute-start.6
  10.4 0.2 collective-permute-start.4
  10.7 0.6 %collective-permute-done.5.arrived = bf16[16,16,256]{2,1,0:T(8,128)(2,1)S(1)} collective-permute-done((bf16[16,16,256]{2,1,0:T(8,128)(2,1)S(1)}, bf16[16,16,256]{2,1,0:T(8,128)(2,1)S(1)}, u32[]{:S(2)}, u32[]{:S(2)}) %collective-permute-start.5) | collective-permute-done | bytes 131104 | tf_op jit(solution)/shard_map/ppermute | solution.py:360
  11.3 1.7 %collective-permute-start.7 = (bf16[16,16,256]{2,1,0:T(8,128)(2,1)S(1)}, bf16[16,16,256]{2,1,0:T(8,128)(2,1)S(1)}, u32[]{:S(2)}, u32[]{:S(2)}) collective-permute-start(bf16[16,16,256]{2,1,0:T(8,128)(2,1)S(1)} %get-tuple-element.28.others_0_.sent_before), channel_id=1, source_target_pairs={{0,8},{4,12},{8,0},{12,4},{1,9},{5,13},{9,1},{13,5},{2,10},{6,14},... | collective-permute-start | bytes 393224 | tf_op jit(solution)/shard_map/ppermute | solution.py:363
  13.0 0.6 %far.2.far_part = f32[16,16,256]{2,1,0:T(8,128)S(1)} custom-call(s32[16,128]{1,0:T(8,128)S(4)} %get-tuple-element.21.table, bf16[16,64,64]{2,1,0:T(8,128)(2,1)S(1)} %copy-done.6, bf16[16,64,256]{2,1,0:T(8,128)(2,1)S(1)} %copy-done.3, bf16[8,64,512]{2,1,0:T(8,128)(2,1)S(1)} %copy-done.4, bf16[2,16,256]{2,1,0:T(8,128)(2,1)S(1)} %get-tuple-element.23.refs_1_.refs_0_, ...), custom_call_target="tpu_custom_call" | custom-call | flops 500000000 | tf_op jit(solution)/shard_map/far/pallas_call | solution.py:445
  13.6 0.0 copy-done.1
  13.6 0.6 %self.2.self_part = f32[16,16,256]{2,1,0:T(8,128)S(1)} custom-call(bf16[16,16,256]{2,1,0:T(8,128)(2,1)S(1)} %get-tuple-element.22.refs_0_.current, bf16[16,256,256]{2,1,0:T(8,128)(2,1)S(1)} %copy-done.1, bf16[16,16,256]{2,1,0:T(8,128)(2,1)S(1)} %get-tuple-element.28.others_0_.sent_before), custom_call_target="tpu_custom_call" | custom-call | flops 600000000 | tf_op jit(solution)/shard_map/self/pallas_call | solution.py:397
  14.3 0.0 collective-permute-done.4.arrived
  14.3 0.1 own.1
  14.4 0.5 %collective-permute-start.9 = (bf16[16,16,256]{2,1,0:T(8,128)(2,1)S(1)}, bf16[16,16,256]{2,1,0:T(8,128)(2,1)S(1)}, u32[]{:S(2)}, u32[]{:S(2)}) collective-permute-start(bf16[16,16,256]{2,1,0:T(8,128)(2,1)S(1)} %get-tuple-element.31), channel_id=1, source_target_pairs={{0,8},{4,12},{8,0},{12,4},{1,9},{5,13},{9,1},{13,5},{2,10},{6,14},... | collective-permute-start | bytes 393224 | tf_op jit(solution)/shard_map/ppermute | solution.py:363
  14.8 2.2 %collective-permute-done.7.message = bf16[16,16,256]{2,1,0:T(8,128)(2,1)S(1)} collective-permute-done((bf16[16,16,256]{2,1,0:T(8,128)(2,1)S(1)}, bf16[16,16,256]{2,1,0:T(8,128)(2,1)S(1)}, u32[]{:S(2)}, u32[]{:S(2)}) %collective-permute-start.7) | collective-permute-done | bytes 131104 | tf_op jit(solution)/shard_map/ppermute | solution.py:363
  17.0 0.1 collective-permute-start.8
  17.1 0.5 %coeffs.1.others_0_.refs_0_ = bf16[2,16,256]{2,1,0:T(8,128)(2,1)S(1)} custom-call(bf16[16,16,256]{2,1,0:T(8,128)(2,1)S(1)} %settle.2.current.refs_0_, bf16[16,64,256]{2,1,0:T(8,128)(2,1)S(1)} %copy-done.2, bf16[16,64,64]{2,1,0:T(8,128)(2,1)S(1)} %copy-done.5), custom_call_target="tpu_custom_call" | custom-call | flops 500000000 | tf_op jit(solution)/shard_map/coeffs/pallas_call | solution.py:498
  17.6 2.3 %collective-permute-start.14 = (bf16[2,16,256]{2,1,0:T(8,128)(2,1)S(1)}, bf16[2,16,256]{2,1,0:T(8,128)(2,1)S(1)}, u32[]{:S(2)}, u32[]{:S(2)}) collective-permute-start(bf16[2,16,256]{2,1,0:T(8,128)(2,1)S(1)} %coeffs.1.others_0_.refs_0_), channel_id=1, source_target_pairs={{0,8},{4,12},{8,0},{12,4},{1,9},{5,13},{9,1},{13,5},{2,10},{6,14},... | collective-permute-start | bytes 49160 | tf_op jit(solution)/shard_map/ppermute | solution.py:363
  19.9 0.0 collective-permute-done.9.message
  19.9 0.0 collective-permute-done.8.others_1_.refs_1_
  20.0 0.3 collective-permute-start.10
  20.2 0.6 %self.3.refs_0_.refs_6_ = f32[16,16,256]{2,1,0:T(8,128)S(1)} custom-call(bf16[16,16,256]{2,1,0:T(8,128)(2,1)S(1)} %settle.2.current.refs_0_, bf16[16,256,256]{2,1,0:T(8,128)(2,1)S(1)} %copy-done.1), custom_call_target="tpu_custom_call" | custom-call | flops 2500000000 | tf_op jit(solution)/shard_map/self/pallas_call | solution.py:397
  20.9 0.5 %collective-permute-done.10.refs_3_ = bf16[16,16,256]{2,1,0:T(8,128)(2,1)S(1)} collective-permute-done((bf16[16,16,256]{2,1,0:T(8,128)(2,1)S(1)}, bf16[16,16,256]{2,1,0:T(8,128)(2,1)S(1)}, u32[]{:S(2)}, u32[]{:S(2)}) %collective-permute-start.10) | collective-permute-done | bytes 131104 | tf_op jit(solution)/shard_map/ppermute | solution.py:360
  21.4 0.6 %first_half.1 = (bf16[32,16,128]{2,1,0:T(8,128)(2,1)S(1)}, f32[32,16,128]{2,1,0:T(8,128)S(1)}, bf16[64,16,256]{2,1,0:T(8,128)(2,1)S(1)}) custom-call(s32[16,128]{1,0:T(8,128)S(4)} %get-tuple-element.21.table, bf16[48,256,256]{2,1,0:T(8,128)(2,1)S(1)} %turn.1.tiles, bf16[16,16,256]{2,1,0:T(8,128)(2,1)S(1)} %settle.2.current.refs_0_, ...), custom_call_target="tpu_custom_call" | custom-call | flops 500000000 | tf_op jit(solution)/shard_map/first_half/pallas_call | solution.py:428
  22.0 0.3 collective-permute-start.11
  22.3 0.6 %second_half.1 = (bf16[32,16,128]{2,1,0:T(8,128)(2,1)S(1)}, f32[32,16,128]{2,1,0:T(8,128)S(1)}) custom-call(s32[16,128]{1,0:T(8,128)S(4)} %get-tuple-element.21.table, bf16[48,256,256]{2,1,0:T(8,128)(2,1)S(1)} %turn.1.tiles, bf16[64,16,256]{2,1,0:T(8,128)(2,1)S(1)} %get-tuple-element.33.gathered), custom_call_target="tpu_custom_call" | custom-call | flops 500000000 | tf_op jit(solution)/shard_map/second_half/pallas_call | solution.py:436
  22.8 0.4 %collective-permute-start.12 = (bf16[32,16,128]{2,1,0:T(8,128)(2,1)S(1)}, bf16[32,16,128]{2,1,0:T(8,128)(2,1)S(1)}, u32[]{:S(2)}, u32[]{:S(2)}) collective-permute-start(bf16[32,16,128]{2,1,0:T(8,128)(2,1)S(1)} %get-tuple-element.36), channel_id=1, source_target_pairs={{0,4},{4,0},{8,12},{12,8},{1,5},{5,1},{9,13},{13,9},{2,6},{6,2},{1... | collective-permute-start | bytes 393224 | tf_op jit(solution)/shard_map/ppermute | solution.py:360
  23.2 0.0 collective-permute-done.14.refs_1_.refs_2_
  23.2 0.3 collective-permute-start.16
  23.5 1.7 %collective-permute-start.13 = (bf16[16,16,128]{2,1,0:T(8,128)(2,1)S(1)}, bf16[16,16,128]{2,1,0:T(8,128)(2,1)S(1)}, u32[]{:S(2)}, u32[]{:S(2)}) collective-permute-start(bf16[16,16,128]{2,1,0:T(8,128)(2,1)S(1)} %cross.2.refs_2_), channel_id=1, source_target_pairs={{0,8},{4,12},{8,0},{12,4},{1,9},{5,13},{9,1},{13,5},{2,10},{6,14},... | collective-permute-start | bytes 196616 | tf_op jit(solution)/shard_map/ppermute | solution.py:363
  25.2 0.0 collective-permute-done.12.arrived.refs_3_
  25.2 0.7 %collective-permute-start.15 = (bf16[16,16,128]{2,1,0:T(8,128)(2,1)S(1)}, bf16[16,16,128]{2,1,0:T(8,128)(2,1)S(1)}, u32[]{:S(2)}, u32[]{:S(2)}) collective-permute-start(bf16[16,16,128]{2,1,0:T(8,128)(2,1)S(1)} %cross.3), channel_id=1, source_target_pairs={{0,8},{4,12},{8,0},{12,4},{1,9},{5,13},{9,1},{13,5},{2,10},{6,14},... | collective-permute-start | bytes 196616 | tf_op jit(solution)/shard_map/ppermute | solution.py:363
  25.9 0.6 %far.3.refs_7_ = f32[16,16,256]{2,1,0:T(8,128)S(1)} custom-call(s32[16,128]{1,0:T(8,128)S(4)} %get-tuple-element.21.table, bf16[16,64,64]{2,1,0:T(8,128)(2,1)S(1)} %copy-done.6, bf16[16,64,256]{2,1,0:T(8,128)(2,1)S(1)} %copy-done.3, bf16[8,64,512]{2,1,0:T(8,128)(2,1)S(1)} %copy-done.4, bf16[2,16,256]{2,1,0:T(8,128)(2,1)S(1)} %coeffs.1.others_0_.refs_0_, ...), custom_call_target="tpu_custom_call" | custom-call | flops 500000000 | tf_op jit(solution)/shard_map/far/pallas_call | solution.py:445
  26.5 1.4 %collective-permute-done.13.refs_4_ = bf16[16,16,128]{2,1,0:T(8,128)(2,1)S(1)} collective-permute-done((bf16[16,16,128]{2,1,0:T(8,128)(2,1)S(1)}, bf16[16,16,128]{2,1,0:T(8,128)(2,1)S(1)}, u32[]{:S(2)}, u32[]{:S(2)}) %collective-permute-start.13) | collective-permute-done | bytes 65568 | tf_op jit(solution)/shard_map/ppermute | solution.py:363
  27.9 1.6 %collective-permute-done.15.refs_5_ = bf16[16,16,128]{2,1,0:T(8,128)(2,1)S(1)} collective-permute-done((bf16[16,16,128]{2,1,0:T(8,128)(2,1)S(1)}, bf16[16,16,128]{2,1,0:T(8,128)(2,1)S(1)}, u32[]{:S(2)}, u32[]{:S(2)}) %collective-permute-start.15) | collective-permute-done | bytes 65568 | tf_op jit(solution)/shard_map/ppermute | solution.py:363
  29.5 0.7 %last.1 = bf16[16,16,256]{2,1,0:T(8,128)(2,1)} custom-call(f32[32,16,128]{2,1,0:T(8,128)S(1)} %get-tuple-element.32.keep.refs_0_, f32[32,16,128]{2,1,0:T(8,128)S(1)} %get-tuple-element.34.keep.refs_1_, bf16[32,16,128]{2,1,0:T(8,128)(2,1)S(1)} %collective-permute-done.11.arrived.refs_2_, bf16[32,16,128]{2,1,0:T(8,128)(2,1)S(1)} %collective-permute-done.12.arrived.refs_3_, ...), custom_call_target="tpu_custom_call" | custom-call | flops 100000000 | tf_op jit(solution)/shard_map/last/pallas_call | solution.py:517
  (23 shorter events, 0.2 us)
Async XLA Ops:
  0.0 6.7 %collective-permute-start.1 = (bf16[16,16,256]{2,1,0:T(8,128)(2,1)}, bf16[16,16,256]{2,1,0:T(8,128)(2,1)S(1)}, u32[]{:S(2)}, u32[]{:S(2)}) collective-permute-start(bf16[16,16,256]{2,1,0:T(8,128)(2,1)} %vectors.1), channel_id=1, source_target_pairs={{0,8},{4,12},{8,0},{12,4},{1,9},{5,13},{9,1},{13,5},{2,10},{6,14},... | collective-permute-start | bytes 393224 | tf_op jit(solution)/shard_map/ppermute | solution.py:363
  3.0 3.8 %copy-start = (bf16[48,256,256]{2,1,0:T(8,128)(2,1)S(1)}, bf16[48,256,256]{2,1,0:T(8,128)(2,1)}, u32[]{:S(2)}) copy-start(bf16[48,256,256]{2,1,0:T(8,128)(2,1)} %tiles.1) | copy-start | bytes 18874372
  4.9 3.9 %collective-permute-start = (bf16[16,16,256]{2,1,0:T(8,128)(2,1)S(1)}, bf16[16,16,256]{2,1,0:T(8,128)(2,1)S(1)}, u32[]{:S(2)}, u32[]{:S(2)}) collective-permute-start(bf16[16,16,256]{2,1,0:T(8,128)(2,1)S(1)} %get-tuple-element.22.refs_0_.current), channel_id=1, source_target_pairs={{0,4},{4,0},{8,12},{12,8},{1,5},{5,1},{9,13},{13,9},{2,6},{6,2},{1... | collective-permute-start | bytes 393224 | tf_op jit(solution)/shard_map/ppermute | solution.py:360
  5.0 3.8 %collective-permute-start.3 = (bf16[2,16,256]{2,1,0:T(8,128)(2,1)S(1)}, bf16[2,16,256]{2,1,0:T(8,128)(2,1)S(1)}, u32[]{:S(2)}, u32[]{:S(2)}) collective-permute-start(bf16[2,16,256]{2,1,0:T(8,128)(2,1)S(1)} %get-tuple-element.23.refs_1_.refs_0_), channel_id=1, source_target_pairs={{0,8},{4,12},{8,0},{12,4},{1,9},{5,13},{9,1},{13,5},{2,10},{6,14},... | collective-permute-start | bytes 49160 | tf_op jit(solution)/shard_map/ppermute | solution.py:363
  6.7 2.1 %collective-permute-start.2 = (bf16[16,16,256]{2,1,0:T(8,128)(2,1)S(1)}, bf16[16,16,256]{2,1,0:T(8,128)(2,1)S(1)}, u32[]{:S(2)}, u32[]{:S(2)}) collective-permute-start(bf16[16,16,256]{2,1,0:T(8,128)(2,1)S(1)} %tie.1), channel_id=1, source_target_pairs={{0,4},{4,0},{8,12},{12,8},{1,5},{5,1},{9,13},{13,9},{2,6},{6,2},{1... | collective-permute-start | bytes 393224 | tf_op jit(solution)/shard_map/ppermute | solution.py:360
  8.5 4.6 %copy-start.3 = (bf16[16,64,256]{2,1,0:T(8,128)(2,1)S(1)}, bf16[16,64,256]{2,1,0:T(8,128)(2,1)}, u32[]{:S(2)}) copy-start(bf16[16,64,256]{2,1,0:T(8,128)(2,1)} %row_basis.3) | copy-start | bytes 1572868
  8.5 4.5 %copy-start.4 = (bf16[8,64,512]{2,1,0:T(8,128)(2,1)S(1)}, bf16[8,64,512]{2,1,0:T(8,128)(2,1)}, u32[]{:S(2)}) copy-start(bf16[8,64,512]{2,1,0:T(8,128)(2,1)} %coupling.3) | copy-start | bytes 1572868
  8.5 4.5 %copy-start.6 = (bf16[16,64,64]{2,1,0:T(8,128)(2,1)S(1)}, bf16[16,64,64]{2,1,0:T(8,128)(2,1)}, u32[]{:S(2)}) copy-start(bf16[16,64,64]{2,1,0:T(8,128)(2,1)} %row_transfer.3) | copy-start | bytes 393220
  8.5 5.1 %copy-start.1 = (bf16[16,256,256]{2,1,0:T(8,128)(2,1)S(1)}, bf16[16,256,256]{2,1,0:T(8,128)(2,1)}, u32[]{:S(2)}) copy-start(bf16[16,256,256]{2,1,0:T(8,128)(2,1)} %self_tiles.3) | copy-start | bytes 6291460
  8.8 8.3 %copy-start.2 = (bf16[16,64,256]{2,1,0:T(8,128)(2,1)S(1)}, bf16[16,64,256]{2,1,0:T(8,128)(2,1)}, u32[]{:S(2)}) copy-start(bf16[16,64,256]{2,1,0:T(8,128)(2,1)} %column_basis.3) | copy-start | bytes 1572868
  8.8 8.3 %copy-start.5 = (bf16[16,64,64]{2,1,0:T(8,128)(2,1)S(1)}, bf16[16,64,64]{2,1,0:T(8,128)(2,1)}, u32[]{:S(2)}) copy-start(bf16[16,64,64]{2,1,0:T(8,128)(2,1)} %column_transfer.3) | copy-start | bytes 393220
  9.9 1.4 %collective-permute-start.5 = (bf16[16,16,256]{2,1,0:T(8,128)(2,1)S(1)}, bf16[16,16,256]{2,1,0:T(8,128)(2,1)S(1)}, u32[]{:S(2)}, u32[]{:S(2)}) collective-permute-start(bf16[16,16,256]{2,1,0:T(8,128)(2,1)S(1)} %get-tuple-element.27), channel_id=1, source_target_pairs={{0,4},{4,0},{8,12},{12,8},{1,5},{5,1},{9,13},{13,9},{2,6},{6,2},{1... | collective-permute-start | bytes 393224 | tf_op jit(solution)/shard_map/ppermute | solution.py:360
  10.2 2.9 %collective-permute-start.6 = (bf16[4,16,256]{2,1,0:T(8,128)(2,1)S(1)}, bf16[4,16,256]{2,1,0:T(8,128)(2,1)S(1)}, u32[]{:S(2)}, u32[]{:S(2)}) collective-permute-start(bf16[4,16,256]{2,1,0:T(8,128)(2,1)S(1)} %pad_maximum_fusion), channel_id=1, source_target_pairs={{0,4},{4,0},{8,12},{12,8},{1,5},{5,1},{9,13},{13,9},{2,6},{6,2},{1... | collective-permute-start | bytes 98312 | tf_op jit(solution)/shard_map/ppermute | solution.py:360
  10.4 3.8 %collective-permute-start.4 = (bf16[16,16,256]{2,1,0:T(8,128)(2,1)S(1)}, bf16[16,16,256]{2,1,0:T(8,128)(2,1)S(1)}, u32[]{:S(2)}, u32[]{:S(2)}) collective-permute-start(bf16[16,16,256]{2,1,0:T(8,128)(2,1)S(1)} %get-tuple-element.25), channel_id=1, source_target_pairs={{0,4},{4,0},{8,12},{12,8},{1,5},{5,1},{9,13},{13,9},{2,6},{6,2},{1... | collective-permute-start | bytes 393224 | tf_op jit(solution)/shard_map/ppermute | solution.py:360
  11.3 5.7 %collective-permute-start.7 = (bf16[16,16,256]{2,1,0:T(8,128)(2,1)S(1)}, bf16[16,16,256]{2,1,0:T(8,128)(2,1)S(1)}, u32[]{:S(2)}, u32[]{:S(2)}) collective-permute-start(bf16[16,16,256]{2,1,0:T(8,128)(2,1)S(1)} %get-tuple-element.28.others_0_.sent_before), channel_id=1, source_target_pairs={{0,8},{4,12},{8,0},{12,4},{1,9},{5,13},{9,1},{13,5},{2,10},{6,14},... | collective-permute-start | bytes 393224 | tf_op jit(solution)/shard_map/ppermute | solution.py:363
  14.4 5.6 %collective-permute-start.9 = (bf16[16,16,256]{2,1,0:T(8,128)(2,1)S(1)}, bf16[16,16,256]{2,1,0:T(8,128)(2,1)S(1)}, u32[]{:S(2)}, u32[]{:S(2)}) collective-permute-start(bf16[16,16,256]{2,1,0:T(8,128)(2,1)S(1)} %get-tuple-element.31), channel_id=1, source_target_pairs={{0,8},{4,12},{8,0},{12,4},{1,9},{5,13},{9,1},{13,5},{2,10},{6,14},... | collective-permute-start | bytes 393224 | tf_op jit(solution)/shard_map/ppermute | solution.py:363
  17.0 2.9 %collective-permute-start.8 = (bf16[16,16,256]{2,1,0:T(8,128)(2,1)S(1)}, bf16[16,16,256]{2,1,0:T(8,128)(2,1)S(1)}, u32[]{:S(2)}, u32[]{:S(2)}) collective-permute-start(bf16[16,16,256]{2,1,0:T(8,128)(2,1)S(1)} %settle.2.current.refs_0_), channel_id=1, source_target_pairs={{0,4},{4,0},{8,12},{12,8},{1,5},{5,1},{9,13},{13,9},{2,6},{6,2},{1... | collective-permute-start | bytes 393224 | tf_op jit(solution)/shard_map/ppermute | solution.py:360
  17.6 5.6 %collective-permute-start.14 = (bf16[2,16,256]{2,1,0:T(8,128)(2,1)S(1)}, bf16[2,16,256]{2,1,0:T(8,128)(2,1)S(1)}, u32[]{:S(2)}, u32[]{:S(2)}) collective-permute-start(bf16[2,16,256]{2,1,0:T(8,128)(2,1)S(1)} %coeffs.1.others_0_.refs_0_), channel_id=1, source_target_pairs={{0,8},{4,12},{8,0},{12,4},{1,9},{5,13},{9,1},{13,5},{2,10},{6,14},... | collective-permute-start | bytes 49160 | tf_op jit(solution)/shard_map/ppermute | solution.py:363
  20.0 1.4 %collective-permute-start.10 = (bf16[16,16,256]{2,1,0:T(8,128)(2,1)S(1)}, bf16[16,16,256]{2,1,0:T(8,128)(2,1)S(1)}, u32[]{:S(2)}, u32[]{:S(2)}) collective-permute-start(bf16[16,16,256]{2,1,0:T(8,128)(2,1)S(1)} %settle.3.refs_2_), channel_id=1, source_target_pairs={{0,4},{4,0},{8,12},{12,8},{1,5},{5,1},{9,13},{13,9},{2,6},{6,2},{1... | collective-permute-start | bytes 393224 | tf_op jit(solution)/shard_map/ppermute | solution.py:360
  22.0 1.5 %collective-permute-start.11 = (bf16[32,16,128]{2,1,0:T(8,128)(2,1)S(1)}, bf16[32,16,128]{2,1,0:T(8,128)(2,1)S(1)}, u32[]{:S(2)}, u32[]{:S(2)}) collective-permute-start(bf16[32,16,128]{2,1,0:T(8,128)(2,1)S(1)} %get-tuple-element.35), channel_id=1, source_target_pairs={{0,4},{4,0},{8,12},{12,8},{1,5},{5,1},{9,13},{13,9},{2,6},{6,2},{1... | collective-permute-start | bytes 393224 | tf_op jit(solution)/shard_map/ppermute | solution.py:360
  22.8 2.3 %collective-permute-start.12 = (bf16[32,16,128]{2,1,0:T(8,128)(2,1)S(1)}, bf16[32,16,128]{2,1,0:T(8,128)(2,1)S(1)}, u32[]{:S(2)}, u32[]{:S(2)}) collective-permute-start(bf16[32,16,128]{2,1,0:T(8,128)(2,1)S(1)} %get-tuple-element.36), channel_id=1, source_target_pairs={{0,4},{4,0},{8,12},{12,8},{1,5},{5,1},{9,13},{13,9},{2,6},{6,2},{1... | collective-permute-start | bytes 393224 | tf_op jit(solution)/shard_map/ppermute | solution.py:360
  23.2 2.7 %collective-permute-start.16 = (bf16[4,16,256]{2,1,0:T(8,128)(2,1)S(1)}, bf16[4,16,256]{2,1,0:T(8,128)(2,1)S(1)}, u32[]{:S(2)}, u32[]{:S(2)}) collective-permute-start(bf16[4,16,256]{2,1,0:T(8,128)(2,1)S(1)} %pad_maximum_fusion.1), channel_id=1, source_target_pairs={{0,4},{4,0},{8,12},{12,8},{1,5},{5,1},{9,13},{13,9},{2,6},{6,2},{1... | collective-permute-start | bytes 98312 | tf_op jit(solution)/shard_map/ppermute | solution.py:360
  23.5 4.4 %collective-permute-start.13 = (bf16[16,16,128]{2,1,0:T(8,128)(2,1)S(1)}, bf16[16,16,128]{2,1,0:T(8,128)(2,1)S(1)}, u32[]{:S(2)}, u32[]{:S(2)}) collective-permute-start(bf16[16,16,128]{2,1,0:T(8,128)(2,1)S(1)} %cross.2.refs_2_), channel_id=1, source_target_pairs={{0,8},{4,12},{8,0},{12,4},{1,9},{5,13},{9,1},{13,5},{2,10},{6,14},... | collective-permute-start | bytes 196616 | tf_op jit(solution)/shard_map/ppermute | solution.py:363
  25.2 4.3 %collective-permute-start.15 = (bf16[16,16,128]{2,1,0:T(8,128)(2,1)S(1)}, bf16[16,16,128]{2,1,0:T(8,128)(2,1)S(1)}, u32[]{:S(2)}, u32[]{:S(2)}) collective-permute-start(bf16[16,16,128]{2,1,0:T(8,128)(2,1)S(1)} %cross.3), channel_id=1, source_target_pairs={{0,8},{4,12},{8,0},{12,4},{1,9},{5,13},{9,1},{13,5},{2,10},{6,14},... | collective-permute-start | bytes 196616 | tf_op jit(solution)/shard_map/ppermute | solution.py:363

commit v5 on v3

--- a/solution.py
+++ b/solution.py
@@ -74,7 +74,7 @@
     return slot
 
 
-def place_table(columns, clusters, source, target, local, far, values):
+def place_table(columns, clusters, source, target, local, far, values, places):
     me = lax.axis_index("loop")
     my_column = me // 2
 
@@ -99,6 +99,12 @@
     shift = around(my_column - (home >> 1))
     place = (2 * shift + other_core(home)) * parents + cluster - home * parents
     values[FAR_ROW : FAR_ROW + parents, :far_count] = place
+    home = source[...]
+    shift = around(my_column - (home >> 1))
+    places[0:1, :blocks] = (2 * shift + (home & 1)) * clusters + local[0:1]
+    home = target[...]
+    shift = around((home >> 1) - my_column)
+    places[1:2, :blocks] = (2 * shift + (home & 1)) * clusters + local[1:2]
 
 
 def first_kernel(
@@ -112,6 +118,7 @@
     column_transfer,
     packed,
     current,
+    places,
     table,
     basis_held,
     transfer_held,
@@ -134,7 +141,7 @@
     )
     for copy in copies[:4]:
         copy.wait()
-    place_table(columns, vectors.shape[0], source, target, local, far, values)
+    place_table(columns, vectors.shape[0], source, target, local, far, values, places)
     placed = pltpu.make_async_copy(values, table, sems.at[7])
     placed.start()
     for copy in copies[4:]:
@@ -159,28 +166,101 @@
         self_part[c] = dot(current[c], self_tiles[c], ROWS_BY_ROWS)
 
 
-def turn_kernel(tiles, turned):
+def turn_kernel(tiles, mine, theirs):
+    lanes = mine.shape[2]
+    core = lax.axis_index("loop") % 2
+    start = pl.multiple_of(core * lanes, lanes)
+    other = pl.multiple_of((1 - core) * lanes, lanes)
     for b in range(tiles.shape[0]):
-        turned[b] = tiles[b].T
-
-
-def near_kernel(panel_count, table, tiles, *refs):
+        mine[b] = tiles[b, pl.ds(start, lanes), :].T
+        theirs[b] = tiles[b, pl.ds(other, lanes), :].T
+
+
+def near_kernel(panel_count, packed_count, table, mine, theirs, *refs):
     panels, refs = refs[:panel_count], refs[panel_count:]
+    packed = refs[:packed_count]
     send, send_own, keep, keep_own, gathered, products, sums = refs[-7:]
     each = gathered.shape[0] // panel_count
     for k, panel in enumerate(panels):
         gathered[k * each : (k + 1) * each] = panel[:each]
     sums[...] = jnp.zeros_like(sums)
-    blocks = tiles.shape[0]
+    blocks = mine.shape[0]
     for b in range(blocks):
-        products[b] = dot(gathered[table[0, b]], tiles[b], ROWS_BY_COLUMNS)
+        tile = jnp.concatenate([mine[b], theirs[b]], axis=-1)
+        products[b] = dot(gathered[table[0, b]], tile, ROWS_BY_COLUMNS)
     for b in range(blocks):
         sums[table[1, b]] += products[b]
     own, half = keep_own.shape[0], sums.shape[0] // 2
-    send_own[...] = sums[:own].astype(BF16)
-    send[...] = sums[own:half].astype(BF16)
-    keep_own[...] = sums[half : half + own]
-    keep[...] = sums[half + own :]
+    core = lax.axis_index("loop") % 2
+
+    def in_order(x):
+        lanes = x.shape[-1] // 2
+        here, beside = x[..., :lanes], x[..., lanes:]
+        return jnp.concatenate(
+            [jnp.where(core == 0, here, beside), jnp.where(core == 0, beside, here)], axis=-1
+        )
+
+    send_own[:own] = in_order(sums[:own]).astype(BF16)
+    for k, coeffs in enumerate(packed):
+        rows = coeffs.shape[0]
+        send_own[own + k * rows : own + (k + 1) * rows] = coeffs[...]
+    send[...] = in_order(sums[own:half]).astype(BF16)
+    keep_own[...] = in_order(sums[half : half + own])
+    keep[...] = in_order(sums[half + own :])
+
+
+def first_self_kernel(
+    current, self_tiles, places, places_beside, sent_before, self_part, table, sems
+):
+    copies = load_all(
+        sems,
+        (places, table.at[pl.ds(0, FAR_ROW)]),
+        (places_beside, table.at[pl.ds(FAR_ROW, FAR_ROW)]),
+    )
+    self_kernel(current, self_tiles, self_part)
+    for copy in copies:
+        copy.wait()
+
+
+def half_kernel(
+    table,
+    mine,
+    beside,
+    current,
+    current_beside,
+    column,
+    column_beside,
+    across,
+    diagonal,
+    send,
+    keep,
+    gathered,
+    products,
+    sums,
+):
+    clusters = current.shape[0]
+    core = lax.axis_index("loop") % 2
+
+    def at(slot):
+        return pl.ds(slot * clusters, clusters)
+
+    gathered[at(core)] = current[...]
+    gathered[at(1 - core)] = current_beside[...]
+    gathered[at(2 + core)] = column[...]
+    gathered[at(3 - core)] = column_beside[...]
+    sums[...] = jnp.zeros_like(sums)
+    blocks = mine.shape[0]
+    for k, tiles in enumerate((mine, beside)):
+        for b in range(blocks):
+            source = table[k * FAR_ROW, b]
+            products[k * blocks + b] = dot(gathered[source], tiles[b], ROWS_BY_COLUMNS)
+    for k in range(2):
+        for b in range(blocks):
+            sums[table[k * FAR_ROW + 1, b]] += products[k * blocks + b]
+    across[...] = sums[at(2 + core)].astype(BF16)
+    diagonal[...] = sums[at(3 - core)].astype(BF16)
+    send[...] = sums[at(1 - core)].astype(BF16)
+    keep[...] = sums[at(core)]
 
 
 def far_products(table, row_transfer, row_basis, coupling, gathered, store):
@@ -211,11 +291,11 @@
         store(2 * p, both.reshape(2, vectors, leaf_size))
 
 
-def far_kernel(message_count, rows, table, row_transfer, row_basis, coupling, *refs):
-    messages, (far_part, gathered) = refs[:message_count], refs[-2:]
+def far_kernel(starts, rows, table, row_transfer, row_basis, coupling, *refs):
+    messages, (far_part, gathered) = refs[: len(starts)], refs[-2:]
     slot = 0
-    for message in messages:
-        slot = unpack(message, message.shape[0] - rows, rows, row_basis.shape[1], gathered, slot)
+    for message, start in zip(messages, starts):
+        slot = unpack(message, start, rows, row_basis.shape[1], gathered, slot)
 
     def store(c, both):
         far_part[c : c + 2] = both
@@ -230,7 +310,8 @@
 
 
 def own_kernel(keep, arrived, self_part, far_part, sent_before, message, sums):
-    own = keep[...] + arrived[...].astype(F32) + self_part[...] + far_part[...]
+    near = keep[...] + arrived[: keep.shape[0]].astype(F32)
+    own = near + self_part[...] + far_part[...]
     sums[...] = own
     message[...] = own.astype(BF16)
 
@@ -240,12 +321,13 @@
     current[...] = (sums[...] + message[...].astype(F32)).astype(BF16)
 
 
-def cross_kernel(keep, arrived, self_part, column_coeffs, message):
-    message[...] = (keep[...] + arrived[...].astype(F32)).astype(BF16)
-
-
-def last_kernel(self_part, far_part, keep, arrived, message, product):
-    near = keep[...] + arrived[...].astype(F32) + message[...].astype(F32)
+def last_kernel(self_part, far_part, keep, crossed, arrived, diagonal, product):
+    core = lax.axis_index("loop") % 2
+    here = keep[...] + crossed[...].astype(F32)
+    beside = arrived[...].astype(F32) + diagonal[...].astype(F32)
+    near = jnp.concatenate(
+        [jnp.where(core == 0, here, beside), jnp.where(core == 0, beside, here)], axis=-1
+    )
     product[...] = (self_part[...] + far_part[...] + near).astype(BF16)
 
 
@@ -286,7 +368,7 @@
     )
 
 
-def tie(x, *others):
+def tie(x, *others, us=0.0):
     return pl.pallas_call(
         tie_kernel,
         name="tie",
@@ -295,6 +377,9 @@
         out_specs=VMEM_SPEC,
         input_output_aliases={0: 0},
         compiler_params=pltpu.CompilerParams(vmem_limit_bytes=VMEM_LIMIT),
+        cost_estimate=pl.CostEstimate(
+            flops=int(us * 1.0e9), bytes_accessed=0, transcendentals=0
+        ),
     )(*in_vmem(x), *others)
 
 
@@ -329,8 +414,8 @@
     def across(x):
         return [to_column(x, shift) for shift in range(1, columns)]
 
-    def panels(number, dtype):
-        return jax.ShapeDtypeStruct((number, vector_count, leaf_size), dtype)
+    def panels(number, dtype, width=leaf_size):
+        return jax.ShapeDtypeStruct((number, vector_count, width), dtype)
 
     def scratch(number, dtype, width=leaf_size):
         return pltpu.VMEM((number, vector_count, width), dtype)
@@ -344,17 +429,17 @@
         (
             panels(rows, BF16),
             pltpu.VMEM(vectors.shape, BF16),
+            pltpu.VMEM((FAR_ROW, 128), jnp.int32),
             pltpu.SMEM(table_shape, jnp.int32),
         ),
         [HBM_SPEC] * 7,
         [pltpu.VMEM(x.shape, x.dtype) for x in (column_basis, column_transfer, *raw)]
         + [pltpu.VMEM(table_shape, jnp.int32), pltpu.SemaphoreType.DMA((8,))],
-        out_specs=(VMEM_SPEC, VMEM_SPEC, SMEM_SPEC),
+        out_specs=(VMEM_SPEC, VMEM_SPEC, VMEM_SPEC, SMEM_SPEC),
         us=10.0,
     )
-    turn_call = call(
-        turn_kernel, "turn", pltpu.VMEM(near_tiles.shape, BF16), [VMEM_SPEC], us=2.5
-    )
+    half_tiles = pltpu.VMEM((blocks, leaf_size, leaf_size // 2), BF16)
+    turn_call = call(turn_kernel, "turn", (half_tiles, half_tiles), [VMEM_SPEC], us=2.5)
     coeffs_call = call(coeffs_kernel, "coeffs", panels(rows, BF16), [VMEM_SPEC] * 3, us=0.5)
     def self_call(current, *others, us=0.6):
         specs = [VMEM_SPEC] * 2 + [ANY_SPEC] * len(others)
@@ -362,30 +447,55 @@
             *in_vmem(current, self_tiles), *others
         )
 
-    def near_call(table, turned, given, *others):
+    def near_call(table, given, packed=()):
         return call(
-            functools.partial(near_kernel, len(given)),
+            functools.partial(near_kernel, len(given), len(packed)),
             "near",
             (
                 panels((columns - 1) * clusters, BF16),
-                panels(clusters, BF16),
+                panels(clusters + len(packed) * rows, BF16),
                 panels((columns - 1) * clusters, F32),
                 panels(clusters, F32),
             ),
-            [SMEM_SPEC] + [VMEM_SPEC] * (1 + len(given)) + [ANY_SPEC] * len(others),
+            [SMEM_SPEC] + [VMEM_SPEC] * (2 + len(given) + len(packed)),
             [
                 scratch(count * clusters, BF16),
                 scratch(blocks, F32),
                 scratch(count * clusters, F32),
             ],
             us=1.0,
-        )(in_smem(table), *in_vmem(turned, *given), *others)
+        )(in_smem(table), *in_vmem(mine, theirs, *given, *packed))
+
+    half_size = leaf_size // 2
+    first_self_call = call(
+        first_self_kernel,
+        "first_self",
+        (panels(clusters, F32), pltpu.SMEM((2 * FAR_ROW, 128), jnp.int32)),
+        [VMEM_SPEC] * 4 + [ANY_SPEC],
+        [pltpu.SemaphoreType.DMA((2,))],
+        out_specs=(VMEM_SPEC, SMEM_SPEC),
+        us=0.6,
+    )
+    half_call = call(
+        half_kernel,
+        "half",
+        (*(panels(clusters, BF16, half_size),) * 3, panels(clusters, F32, half_size)),
+        [SMEM_SPEC] + [VMEM_SPEC] * 6,
+        [
+            scratch(count * clusters, BF16),
+            scratch(2 * blocks, F32, half_size),
+            scratch(count * clusters, F32, half_size),
+        ],
+        us=1.0,
+    )
 
     gathered_coeffs = scratch(count * parents, BF16, 2 * rank)
 
-    def far_call(table, messages):
+    def far_call(table, messages, starts=None):
+        if starts is None:
+            starts = [x.shape[0] - rows for x in messages]
         return call(
-            functools.partial(far_kernel, len(messages), rows),
+            functools.partial(far_kernel, tuple(starts), rows),
             "far",
             panels(clusters, F32),
             [SMEM_SPEC] + [VMEM_SPEC] * (3 + len(messages)),
@@ -399,10 +509,6 @@
             gathered += [x, to_sibling(tie(x, *others) if others else x)]
         return gathered
 
-    def both_to_sibling(send, send_own):
-        arrived = to_sibling(jnp.concatenate([send, send_own]))
-        return arrived[: send.shape[0]], arrived[send.shape[0] :]
-
     def all_coeffs(packed, crossed):
         beside = to_sibling(jnp.concatenate([packed, *crossed]))
         pieces = []
@@ -411,24 +517,30 @@
         return pieces
 
     crossed = across(vectors)
-    beside = to_sibling(vectors)
-    packed, current, table = first_call(*in_hbm(*raw, vectors, column_basis, column_transfer))
-    given = [current, beside]
+    packed, current, places, table = first_call(*in_hbm(*raw, vectors, column_basis, column_transfer))
+    places_beside = to_sibling(places)
+    given = [current, to_sibling(current)]
     for x in crossed:
-        given += [x, to_sibling(tie(x, packed))]
+        given += [x, to_sibling(tie(x, packed, places_beside))]
     crossed = across(packed)
-    turned = turn_call(*in_vmem(near_tiles))
-    send, send_own, keep, keep_own = near_call(table, turned, given, *crossed)
+    mine, theirs = turn_call(*in_vmem(near_tiles))
+    send, send_own, keep, keep_own = near_call(table, given, [packed, *crossed])
     arrived, arrived_own = to_sibling(send), to_sibling(send_own)
-    pieces = all_coeffs(packed, crossed)
+    pieces, starts = [], []
+    for k, piece in enumerate([packed, *crossed]):
+        pieces += [piece, arrived_own]
+        starts += [0, clusters + k * rows]
 
     if columns == 2 and ITERS == 2:
         both_out = (panels(clusters, BF16), panels(clusters, F32))
         other, other_sums = call(other_kernel, "other", both_out, [VMEM_SPEC] * 2, us=0.1)(
             *in_vmem(keep, arrived)
         )
-        self_part = self_call(current, other)
-        far_part = far_call(table, pieces)
+        far_part = far_call(table, pieces, starts)
+        self_part, both_places = first_self_call(
+            *in_vmem(current, self_tiles, places, places_beside), other
+        )
+        theirs = to_sibling(tie(theirs, other,arrived_own, places_beside))
         own, own_sums = call(
             own_kernel, "own", both_out, [VMEM_SPEC] * 4 + [ANY_SPEC], us=0.1
         )(*in_vmem(keep_own, arrived_own, self_part, far_part), other)
@@ -445,27 +557,22 @@
         packed = coeffs_call(*in_vmem(current, column_basis, column_transfer))
         packed_column = to_column(packed, 1)
         column = settled(other_sums, own, packed, beside)
-        given = [current, beside, column, to_sibling(column)]
-        send, send_own, keep, keep_own = near_call(table, turned, given, packed)
-        arrived, arrived_own = both_to_sibling(send, send_own)
-        self_part = self_call(current, us=2.5)
-        crossing = call(
-            cross_kernel,
-            "cross",
-            panels(clusters, BF16),
-            [VMEM_SPEC] * 2 + [ANY_SPEC] * 2,
-            us=0.1,
-        )(*in_vmem(keep, arrived), self_part, packed_column)
+        crossing, diagonal, send, keep = half_call(
+            in_smem(both_places), *in_vmem(mine, theirs, current, beside, column, to_sibling(column))
+        )
+        crossed, arrived = to_column(crossing, 1), to_sibling(send)
+        diagonal = lax.ppermute(diagonal, "loop", [(i, i ^ 3) for i in range(count)])
+        self_part = self_call(current, us=0.6)
         far_part = far_call(table, all_coeffs(packed, [packed_column]))
-        return call(last_kernel, "last", panels(clusters, BF16), [VMEM_SPEC] * 5, us=0.1)(
-            *in_vmem(self_part, far_part, keep_own, arrived_own, to_column(crossing, 1))
+        return call(last_kernel, "last", panels(clusters, BF16), [VMEM_SPEC] * 6, us=0.1)(
+            *in_vmem(self_part, far_part, keep, crossed, arrived, diagonal)
         )
 
     self_part = self_call(current)
-    far_part = far_call(table, pieces)
+    far_part = far_call(table, pieces, starts)
 
     def finished():
-        near = keep_own + arrived_own.astype(F32)
+        near = keep_own + arrived_own[:clusters].astype(F32)
         for s in range(1, columns):
             part = slice((s - 1) * clusters, s * clusters)
             partial = (keep[part] + arrived[part].astype(F32)).astype(BF16)
@@ -477,7 +584,7 @@
             message_kernel, "message", panels(clusters + rows, BF16), [VMEM_SPEC] * 3, us=0.5
         )(*in_vmem(finished(), column_basis, column_transfer))
         messages = gather(message)
-        send, send_own, keep, keep_own = near_call(table, turned, messages)
+        send, send_own, keep, keep_own = near_call(table, messages)
         arrived, arrived_own = to_sibling(send), to_sibling(send_own)
         self_part = self_call(message)
         far_part = far_call(table, messages)

time: 31 us -> 29.9 us (0.965)
  waiting for transfers between devices: 11.1 us -> 8.35 us
  starting transfers between devices: 9.91 us -> 11.6 us
    ppermute x6, waiting for transfers between devices: 10.3 us -> 5.8 us  [to_column(): lax.ppermute(x, 'loop', [(i, (i + 2 * shift) % count) for i in range(coun...]
    ppermute x0 -> x1, waiting for transfers between devices: none -> 1.45 us  [on_device(): lax.ppermute(diagonal, 'loop', [(i, i ^ 3) for i in range(count)])]
    ppermute x6, starting transfers between devices: 8.28 us -> 9.66 us  [to_column(): lax.ppermute(x, 'loop', [(i, (i + 2 * shift) % count) for i in range(coun...]
    pallas_call x7, Pallas kernels: 5.59 us -> 6.29 us  [the longest x1 1.68 us: on_device(): mine, theirs = turn_call(*in_vmem(near_tiles))]
    pallas_call x2 -> x1, Pallas kernels: 1.29 us -> 0.64 us  [self_call(): call(self_kernel, 'self', panels(clusters, F32), specs, us=us)]
    ppermute x9 -> x10, waiting for transfers between devices: 0.83 us -> 1.1 us  [to_sibling(): return lax.ppermute(x, 'loop', sibling)]
    ppermute x9 -> x10, starting transfers between devices: 1.64 us -> 1.83 us  [to_sibling(): return lax.ppermute(x, 'loop', sibling)]
  transfers between devices with their start and end apart: 15 -> 17, of which waited for: 8 -> 8; matrix products, arithmetic and copies ran while one was open for 0% -> 0% of each run, Pallas kernels for 25% -> 26%
where the time goes in v5:
time: 29.9 us; the launch traced here: 29.8 us
  starting transfers between devices  11.6 us (39%)
  Pallas kernels  9.51 us (32%)
  waiting for transfers between devices  8.35 us (28%)
    ppermute x6, starting transfers between devices, to_column(): lax.ppermute(x, 'loop', [(i, (i + 2 * shift) % count) for i in range(coun...  9.66 us
    ppermute x6, waiting for transfers between devices, to_column(): lax.ppermute(x, 'loop', [(i, (i + 2 * shift) % count) for i in range(coun...  5.8 us
    pallas_call x1, Pallas kernels, on_device(): first_call(*in_hbm(*raw, vectors, column_basis, column_transfer))  1.93 us
    ppermute x10, starting transfers between devices, to_sibling(): return lax.ppermute(x, 'loop', sibling)  1.83 us
    pallas_call x1, Pallas kernels, on_device(): mine, theirs = turn_call(*in_vmem(near_tiles))  1.68 us
    ppermute x1, waiting for transfers between devices, on_device(): lax.ppermute(diagonal, 'loop', [(i, i ^ 3) for i in range(count)])  1.45 us
    pallas_call x2, Pallas kernels, far_call(): call(functools.partial(far_kernel, tuple(starts), rows), 'far', panels(cl...  1.14 us
    ppermute x10, waiting for transfers between devices, to_sibling(): return lax.ppermute(x, 'loop', sibling)  1.1 us
  transfers between devices with their start and end apart: 17, of which 8 were waited for; matrix products, arithmetic and copies ran while one was open for 0% of the time, Pallas kernels for 26%

profile of v5, /device:TPU:0, one launch (start us, length us, event | category | flops | bytes accessed | tf_op | source)
XLA Modules:
  0.0 29.8 jit_solution(5320782145761496689)
XLA Ops:
  0.0 3.0 %collective-permute-start.1 = (bf16[16,16,256]{2,1,0:T(8,128)(2,1)}, bf16[16,16,256]{2,1,0:T(8,128)(2,1)S(1)}, u32[]{:S(2)}, u32[]{:S(2)}) collective-permute-start(bf16[16,16,256]{2,1,0:T(8,128)(2,1)} %vectors.1), channel_id=1, source_target_pairs={{0,8},{4,12},{8,0},{12,4},{1,9},{5,13},{9,1},{13,5},{2,10},{6,14},... | collective-permute-start | bytes 393224 | tf_op jit(solution)/shard_map/ppermute | solution.py:412
  3.0 1.9 %first.1 = (bf16[2,16,256]{2,1,0:T(8,128)(2,1)S(1)}, bf16[16,16,256]{2,1,0:T(8,128)(2,1)S(1)}, s32[8,128]{1,0:T(8,128)S(1)}, s32[16,128]{1,0:T(8,128)S(4)}) custom-call(s32[1,48]{1,0:T(1,128)} %bitcast.4, s32[1,48]{1,0:T(1,128)} %bitcast.5, s32[2,48]{1,0:T(2,128)} %bitcast.3, s32[8,8]{1,0:T(8,128)} %far_source.1, bf16[16,16,256]{2,1,0:T(8,128)(2,1)} %vectors.1, ...), custom_call_target="tpu_custom_call" | custom-call | flops 10000000000 | tf_op jit(solution)/shard_map/first/pallas_call | solution.py:520
  4.9 0.1 collective-permute-start.2
  5.0 0.1 collective-permute-start.4
  5.1 0.4 %collective-permute-start = (bf16[16,16,256]{2,1,0:T(8,128)(2,1)S(1)}, bf16[16,16,256]{2,1,0:T(8,128)(2,1)S(1)}, u32[]{:S(2)}, u32[]{:S(2)}) collective-permute-start(bf16[16,16,256]{2,1,0:T(8,128)(2,1)S(1)} %get-tuple-element.28.refs_0_.current), channel_id=1, source_target_pairs={{0,4},{4,0},{8,12},{12,8},{1,5},{5,1},{9,13},{13,9},{2,6},{6,2},{1... | collective-permute-start | bytes 393224 | tf_op jit(solution)/shard_map/ppermute | solution.py:409
  5.5 1.2 %collective-permute-done.1.refs_2_ = bf16[16,16,256]{2,1,0:T(8,128)(2,1)S(1)} collective-permute-done((bf16[16,16,256]{2,1,0:T(8,128)(2,1)}, bf16[16,16,256]{2,1,0:T(8,128)(2,1)S(1)}, u32[]{:S(2)}, u32[]{:S(2)}) %collective-permute-start.1) | collective-permute-done | bytes 131104 | tf_op jit(solution)/shard_map/ppermute | solution.py:412
  6.7 0.0 collective-permute-done.2.refs_2_.places_beside.refs_3_
  6.7 0.1 collective-permute-start.3
  6.8 1.7 %turn.1 = (bf16[48,256,128]{2,1,0:T(8,128)(2,1)S(1)}, bf16[48,256,128]{2,1,0:T(8,128)(2,1)S(1)}) custom-call(bf16[48,256,256]{2,1,0:T(8,128)(2,1)S(1)} %copy-done.4), custom_call_target="tpu_custom_call" | custom-call | flops 2500000000 | tf_op jit(solution)/shard_map/turn/pallas_call | solution.py:526
  8.5 0.3 %collective-permute-done.4.refs_5_.refs_2_ = bf16[2,16,256]{2,1,0:T(8,128)(2,1)S(1)} collective-permute-done((bf16[2,16,256]{2,1,0:T(8,128)(2,1)S(1)}, bf16[2,16,256]{2,1,0:T(8,128)(2,1)S(1)}, u32[]{:S(2)}, u32[]{:S(2)}) %collective-permute-start.4) | collective-permute-done | bytes 16416 | tf_op jit(solution)/shard_map/ppermute | solution.py:412
  8.8 0.0 collective-permute-done.refs_1_
  8.8 0.0 collective-permute-done.3.refs_3_
  8.8 1.0 %near.1 = (bf16[16,16,256]{2,1,0:T(8,128)(2,1)S(1)}, bf16[20,16,256]{2,1,0:T(8,128)(2,1)S(1)}, f32[16,16,256]{2,1,0:T(8,128)S(1)}, f32[16,16,256]{2,1,0:T(8,128)S(1)}) custom-call(s32[16,128]{1,0:T(8,128)S(4)} %get-tuple-element.25.table, bf16[48,256,128]{2,1,0:T(8,128)(2,1)S(1)} %get-tuple-element.26.mine, ...), custom_call_target="tpu_custom_call" | custom-call | flops 1000000000 | tf_op jit(solution)/shard_map/near/pallas_call | solution.py:451
  9.8 0.3 collective-permute-start.5
  10.1 0.3 %collective-permute-start.6 = (bf16[16,16,256]{2,1,0:T(8,128)(2,1)S(1)}, bf16[16,16,256]{2,1,0:T(8,128)(2,1)S(1)}, u32[]{:S(2)}, u32[]{:S(2)}) collective-permute-start(bf16[16,16,256]{2,1,0:T(8,128)(2,1)S(1)} %get-tuple-element.34), channel_id=1, source_target_pairs={{0,4},{4,0},{8,12},{12,8},{1,5},{5,1},{9,13},{13,9},{2,6},{6,2},{1... | collective-permute-start | bytes 393224 | tf_op jit(solution)/shard_map/ppermute | solution.py:409
  10.4 1.1 %collective-permute-done.6.arrived = bf16[16,16,256]{2,1,0:T(8,128)(2,1)S(1)} collective-permute-done((bf16[16,16,256]{2,1,0:T(8,128)(2,1)S(1)}, bf16[16,16,256]{2,1,0:T(8,128)(2,1)S(1)}, u32[]{:S(2)}, u32[]{:S(2)}) %collective-permute-start.6) | collective-permute-done | bytes 131104 | tf_op jit(solution)/shard_map/ppermute | solution.py:409
  11.5 0.0 copy-start
  11.5 0.0 copy-start.1
  11.6 0.0 copy-start.2
  11.6 0.0 copy-start.3
  11.6 0.0 copy-start.5
  11.6 0.0 copy-start.6
  11.6 0.3 %collective-permute-start.10 = (bf16[48,256,128]{2,1,0:T(8,128)(2,1)S(1)}, bf16[48,256,128]{2,1,0:T(8,128)(2,1)S(1)}, u32[]{:S(2)}, u32[]{:S(2)}) collective-permute-start(bf16[48,256,128]{2,1,0:T(8,128)(2,1)S(1)} %tie.3), channel_id=1, source_target_pairs={{0,4},{4,0},{8,12},{12,8},{1,5},{5,1},{9,13},{13,9},{2,6},{6,2},{1... | collective-permute-start | bytes 9437192 | tf_op jit(solution)/shard_map/ppermute | solution.py:409
  12.0 1.7 %collective-permute-start.7 = (bf16[16,16,256]{2,1,0:T(8,128)(2,1)S(1)}, bf16[16,16,256]{2,1,0:T(8,128)(2,1)S(1)}, u32[]{:S(2)}, u32[]{:S(2)}) collective-permute-start(bf16[16,16,256]{2,1,0:T(8,128)(2,1)S(1)} %get-tuple-element.35.sent_before.refs_1_), channel_id=1, source_target_pairs={{0,8},{4,12},{8,0},{12,4},{1,9},{5,13},{9,1},{13,5},{2,10},{6,14},... | collective-permute-start | bytes 393224 | tf_op jit(solution)/shard_map/ppermute | solution.py:412
  13.6 0.7 %first_self.1 = (f32[16,16,256]{2,1,0:T(8,128)S(1)}, s32[16,128]{1,0:T(8,128)S(4)}) custom-call(bf16[16,16,256]{2,1,0:T(8,128)(2,1)S(1)} %get-tuple-element.28.refs_0_.current, bf16[16,256,256]{2,1,0:T(8,128)(2,1)S(1)} %copy-done, s32[8,128]{1,0:T(8,128)S(1)} %get-tuple-element.30.places, s32[8,128]{1,0:T(8,128)S(1)} %collective-permute-done.2.refs_2_.places_beside.refs_3_, ...), custom_call_target="tpu_custom_call" | custom-call | flops 600000000 | tf_op jit(solution)/shard_map/first_self/pallas_call | solution.py:540
  14.4 0.6 %far.2.far_part = f32[16,16,256]{2,1,0:T(8,128)S(1)} custom-call(s32[16,128]{1,0:T(8,128)S(4)} %get-tuple-element.25.table, bf16[16,64,64]{2,1,0:T(8,128)(2,1)S(1)} %copy-done.3, bf16[16,64,256]{2,1,0:T(8,128)(2,1)S(1)} %copy-done.1, bf16[8,64,512]{2,1,0:T(8,128)(2,1)S(1)} %copy-done.2, bf16[2,16,256]{2,1,0:T(8,128)(2,1)S(1)} %get-tuple-element.29.refs_1_.refs_4_.refs_0_, ...), custom_call_target="tpu_custom_call" | custom-call | flops 500000000 | tf_op jit(solution)/shard_map/far/pallas_call | solution.py:497
  14.9 0.1 own.1
  15.0 1.3 %collective-permute-start.12 = (bf16[16,16,256]{2,1,0:T(8,128)(2,1)S(1)}, bf16[16,16,256]{2,1,0:T(8,128)(2,1)S(1)}, u32[]{:S(2)}, u32[]{:S(2)}) collective-permute-start(bf16[16,16,256]{2,1,0:T(8,128)(2,1)S(1)} %get-tuple-element.40), channel_id=1, source_target_pairs={{0,8},{4,12},{8,0},{12,4},{1,9},{5,13},{9,1},{13,5},{2,10},{6,14},... | collective-permute-start | bytes 393224 | tf_op jit(solution)/shard_map/ppermute | solution.py:412
  16.3 1.3 %collective-permute-done.7.message = bf16[16,16,256]{2,1,0:T(8,128)(2,1)S(1)} collective-permute-done((bf16[16,16,256]{2,1,0:T(8,128)(2,1)S(1)}, bf16[16,16,256]{2,1,0:T(8,128)(2,1)S(1)}, u32[]{:S(2)}, u32[]{:S(2)}) %collective-permute-start.7) | collective-permute-done | bytes 131104 | tf_op jit(solution)/shard_map/ppermute | solution.py:412
  17.6 0.1 collective-permute-start.11
  17.7 0.5 %coeffs.1.refs_0_.others_0_ = bf16[2,16,256]{2,1,0:T(8,128)(2,1)S(1)} custom-call(bf16[16,16,256]{2,1,0:T(8,128)(2,1)S(1)} %settle.2.current, bf16[16,64,256]{2,1,0:T(8,128)(2,1)S(1)} %copy-done.5, bf16[16,64,64]{2,1,0:T(8,128)(2,1)S(1)} %copy-done.6), custom_call_target="tpu_custom_call" | custom-call | flops 500000000 | tf_op jit(solution)/shard_map/coeffs/pallas_call | solution.py:557
  18.2 1.8 %collective-permute-start.8 = (bf16[2,16,256]{2,1,0:T(8,128)(2,1)S(1)}, bf16[2,16,256]{2,1,0:T(8,128)(2,1)S(1)}, u32[]{:S(2)}, u32[]{:S(2)}) collective-permute-start(bf16[2,16,256]{2,1,0:T(8,128)(2,1)S(1)} %coeffs.1.refs_0_.others_0_), channel_id=1, source_target_pairs={{0,8},{4,12},{8,0},{12,4},{1,9},{5,13},{9,1},{13,5},{2,10},{6,14},... | collective-permute-start | bytes 49160 | tf_op jit(solution)/shard_map/ppermute | solution.py:412
  20.0 0.5 %collective-permute-done.12.message = bf16[16,16,256]{2,1,0:T(8,128)(2,1)S(1)} collective-permute-done((bf16[16,16,256]{2,1,0:T(8,128)(2,1)S(1)}, bf16[16,16,256]{2,1,0:T(8,128)(2,1)S(1)}, u32[]{:S(2)}, u32[]{:S(2)}) %collective-permute-start.12) | collective-permute-done | bytes 131104 | tf_op jit(solution)/shard_map/ppermute | solution.py:412
  20.5 0.0 collective-permute-done.11.others_1_.current_beside
  20.5 0.1 collective-permute-start.13
  20.6 0.6 %self.1.self_part = f32[16,16,256]{2,1,0:T(8,128)S(1)} custom-call(bf16[16,16,256]{2,1,0:T(8,128)(2,1)S(1)} %settle.2.current, bf16[16,256,256]{2,1,0:T(8,128)(2,1)S(1)} %copy-done), custom_call_target="tpu_custom_call" | custom-call | flops 600000000 | tf_op jit(solution)/shard_map/self/pallas_call | solution.py:446
  21.2 0.7 %collective-permute-done.8.refs_2_ = bf16[2,16,256]{2,1,0:T(8,128)(2,1)S(1)} collective-permute-done((bf16[2,16,256]{2,1,0:T(8,128)(2,1)S(1)}, bf16[2,16,256]{2,1,0:T(8,128)(2,1)S(1)}, u32[]{:S(2)}, u32[]{:S(2)}) %collective-permute-start.8) | collective-permute-done | bytes 16416 | tf_op jit(solution)/shard_map/ppermute | solution.py:412
  21.9 0.0 collective-permute-start.9
  22.0 0.0 collective-permute-done.13.column_beside
  22.0 0.0 collective-permute-done.10.beside
  22.0 1.0 %half.1 = (bf16[16,16,128]{2,1,0:T(8,128)(2,1)S(1)}, bf16[16,16,128]{2,1,0:T(8,128)(2,1)S(1)}, bf16[16,16,128]{2,1,0:T(8,128)(2,1)S(1)}, f32[16,16,128]{2,1,0:T(8,128)S(1)}) custom-call(s32[16,128]{1,0:T(8,128)S(4)} %get-tuple-element.38.table, bf16[48,256,128]{2,1,0:T(8,128)(2,1)S(1)} %get-tuple-element.26.mine, ...), custom_call_target="tpu_custom_call" | custom-call | flops 1000000000 | tf_op jit(solution)/shard_map/half/pallas_call | solution.py:560
  23.0 1.9 %collective-permute-start.14 = (bf16[16,16,128]{2,1,0:T(8,128)(2,1)S(1)}, bf16[16,16,128]{2,1,0:T(8,128)(2,1)S(1)}, u32[]{:S(2)}, u32[]{:S(2)}) collective-permute-start(bf16[16,16,128]{2,1,0:T(8,128)(2,1)S(1)} %get-tuple-element.42), channel_id=1, source_target_pairs={{0,8},{4,12},{8,0},{12,4},{1,9},{5,13},{9,1},{13,5},{2,10},{6,14},... | collective-permute-start | bytes 196616 | tf_op jit(solution)/shard_map/ppermute | solution.py:412
  24.9 0.2 collective-permute-start.15
  25.1 0.1 collective-permute-start.16
  25.2 0.6 %far.3.far_part = f32[16,16,256]{2,1,0:T(8,128)S(1)} custom-call(s32[16,128]{1,0:T(8,128)S(4)} %get-tuple-element.25.table, bf16[16,64,64]{2,1,0:T(8,128)(2,1)S(1)} %copy-done.3, bf16[16,64,256]{2,1,0:T(8,128)(2,1)S(1)} %copy-done.1, bf16[8,64,512]{2,1,0:T(8,128)(2,1)S(1)} %copy-done.2, bf16[2,16,256]{2,1,0:T(8,128)(2,1)S(1)} %coeffs.1.refs_0_.others_0_, ...), custom_call_target="tpu_custom_call" | custom-call | flops 500000000 | tf_op jit(solution)/shard_map/far/pallas_call | solution.py:497
  25.8 1.8 %collective-permute-done.14.crossed = bf16[16,16,128]{2,1,0:T(8,128)(2,1)S(1)} collective-permute-done((bf16[16,16,128]{2,1,0:T(8,128)(2,1)S(1)}, bf16[16,16,128]{2,1,0:T(8,128)(2,1)S(1)}, u32[]{:S(2)}, u32[]{:S(2)}) %collective-permute-start.14) | collective-permute-done | bytes 65568 | tf_op jit(solution)/shard_map/ppermute | solution.py:412
  27.6 1.4 %collective-permute-done.16.diagonal = bf16[16,16,128]{2,1,0:T(8,128)(2,1)S(1)} collective-permute-done((bf16[16,16,128]{2,1,0:T(8,128)(2,1)S(1)}, bf16[16,16,128]{2,1,0:T(8,128)(2,1)S(1)}, u32[]{:S(2)}, u32[]{:S(2)}) %collective-permute-start.16) | collective-permute-done | bytes 65568 | tf_op jit(solution)/shard_map/ppermute | solution.py:564
  29.1 0.7 %last.1 = bf16[16,16,256]{2,1,0:T(8,128)(2,1)} custom-call(f32[16,16,256]{2,1,0:T(8,128)S(1)} %self.1.self_part, f32[16,16,256]{2,1,0:T(8,128)S(1)} %far.3.far_part, f32[16,16,128]{2,1,0:T(8,128)S(1)} %get-tuple-element.41.keep, bf16[16,16,128]{2,1,0:T(8,128)(2,1)S(1)} %collective-permute-done.14.crossed, ...), custom_call_target="tpu_custom_call" | custom-call | flops 100000000 | tf_op jit(solution)/shard_map/last/pallas_call | solution.py:567
  (19 shorter events, 0.1 us)
Async XLA Ops:
  0.0 6.7 %collective-permute-start.1 = (bf16[16,16,256]{2,1,0:T(8,128)(2,1)}, bf16[16,16,256]{2,1,0:T(8,128)(2,1)S(1)}, u32[]{:S(2)}, u32[]{:S(2)}) collective-permute-start(bf16[16,16,256]{2,1,0:T(8,128)(2,1)} %vectors.1), channel_id=1, source_target_pairs={{0,8},{4,12},{8,0},{12,4},{1,9},{5,13},{9,1},{13,5},{2,10},{6,14},... | collective-permute-start | bytes 393224 | tf_op jit(solution)/shard_map/ppermute | solution.py:412
  3.0 3.8 %copy-start.4 = (bf16[48,256,256]{2,1,0:T(8,128)(2,1)S(1)}, bf16[48,256,256]{2,1,0:T(8,128)(2,1)}, u32[]{:S(2)}) copy-start(bf16[48,256,256]{2,1,0:T(8,128)(2,1)} %tiles.1) | copy-start | bytes 18874372
  4.9 1.8 %collective-permute-start.2 = (s32[8,128]{1,0:T(8,128)S(1)}, s32[8,128]{1,0:T(8,128)S(1)}, u32[]{:S(2)}, u32[]{:S(2)}) collective-permute-start(s32[8,128]{1,0:T(8,128)S(1)} %get-tuple-element.30.places), channel_id=1, source_target_pairs={{0,4},{4,0},{8,12},{12,8},{1,5},{5,1},{9,13},{13,9},{2,6},{6,2},{1... | collective-permute-start | bytes 12296 | tf_op jit(solution)/shard_map/ppermute | solution.py:409
  5.0 3.8 %collective-permute-start.4 = (bf16[2,16,256]{2,1,0:T(8,128)(2,1)S(1)}, bf16[2,16,256]{2,1,0:T(8,128)(2,1)S(1)}, u32[]{:S(2)}, u32[]{:S(2)}) collective-permute-start(bf16[2,16,256]{2,1,0:T(8,128)(2,1)S(1)} %get-tuple-element.29.refs_1_.refs_4_.refs_0_), channel_id=1, source_target_pairs={{0,8},{4,12},{8,0},{12,4},{1,9},{5,13},{9,1},{13,5},{2,10},{6,14},... | collective-permute-start | bytes 49160 | tf_op jit(solution)/shard_map/ppermute | solution.py:412
  5.1 3.7 %collective-permute-start = (bf16[16,16,256]{2,1,0:T(8,128)(2,1)S(1)}, bf16[16,16,256]{2,1,0:T(8,128)(2,1)S(1)}, u32[]{:S(2)}, u32[]{:S(2)}) collective-permute-start(bf16[16,16,256]{2,1,0:T(8,128)(2,1)S(1)} %get-tuple-element.28.refs_0_.current), channel_id=1, source_target_pairs={{0,4},{4,0},{8,12},{12,8},{1,5},{5,1},{9,13},{13,9},{2,6},{6,2},{1... | collective-permute-start | bytes 393224 | tf_op jit(solution)/shard_map/ppermute | solution.py:409
  6.7 2.1 %collective-permute-start.3 = (bf16[16,16,256]{2,1,0:T(8,128)(2,1)S(1)}, bf16[16,16,256]{2,1,0:T(8,128)(2,1)S(1)}, u32[]{:S(2)}, u32[]{:S(2)}) collective-permute-start(bf16[16,16,256]{2,1,0:T(8,128)(2,1)S(1)} %tie.2), channel_id=1, source_target_pairs={{0,4},{4,0},{8,12},{12,8},{1,5},{5,1},{9,13},{13,9},{2,6},{6,2},{1... | collective-permute-start | bytes 393224 | tf_op jit(solution)/shard_map/ppermute | solution.py:409
  9.8 1.7 %collective-permute-start.5 = (bf16[20,16,256]{2,1,0:T(8,128)(2,1)S(1)}, bf16[20,16,256]{2,1,0:T(8,128)(2,1)S(1)}, u32[]{:S(2)}, u32[]{:S(2)}) collective-permute-start(bf16[20,16,256]{2,1,0:T(8,128)(2,1)S(1)} %get-tuple-element.32), channel_id=1, source_target_pairs={{0,4},{4,0},{8,12},{12,8},{1,5},{5,1},{9,13},{13,9},{2,6},{6,2},{1... | collective-permute-start | bytes 491528 | tf_op jit(solution)/shard_map/ppermute | solution.py:409
  10.1 1.4 %collective-permute-start.6 = (bf16[16,16,256]{2,1,0:T(8,128)(2,1)S(1)}, bf16[16,16,256]{2,1,0:T(8,128)(2,1)S(1)}, u32[]{:S(2)}, u32[]{:S(2)}) collective-permute-start(bf16[16,16,256]{2,1,0:T(8,128)(2,1)S(1)} %get-tuple-element.34), channel_id=1, source_target_pairs={{0,4},{4,0},{8,12},{12,8},{1,5},{5,1},{9,13},{13,9},{2,6},{6,2},{1... | collective-permute-start | bytes 393224 | tf_op jit(solution)/shard_map/ppermute | solution.py:409
  11.5 2.1 %copy-start = (bf16[16,256,256]{2,1,0:T(8,128)(2,1)S(1)}, bf16[16,256,256]{2,1,0:T(8,128)(2,1)}, u32[]{:S(2)}) copy-start(bf16[16,256,256]{2,1,0:T(8,128)(2,1)} %self_tiles.3) | copy-start | bytes 6291460
  11.5 2.8 %copy-start.1 = (bf16[16,64,256]{2,1,0:T(8,128)(2,1)S(1)}, bf16[16,64,256]{2,1,0:T(8,128)(2,1)}, u32[]{:S(2)}) copy-start(bf16[16,64,256]{2,1,0:T(8,128)(2,1)} %row_basis.3) | copy-start | bytes 1572868
  11.6 2.8 %copy-start.2 = (bf16[8,64,512]{2,1,0:T(8,128)(2,1)S(1)}, bf16[8,64,512]{2,1,0:T(8,128)(2,1)}, u32[]{:S(2)}) copy-start(bf16[8,64,512]{2,1,0:T(8,128)(2,1)} %coupling.3) | copy-start | bytes 1572868
  11.6 2.8 %copy-start.3 = (bf16[16,64,64]{2,1,0:T(8,128)(2,1)S(1)}, bf16[16,64,64]{2,1,0:T(8,128)(2,1)}, u32[]{:S(2)}) copy-start(bf16[16,64,64]{2,1,0:T(8,128)(2,1)} %row_transfer.3) | copy-start | bytes 393220
  11.6 6.1 %copy-start.5 = (bf16[16,64,256]{2,1,0:T(8,128)(2,1)S(1)}, bf16[16,64,256]{2,1,0:T(8,128)(2,1)}, u32[]{:S(2)}) copy-start(bf16[16,64,256]{2,1,0:T(8,128)(2,1)} %column_basis.3) | copy-start | bytes 1572868
  11.6 6.1 %copy-start.6 = (bf16[16,64,64]{2,1,0:T(8,128)(2,1)S(1)}, bf16[16,64,64]{2,1,0:T(8,128)(2,1)}, u32[]{:S(2)}) copy-start(bf16[16,64,64]{2,1,0:T(8,128)(2,1)} %column_transfer.3) | copy-start | bytes 393220
  11.6 10.4 %collective-permute-start.10 = (bf16[48,256,128]{2,1,0:T(8,128)(2,1)S(1)}, bf16[48,256,128]{2,1,0:T(8,128)(2,1)S(1)}, u32[]{:S(2)}, u32[]{:S(2)}) collective-permute-start(bf16[48,256,128]{2,1,0:T(8,128)(2,1)S(1)} %tie.3), channel_id=1, source_target_pairs={{0,4},{4,0},{8,12},{12,8},{1,5},{5,1},{9,13},{13,9},{2,6},{6,2},{1... | collective-permute-start | bytes 9437192 | tf_op jit(solution)/shard_map/ppermute | solution.py:409
  12.0 5.6 %collective-permute-start.7 = (bf16[16,16,256]{2,1,0:T(8,128)(2,1)S(1)}, bf16[16,16,256]{2,1,0:T(8,128)(2,1)S(1)}, u32[]{:S(2)}, u32[]{:S(2)}) collective-permute-start(bf16[16,16,256]{2,1,0:T(8,128)(2,1)S(1)} %get-tuple-element.35.sent_before.refs_1_), channel_id=1, source_target_pairs={{0,8},{4,12},{8,0},{12,4},{1,9},{5,13},{9,1},{13,5},{2,10},{6,14},... | collective-permute-start | bytes 393224 | tf_op jit(solution)/shard_map/ppermute | solution.py:412
  15.0 5.5 %collective-permute-start.12 = (bf16[16,16,256]{2,1,0:T(8,128)(2,1)S(1)}, bf16[16,16,256]{2,1,0:T(8,128)(2,1)S(1)}, u32[]{:S(2)}, u32[]{:S(2)}) collective-permute-start(bf16[16,16,256]{2,1,0:T(8,128)(2,1)S(1)} %get-tuple-element.40), channel_id=1, source_target_pairs={{0,8},{4,12},{8,0},{12,4},{1,9},{5,13},{9,1},{13,5},{2,10},{6,14},... | collective-permute-start | bytes 393224 | tf_op jit(solution)/shard_map/ppermute | solution.py:412
  17.6 2.9 %collective-permute-start.11 = (bf16[16,16,256]{2,1,0:T(8,128)(2,1)S(1)}, bf16[16,16,256]{2,1,0:T(8,128)(2,1)S(1)}, u32[]{:S(2)}, u32[]{:S(2)}) collective-permute-start(bf16[16,16,256]{2,1,0:T(8,128)(2,1)S(1)} %settle.2.current), channel_id=1, source_target_pairs={{0,4},{4,0},{8,12},{12,8},{1,5},{5,1},{9,13},{13,9},{2,6},{6,2},{1... | collective-permute-start | bytes 393224 | tf_op jit(solution)/shard_map/ppermute | solution.py:409
  18.2 3.8 %collective-permute-start.8 = (bf16[2,16,256]{2,1,0:T(8,128)(2,1)S(1)}, bf16[2,16,256]{2,1,0:T(8,128)(2,1)S(1)}, u32[]{:S(2)}, u32[]{:S(2)}) collective-permute-start(bf16[2,16,256]{2,1,0:T(8,128)(2,1)S(1)} %coeffs.1.refs_0_.others_0_), channel_id=1, source_target_pairs={{0,8},{4,12},{8,0},{12,4},{1,9},{5,13},{9,1},{13,5},{2,10},{6,14},... | collective-permute-start | bytes 49160 | tf_op jit(solution)/shard_map/ppermute | solution.py:412
  20.5 1.4 %collective-permute-start.13 = (bf16[16,16,256]{2,1,0:T(8,128)(2,1)S(1)}, bf16[16,16,256]{2,1,0:T(8,128)(2,1)S(1)}, u32[]{:S(2)}, u32[]{:S(2)}) collective-permute-start(bf16[16,16,256]{2,1,0:T(8,128)(2,1)S(1)} %settle.3.column), channel_id=1, source_target_pairs={{0,4},{4,0},{8,12},{12,8},{1,5},{5,1},{9,13},{13,9},{2,6},{6,2},{1... | collective-permute-start | bytes 393224 | tf_op jit(solution)/shard_map/ppermute | solution.py:409
  21.9 3.3 %collective-permute-start.9 = (bf16[4,16,256]{2,1,0:T(8,128)(2,1)S(1)}, bf16[4,16,256]{2,1,0:T(8,128)(2,1)S(1)}, u32[]{:S(2)}, u32[]{:S(2)}) collective-permute-start(bf16[4,16,256]{2,1,0:T(8,128)(2,1)S(1)} %pad_maximum_fusion), channel_id=1, source_target_pairs={{0,4},{4,0},{8,12},{12,8},{1,5},{5,1},{9,13},{13,9},{2,6},{6,2},{1... | collective-permute-start | bytes 98312 | tf_op jit(solution)/shard_map/ppermute | solution.py:409
  23.0 4.6 %collective-permute-start.14 = (bf16[16,16,128]{2,1,0:T(8,128)(2,1)S(1)}, bf16[16,16,128]{2,1,0:T(8,128)(2,1)S(1)}, u32[]{:S(2)}, u32[]{:S(2)}) collective-permute-start(bf16[16,16,128]{2,1,0:T(8,128)(2,1)S(1)} %get-tuple-element.42), channel_id=1, source_target_pairs={{0,8},{4,12},{8,0},{12,4},{1,9},{5,13},{9,1},{13,5},{2,10},{6,14},... | collective-permute-start | bytes 196616 | tf_op jit(solution)/shard_map/ppermute | solution.py:412
  24.9 2.8 %collective-permute-start.15 = (bf16[16,16,128]{2,1,0:T(8,128)(2,1)S(1)}, bf16[16,16,128]{2,1,0:T(8,128)(2,1)S(1)}, u32[]{:S(2)}, u32[]{:S(2)}) collective-permute-start(bf16[16,16,128]{2,1,0:T(8,128)(2,1)S(1)} %get-tuple-element.43), channel_id=1, source_target_pairs={{0,4},{4,0},{8,12},{12,8},{1,5},{5,1},{9,13},{13,9},{2,6},{6,2},{1... | collective-permute-start | bytes 196616 | tf_op jit(solution)/shard_map/ppermute | solution.py:409
  25.1 4.0 %collective-permute-start.16 = (bf16[16,16,128]{2,1,0:T(8,128)(2,1)S(1)}, bf16[16,16,128]{2,1,0:T(8,128)(2,1)S(1)}, u32[]{:S(2)}, u32[]{:S(2)}) collective-permute-start(bf16[16,16,128]{2,1,0:T(8,128)(2,1)S(1)} %get-tuple-element.44), channel_id=1, source_target_pairs={{0,12},{4,8},{8,4},{12,0},{1,13},{5,9},{9,5},{13,1},{2,14},{6,10},... | collective-permute-start | bytes 196616 | tf_op jit(solution)/shard_map/ppermute | solution.py:564

commit v6 on v5

--- a/solution.py
+++ b/solution.py
@@ -179,7 +179,7 @@
 def near_kernel(panel_count, packed_count, table, mine, theirs, *refs):
     panels, refs = refs[:panel_count], refs[panel_count:]
     packed = refs[:packed_count]
-    send, send_own, keep, keep_own, gathered, products, sums = refs[-7:]
+    send, keep, keep_own, gathered, products, sums = refs[-6:]
     each = gathered.shape[0] // panel_count
     for k, panel in enumerate(panels):
         gathered[k * each : (k + 1) * each] = panel[:each]
@@ -200,11 +200,11 @@
             [jnp.where(core == 0, here, beside), jnp.where(core == 0, beside, here)], axis=-1
         )
 
-    send_own[:own] = in_order(sums[:own]).astype(BF16)
+    send[half - own : half] = in_order(sums[:own]).astype(BF16)
     for k, coeffs in enumerate(packed):
         rows = coeffs.shape[0]
-        send_own[own + k * rows : own + (k + 1) * rows] = coeffs[...]
-    send[...] = in_order(sums[own:half]).astype(BF16)
+        send[half + k * rows : half + (k + 1) * rows] = coeffs[...]
+    send[: half - own] = in_order(sums[own:half]).astype(BF16)
     keep_own[...] = in_order(sums[half : half + own])
     keep[...] = in_order(sums[half + own :])
 
@@ -304,13 +304,14 @@
 
 
 def other_kernel(keep, arrived, message, sums):
-    other = keep[...] + arrived[...].astype(F32)
+    other = keep[...] + arrived[: keep.shape[0]].astype(F32)
     sums[...] = other
     message[...] = other.astype(BF16)
 
 
 def own_kernel(keep, arrived, self_part, far_part, sent_before, message, sums):
-    near = keep[...] + arrived[: keep.shape[0]].astype(F32)
+    own_rows = pl.ds(keep.shape[0], keep.shape[0])
+    near = keep[...] + arrived[own_rows].astype(F32)
     own = near + self_part[...] + far_part[...]
     sums[...] = own
     message[...] = own.astype(BF16)
@@ -452,8 +453,7 @@
             functools.partial(near_kernel, len(given), len(packed)),
             "near",
             (
-                panels((columns - 1) * clusters, BF16),
-                panels(clusters + len(packed) * rows, BF16),
+                panels(columns * clusters + len(packed) * rows, BF16),
                 panels((columns - 1) * clusters, F32),
                 panels(clusters, F32),
             ),
@@ -524,12 +524,12 @@
         given += [x, to_sibling(tie(x, packed, places_beside))]
     crossed = across(packed)
     mine, theirs = turn_call(*in_vmem(near_tiles))
-    send, send_own, keep, keep_own = near_call(table, given, [packed, *crossed])
-    arrived, arrived_own = to_sibling(send), to_sibling(send_own)
+    send, keep, keep_own = near_call(table, given, [packed, *crossed])
+    arrived = to_sibling(send)
     pieces, starts = [], []
     for k, piece in enumerate([packed, *crossed]):
-        pieces += [piece, arrived_own]
-        starts += [0, clusters + k * rows]
+        pieces += [piece, arrived]
+        starts += [0, columns * clusters + k * rows]
 
     if columns == 2 and ITERS == 2:
         both_out = (panels(clusters, BF16), panels(clusters, F32))
@@ -540,10 +540,10 @@
         self_part, both_places = first_self_call(
             *in_vmem(current, self_tiles, places, places_beside), other
         )
-        theirs = to_sibling(tie(theirs, other,arrived_own, places_beside))
+        theirs = to_sibling(tie(theirs, other, places_beside))
         own, own_sums = call(
             own_kernel, "own", both_out, [VMEM_SPEC] * 4 + [ANY_SPEC], us=0.1
-        )(*in_vmem(keep_own, arrived_own, self_part, far_part), other)
+        )(*in_vmem(keep_own, arrived, self_part, far_part), other)
 
         def settled(sums, message, *others):
             specs = [VMEM_SPEC] * 2 + [ANY_SPEC] * len(others)
@@ -572,7 +572,7 @@
     far_part = far_call(table, pieces, starts)
 
     def finished():
-        near = keep_own + arrived_own[:clusters].astype(F32)
+        near = keep_own + arrived[(columns - 1) * clusters : columns * clusters].astype(F32)
         for s in range(1, columns):
             part = slice((s - 1) * clusters, s * clusters)
             partial = (keep[part] + arrived[part].astype(F32)).astype(BF16)
@@ -584,8 +584,8 @@
             message_kernel, "message", panels(clusters + rows, BF16), [VMEM_SPEC] * 3, us=0.5
         )(*in_vmem(finished(), column_basis, column_transfer))
         messages = gather(message)
-        send, send_own, keep, keep_own = near_call(table, messages)
-        arrived, arrived_own = to_sibling(send), to_sibling(send_own)
+        send, keep, keep_own = near_call(table, messages)
+        arrived = to_sibling(send)
         self_part = self_call(message)
         far_part = far_call(table, messages)
     return finished()

time: 29.9 us -> 29.9 us (level)
  starting transfers between devices: 11.6 us -> 10.9 us
  waiting for transfers between devices: 8.35 us -> 9.01 us
    ppermute x10 -> x9, starting transfers between devices: 1.83 us -> 1.42 us  [to_sibling(): return lax.ppermute(x, 'loop', sibling)]
    ppermute x6, starting transfers between devices: 9.66 us -> 9.25 us  [to_column(): lax.ppermute(x, 'loop', [(i, (i + 2 * shift) % count) for i in range(coun...]
    ppermute x6, waiting for transfers between devices: 5.8 us -> 6.2 us  [to_column(): lax.ppermute(x, 'loop', [(i, (i + 2 * shift) % count) for i in range(coun...]
    ppermute x10 -> x9, waiting for transfers between devices: 1.1 us -> 1.41 us  [to_sibling(): return lax.ppermute(x, 'loop', sibling)]
  transfers between devices with their start and end apart: 17 -> 16, of which waited for: 8 -> 8; matrix products, arithmetic and copies ran while one was open for 0% -> 0% of each run, Pallas kernels for 26% -> 26%
where the time goes in v6:
time: 29.9 us; the launch traced here: 29.7 us
  starting transfers between devices  10.9 us (36%)
  Pallas kernels  9.49 us (32%)
  waiting for transfers between devices  9.01 us (30%)
    ppermute x6, starting transfers between devices, to_column(): lax.ppermute(x, 'loop', [(i, (i + 2 * shift) % count) for i in range(coun...  9.25 us
    ppermute x6, waiting for transfers between devices, to_column(): lax.ppermute(x, 'loop', [(i, (i + 2 * shift) % count) for i in range(coun...  6.2 us
    pallas_call x1, Pallas kernels, on_device(): first_call(*in_hbm(*raw, vectors, column_basis, column_transfer))  1.93 us
    pallas_call x1, Pallas kernels, on_device(): mine, theirs = turn_call(*in_vmem(near_tiles))  1.68 us
    ppermute x9, starting transfers between devices, to_sibling(): return lax.ppermute(x, 'loop', sibling)  1.42 us
    ppermute x9, waiting for transfers between devices, to_sibling(): return lax.ppermute(x, 'loop', sibling)  1.41 us
    ppermute x1, waiting for transfers between devices, on_device(): lax.ppermute(diagonal, 'loop', [(i, i ^ 3) for i in range(count)])  1.4 us
    pallas_call x2, Pallas kernels, far_call(): call(functools.partial(far_kernel, tuple(starts), rows), 'far', panels(cl...  1.12 us
  transfers between devices with their start and end apart: 16, of which 8 were waited for; matrix products, arithmetic and copies ran while one was open for 0% of the time, Pallas kernels for 26%

profile of v6, /device:TPU:0, one launch (start us, length us, event | category | flops | bytes accessed | tf_op | source)
XLA Modules:
  0.0 29.7 jit_solution(1075271940076905558)
XLA Ops:
  0.0 3.0 %collective-permute-start.1 = (bf16[16,16,256]{2,1,0:T(8,128)(2,1)}, bf16[16,16,256]{2,1,0:T(8,128)(2,1)S(1)}, u32[]{:S(2)}, u32[]{:S(2)}) collective-permute-start(bf16[16,16,256]{2,1,0:T(8,128)(2,1)} %vectors.1), channel_id=1, source_target_pairs={{0,8},{4,12},{8,0},{12,4},{1,9},{5,13},{9,1},{13,5},{2,10},{6,14},... | collective-permute-start | bytes 393224 | tf_op jit(solution)/shard_map/ppermute | solution.py:413
  3.0 1.9 %first.1 = (bf16[2,16,256]{2,1,0:T(8,128)(2,1)S(1)}, bf16[16,16,256]{2,1,0:T(8,128)(2,1)S(1)}, s32[8,128]{1,0:T(8,128)S(1)}, s32[16,128]{1,0:T(8,128)S(4)}) custom-call(s32[1,48]{1,0:T(1,128)} %bitcast.4, s32[1,48]{1,0:T(1,128)} %bitcast.5, s32[2,48]{1,0:T(2,128)} %bitcast.3, s32[8,8]{1,0:T(8,128)} %far_source.1, bf16[16,16,256]{2,1,0:T(8,128)(2,1)} %vectors.1, ...), custom_call_target="tpu_custom_call" | custom-call | flops 10000000000 | tf_op jit(solution)/shard_map/first/pallas_call | solution.py:520
  4.9 0.1 collective-permute-start.2
  5.0 0.1 collective-permute-start.4
  5.1 0.4 %collective-permute-start = (bf16[16,16,256]{2,1,0:T(8,128)(2,1)S(1)}, bf16[16,16,256]{2,1,0:T(8,128)(2,1)S(1)}, u32[]{:S(2)}, u32[]{:S(2)}) collective-permute-start(bf16[16,16,256]{2,1,0:T(8,128)(2,1)S(1)} %get-tuple-element.27.refs_0_.current), channel_id=1, source_target_pairs={{0,4},{4,0},{8,12},{12,8},{1,5},{5,1},{9,13},{13,9},{2,6},{6,2},{1... | collective-permute-start | bytes 393224 | tf_op jit(solution)/shard_map/ppermute | solution.py:410
  5.5 1.2 %collective-permute-done.1.refs_2_ = bf16[16,16,256]{2,1,0:T(8,128)(2,1)S(1)} collective-permute-done((bf16[16,16,256]{2,1,0:T(8,128)(2,1)}, bf16[16,16,256]{2,1,0:T(8,128)(2,1)S(1)}, u32[]{:S(2)}, u32[]{:S(2)}) %collective-permute-start.1) | collective-permute-done | bytes 131104 | tf_op jit(solution)/shard_map/ppermute | solution.py:413
  6.7 0.0 collective-permute-done.2.refs_2_.places_beside
  6.7 0.1 collective-permute-start.3
  6.8 1.7 %turn.1 = (bf16[48,256,128]{2,1,0:T(8,128)(2,1)S(1)}, bf16[48,256,128]{2,1,0:T(8,128)(2,1)S(1)}) custom-call(bf16[48,256,256]{2,1,0:T(8,128)(2,1)S(1)} %copy-done.4), custom_call_target="tpu_custom_call" | custom-call | flops 2500000000 | tf_op jit(solution)/shard_map/turn/pallas_call | solution.py:526
  8.5 0.3 %collective-permute-done.4.refs_5_.refs_2_ = bf16[2,16,256]{2,1,0:T(8,128)(2,1)S(1)} collective-permute-done((bf16[2,16,256]{2,1,0:T(8,128)(2,1)S(1)}, bf16[2,16,256]{2,1,0:T(8,128)(2,1)S(1)}, u32[]{:S(2)}, u32[]{:S(2)}) %collective-permute-start.4) | collective-permute-done | bytes 16416 | tf_op jit(solution)/shard_map/ppermute | solution.py:413
  8.8 0.0 collective-permute-done.refs_1_
  8.8 0.0 collective-permute-done.3.refs_3_
  8.8 1.0 %near.1 = (bf16[36,16,256]{2,1,0:T(8,128)(2,1)S(1)}, f32[16,16,256]{2,1,0:T(8,128)S(1)}, f32[16,16,256]{2,1,0:T(8,128)S(1)}) custom-call(s32[16,128]{1,0:T(8,128)S(4)} %get-tuple-element.24.table, bf16[48,256,128]{2,1,0:T(8,128)(2,1)S(1)} %get-tuple-element.25.mine, bf16[48,256,128]{2,1,0:T(8,128)(2,1)S(1)} %get-tuple-element.26.theirs.refs_0_, ...), custom_call_target="tpu_custom_call" | custom-call | flops 1000000000 | tf_op jit(solution)/shard_map/near/pallas_call | solution.py:452
  9.8 0.3 collective-permute-start.5
  10.1 1.4 %collective-permute-done.5.arrived.refs_1_.refs_3_ = bf16[36,16,256]{2,1,0:T(8,128)(2,1)S(1)} collective-permute-done((bf16[36,16,256]{2,1,0:T(8,128)(2,1)S(1)}, bf16[36,16,256]{2,1,0:T(8,128)(2,1)S(1)}, u32[]{:S(2)}, u32[]{:S(2)}) %collective-permute-start.5) | collective-permute-done | bytes 294944 | tf_op jit(solution)/shard_map/ppermute | solution.py:410
  11.5 0.0 copy-start.1
  11.5 0.0 copy-start.2
  11.6 0.0 copy-start.3
  11.6 0.0 copy-start
  11.6 0.0 copy-start.5
  11.6 0.0 copy-start.6
  11.6 0.3 collective-permute-start.9
  11.9 1.7 %collective-permute-start.6 = (bf16[16,16,256]{2,1,0:T(8,128)(2,1)S(1)}, bf16[16,16,256]{2,1,0:T(8,128)(2,1)S(1)}, u32[]{:S(2)}, u32[]{:S(2)}) collective-permute-start(bf16[16,16,256]{2,1,0:T(8,128)(2,1)S(1)} %get-tuple-element.33.sent_before.refs_1_), channel_id=1, source_target_pairs={{0,8},{4,12},{8,0},{12,4},{1,9},{5,13},{9,1},{13,5},{2,10},{6,14},... | collective-permute-start | bytes 393224 | tf_op jit(solution)/shard_map/ppermute | solution.py:413
  13.6 0.6 %far.2.far_part = f32[16,16,256]{2,1,0:T(8,128)S(1)} custom-call(s32[16,128]{1,0:T(8,128)S(4)} %get-tuple-element.24.table, bf16[16,64,64]{2,1,0:T(8,128)(2,1)S(1)} %copy-done.3, bf16[16,64,256]{2,1,0:T(8,128)(2,1)S(1)} %copy-done.1, bf16[8,64,512]{2,1,0:T(8,128)(2,1)S(1)} %copy-done.2, bf16[2,16,256]{2,1,0:T(8,128)(2,1)S(1)} %get-tuple-element.28.refs_1_.refs_4_.refs_0_, ...), custom_call_target="tpu_custom_call" | custom-call | flops 500000000 | tf_op jit(solution)/shard_map/far/pallas_call | solution.py:497
  14.2 0.0 copy-done
  14.2 0.7 %first_self.1 = (f32[16,16,256]{2,1,0:T(8,128)S(1)}, s32[16,128]{1,0:T(8,128)S(4)}) custom-call(bf16[16,16,256]{2,1,0:T(8,128)(2,1)S(1)} %get-tuple-element.27.refs_0_.current, bf16[16,256,256]{2,1,0:T(8,128)(2,1)S(1)} %copy-done, s32[8,128]{1,0:T(8,128)S(1)} %get-tuple-element.29.places, s32[8,128]{1,0:T(8,128)S(1)} %collective-permute-done.2.refs_2_.places_beside, ...), custom_call_target="tpu_custom_call" | custom-call | flops 600000000 | tf_op jit(solution)/shard_map/first_self/pallas_call | solution.py:540
  14.9 0.1 own.1
  15.0 1.0 %collective-permute-start.11 = (bf16[16,16,256]{2,1,0:T(8,128)(2,1)S(1)}, bf16[16,16,256]{2,1,0:T(8,128)(2,1)S(1)}, u32[]{:S(2)}, u32[]{:S(2)}) collective-permute-start(bf16[16,16,256]{2,1,0:T(8,128)(2,1)S(1)} %get-tuple-element.38), channel_id=1, source_target_pairs={{0,8},{4,12},{8,0},{12,4},{1,9},{5,13},{9,1},{13,5},{2,10},{6,14},... | collective-permute-start | bytes 393224 | tf_op jit(solution)/shard_map/ppermute | solution.py:413
  16.0 1.7 %collective-permute-done.6.message = bf16[16,16,256]{2,1,0:T(8,128)(2,1)S(1)} collective-permute-done((bf16[16,16,256]{2,1,0:T(8,128)(2,1)S(1)}, bf16[16,16,256]{2,1,0:T(8,128)(2,1)S(1)}, u32[]{:S(2)}, u32[]{:S(2)}) %collective-permute-start.6) | collective-permute-done | bytes 131104 | tf_op jit(solution)/shard_map/ppermute | solution.py:413
  17.6 0.1 collective-permute-start.10
  17.7 0.5 %coeffs.1.refs_0_.others_0_ = bf16[2,16,256]{2,1,0:T(8,128)(2,1)S(1)} custom-call(bf16[16,16,256]{2,1,0:T(8,128)(2,1)S(1)} %settle.2.current, bf16[16,64,256]{2,1,0:T(8,128)(2,1)S(1)} %copy-done.5, bf16[16,64,64]{2,1,0:T(8,128)(2,1)S(1)} %copy-done.6), custom_call_target="tpu_custom_call" | custom-call | flops 500000000 | tf_op jit(solution)/shard_map/coeffs/pallas_call | solution.py:557
  18.2 1.7 %collective-permute-start.7 = (bf16[2,16,256]{2,1,0:T(8,128)(2,1)S(1)}, bf16[2,16,256]{2,1,0:T(8,128)(2,1)S(1)}, u32[]{:S(2)}, u32[]{:S(2)}) collective-permute-start(bf16[2,16,256]{2,1,0:T(8,128)(2,1)S(1)} %coeffs.1.refs_0_.others_0_), channel_id=1, source_target_pairs={{0,8},{4,12},{8,0},{12,4},{1,9},{5,13},{9,1},{13,5},{2,10},{6,14},... | collective-permute-start | bytes 49160 | tf_op jit(solution)/shard_map/ppermute | solution.py:413
  19.9 0.5 %collective-permute-done.11.message = bf16[16,16,256]{2,1,0:T(8,128)(2,1)S(1)} collective-permute-done((bf16[16,16,256]{2,1,0:T(8,128)(2,1)S(1)}, bf16[16,16,256]{2,1,0:T(8,128)(2,1)S(1)}, u32[]{:S(2)}, u32[]{:S(2)}) %collective-permute-start.11) | collective-permute-done | bytes 131104 | tf_op jit(solution)/shard_map/ppermute | solution.py:413
  20.4 0.0 collective-permute-done.10.others_1_.current_beside
  20.4 0.1 collective-permute-start.12
  20.5 0.6 %self.1.self_part = f32[16,16,256]{2,1,0:T(8,128)S(1)} custom-call(bf16[16,16,256]{2,1,0:T(8,128)(2,1)S(1)} %settle.2.current, bf16[16,256,256]{2,1,0:T(8,128)(2,1)S(1)} %copy-done), custom_call_target="tpu_custom_call" | custom-call | flops 600000000 | tf_op jit(solution)/shard_map/self/pallas_call | solution.py:447
  21.2 0.8 %collective-permute-done.7.refs_2_ = bf16[2,16,256]{2,1,0:T(8,128)(2,1)S(1)} collective-permute-done((bf16[2,16,256]{2,1,0:T(8,128)(2,1)S(1)}, bf16[2,16,256]{2,1,0:T(8,128)(2,1)S(1)}, u32[]{:S(2)}, u32[]{:S(2)}) %collective-permute-start.7) | collective-permute-done | bytes 16416 | tf_op jit(solution)/shard_map/ppermute | solution.py:413
  22.0 0.0 collective-permute-start.8
  22.0 0.0 collective-permute-done.9.beside
  22.0 1.0 %half.1 = (bf16[16,16,128]{2,1,0:T(8,128)(2,1)S(1)}, bf16[16,16,128]{2,1,0:T(8,128)(2,1)S(1)}, bf16[16,16,128]{2,1,0:T(8,128)(2,1)S(1)}, f32[16,16,128]{2,1,0:T(8,128)S(1)}) custom-call(s32[16,128]{1,0:T(8,128)S(4)} %get-tuple-element.36.table, bf16[48,256,128]{2,1,0:T(8,128)(2,1)S(1)} %get-tuple-element.25.mine, ...), custom_call_target="tpu_custom_call" | custom-call | flops 1000000000 | tf_op jit(solution)/shard_map/half/pallas_call | solution.py:560
  23.0 1.8 %collective-permute-start.13 = (bf16[16,16,128]{2,1,0:T(8,128)(2,1)S(1)}, bf16[16,16,128]{2,1,0:T(8,128)(2,1)S(1)}, u32[]{:S(2)}, u32[]{:S(2)}) collective-permute-start(bf16[16,16,128]{2,1,0:T(8,128)(2,1)S(1)} %get-tuple-element.40), channel_id=1, source_target_pairs={{0,8},{4,12},{8,0},{12,4},{1,9},{5,13},{9,1},{13,5},{2,10},{6,14},... | collective-permute-start | bytes 196616 | tf_op jit(solution)/shard_map/ppermute | solution.py:413
  24.8 0.2 collective-permute-start.14
  25.0 0.2 collective-permute-start.15
  25.2 0.0 collective-permute-done.8
  25.2 0.6 %far.3.far_part = f32[16,16,256]{2,1,0:T(8,128)S(1)} custom-call(s32[16,128]{1,0:T(8,128)S(4)} %get-tuple-element.24.table, bf16[16,64,64]{2,1,0:T(8,128)(2,1)S(1)} %copy-done.3, bf16[16,64,256]{2,1,0:T(8,128)(2,1)S(1)} %copy-done.1, bf16[8,64,512]{2,1,0:T(8,128)(2,1)S(1)} %copy-done.2, bf16[2,16,256]{2,1,0:T(8,128)(2,1)S(1)} %coeffs.1.refs_0_.others_0_, ...), custom_call_target="tpu_custom_call" | custom-call | flops 500000000 | tf_op jit(solution)/shard_map/far/pallas_call | solution.py:497
  25.8 1.8 %collective-permute-done.13.crossed = bf16[16,16,128]{2,1,0:T(8,128)(2,1)S(1)} collective-permute-done((bf16[16,16,128]{2,1,0:T(8,128)(2,1)S(1)}, bf16[16,16,128]{2,1,0:T(8,128)(2,1)S(1)}, u32[]{:S(2)}, u32[]{:S(2)}) %collective-permute-start.13) | collective-permute-done | bytes 65568 | tf_op jit(solution)/shard_map/ppermute | solution.py:413
  27.6 1.4 %collective-permute-done.15.diagonal = bf16[16,16,128]{2,1,0:T(8,128)(2,1)S(1)} collective-permute-done((bf16[16,16,128]{2,1,0:T(8,128)(2,1)S(1)}, bf16[16,16,128]{2,1,0:T(8,128)(2,1)S(1)}, u32[]{:S(2)}, u32[]{:S(2)}) %collective-permute-start.15) | collective-permute-done | bytes 65568 | tf_op jit(solution)/shard_map/ppermute | solution.py:564
  29.0 0.7 %last.1 = bf16[16,16,256]{2,1,0:T(8,128)(2,1)} custom-call(f32[16,16,256]{2,1,0:T(8,128)S(1)} %self.1.self_part, f32[16,16,256]{2,1,0:T(8,128)S(1)} %far.3.far_part, f32[16,16,128]{2,1,0:T(8,128)S(1)} %get-tuple-element.39.keep, bf16[16,16,128]{2,1,0:T(8,128)(2,1)S(1)} %collective-permute-done.13.crossed, ...), custom_call_target="tpu_custom_call" | custom-call | flops 100000000 | tf_op jit(solution)/shard_map/last/pallas_call | solution.py:567
  (17 shorter events, 0.1 us)
Async XLA Ops:
  0.0 6.7 %collective-permute-start.1 = (bf16[16,16,256]{2,1,0:T(8,128)(2,1)}, bf16[16,16,256]{2,1,0:T(8,128)(2,1)S(1)}, u32[]{:S(2)}, u32[]{:S(2)}) collective-permute-start(bf16[16,16,256]{2,1,0:T(8,128)(2,1)} %vectors.1), channel_id=1, source_target_pairs={{0,8},{4,12},{8,0},{12,4},{1,9},{5,13},{9,1},{13,5},{2,10},{6,14},... | collective-permute-start | bytes 393224 | tf_op jit(solution)/shard_map/ppermute | solution.py:413
  3.0 3.8 %copy-start.4 = (bf16[48,256,256]{2,1,0:T(8,128)(2,1)S(1)}, bf16[48,256,256]{2,1,0:T(8,128)(2,1)}, u32[]{:S(2)}) copy-start(bf16[48,256,256]{2,1,0:T(8,128)(2,1)} %tiles.1) | copy-start | bytes 18874372
  4.9 1.8 %collective-permute-start.2 = (s32[8,128]{1,0:T(8,128)S(1)}, s32[8,128]{1,0:T(8,128)S(1)}, u32[]{:S(2)}, u32[]{:S(2)}) collective-permute-start(s32[8,128]{1,0:T(8,128)S(1)} %get-tuple-element.29.places), channel_id=1, source_target_pairs={{0,4},{4,0},{8,12},{12,8},{1,5},{5,1},{9,13},{13,9},{2,6},{6,2},{1... | collective-permute-start | bytes 12296 | tf_op jit(solution)/shard_map/ppermute | solution.py:410
  5.0 3.8 %collective-permute-start.4 = (bf16[2,16,256]{2,1,0:T(8,128)(2,1)S(1)}, bf16[2,16,256]{2,1,0:T(8,128)(2,1)S(1)}, u32[]{:S(2)}, u32[]{:S(2)}) collective-permute-start(bf16[2,16,256]{2,1,0:T(8,128)(2,1)S(1)} %get-tuple-element.28.refs_1_.refs_4_.refs_0_), channel_id=1, source_target_pairs={{0,8},{4,12},{8,0},{12,4},{1,9},{5,13},{9,1},{13,5},{2,10},{6,14},... | collective-permute-start | bytes 49160 | tf_op jit(solution)/shard_map/ppermute | solution.py:413
  5.1 3.7 %collective-permute-start = (bf16[16,16,256]{2,1,0:T(8,128)(2,1)S(1)}, bf16[16,16,256]{2,1,0:T(8,128)(2,1)S(1)}, u32[]{:S(2)}, u32[]{:S(2)}) collective-permute-start(bf16[16,16,256]{2,1,0:T(8,128)(2,1)S(1)} %get-tuple-element.27.refs_0_.current), channel_id=1, source_target_pairs={{0,4},{4,0},{8,12},{12,8},{1,5},{5,1},{9,13},{13,9},{2,6},{6,2},{1... | collective-permute-start | bytes 393224 | tf_op jit(solution)/shard_map/ppermute | solution.py:410
  6.7 2.1 %collective-permute-start.3 = (bf16[16,16,256]{2,1,0:T(8,128)(2,1)S(1)}, bf16[16,16,256]{2,1,0:T(8,128)(2,1)S(1)}, u32[]{:S(2)}, u32[]{:S(2)}) collective-permute-start(bf16[16,16,256]{2,1,0:T(8,128)(2,1)S(1)} %tie.2), channel_id=1, source_target_pairs={{0,4},{4,0},{8,12},{12,8},{1,5},{5,1},{9,13},{13,9},{2,6},{6,2},{1... | collective-permute-start | bytes 393224 | tf_op jit(solution)/shard_map/ppermute | solution.py:410
  9.8 1.6 %collective-permute-start.5 = (bf16[36,16,256]{2,1,0:T(8,128)(2,1)S(1)}, bf16[36,16,256]{2,1,0:T(8,128)(2,1)S(1)}, u32[]{:S(2)}, u32[]{:S(2)}) collective-permute-start(bf16[36,16,256]{2,1,0:T(8,128)(2,1)S(1)} %get-tuple-element.31), channel_id=1, source_target_pairs={{0,4},{4,0},{8,12},{12,8},{1,5},{5,1},{9,13},{13,9},{2,6},{6,2},{1... | collective-permute-start | bytes 884744 | tf_op jit(solution)/shard_map/ppermute | solution.py:410
  11.5 2.1 %copy-start.1 = (bf16[16,64,256]{2,1,0:T(8,128)(2,1)S(1)}, bf16[16,64,256]{2,1,0:T(8,128)(2,1)}, u32[]{:S(2)}) copy-start(bf16[16,64,256]{2,1,0:T(8,128)(2,1)} %row_basis.3) | copy-start | bytes 1572868
  11.5 2.1 %copy-start.2 = (bf16[8,64,512]{2,1,0:T(8,128)(2,1)S(1)}, bf16[8,64,512]{2,1,0:T(8,128)(2,1)}, u32[]{:S(2)}) copy-start(bf16[8,64,512]{2,1,0:T(8,128)(2,1)} %coupling.3) | copy-start | bytes 1572868
  11.6 2.1 %copy-start.3 = (bf16[16,64,64]{2,1,0:T(8,128)(2,1)S(1)}, bf16[16,64,64]{2,1,0:T(8,128)(2,1)}, u32[]{:S(2)}) copy-start(bf16[16,64,64]{2,1,0:T(8,128)(2,1)} %row_transfer.3) | copy-start | bytes 393220
  11.6 2.6 %copy-start = (bf16[16,256,256]{2,1,0:T(8,128)(2,1)S(1)}, bf16[16,256,256]{2,1,0:T(8,128)(2,1)}, u32[]{:S(2)}) copy-start(bf16[16,256,256]{2,1,0:T(8,128)(2,1)} %self_tiles.3) | copy-start | bytes 6291460
  11.6 6.1 %copy-start.5 = (bf16[16,64,256]{2,1,0:T(8,128)(2,1)S(1)}, bf16[16,64,256]{2,1,0:T(8,128)(2,1)}, u32[]{:S(2)}) copy-start(bf16[16,64,256]{2,1,0:T(8,128)(2,1)} %column_basis.3) | copy-start | bytes 1572868
  11.6 6.1 %copy-start.6 = (bf16[16,64,64]{2,1,0:T(8,128)(2,1)S(1)}, bf16[16,64,64]{2,1,0:T(8,128)(2,1)}, u32[]{:S(2)}) copy-start(bf16[16,64,64]{2,1,0:T(8,128)(2,1)} %column_transfer.3) | copy-start | bytes 393220
  11.6 10.4 %collective-permute-start.9 = (bf16[48,256,128]{2,1,0:T(8,128)(2,1)S(1)}, bf16[48,256,128]{2,1,0:T(8,128)(2,1)S(1)}, u32[]{:S(2)}, u32[]{:S(2)}) collective-permute-start(bf16[48,256,128]{2,1,0:T(8,128)(2,1)S(1)} %tie.3), channel_id=1, source_target_pairs={{0,4},{4,0},{8,12},{12,8},{1,5},{5,1},{9,13},{13,9},{2,6},{6,2},{1... | collective-permute-start | bytes 9437192 | tf_op jit(solution)/shard_map/ppermute | solution.py:410
  11.9 5.7 %collective-permute-start.6 = (bf16[16,16,256]{2,1,0:T(8,128)(2,1)S(1)}, bf16[16,16,256]{2,1,0:T(8,128)(2,1)S(1)}, u32[]{:S(2)}, u32[]{:S(2)}) collective-permute-start(bf16[16,16,256]{2,1,0:T(8,128)(2,1)S(1)} %get-tuple-element.33.sent_before.refs_1_), channel_id=1, source_target_pairs={{0,8},{4,12},{8,0},{12,4},{1,9},{5,13},{9,1},{13,5},{2,10},{6,14},... | collective-permute-start | bytes 393224 | tf_op jit(solution)/shard_map/ppermute | solution.py:413
  15.0 5.4 %collective-permute-start.11 = (bf16[16,16,256]{2,1,0:T(8,128)(2,1)S(1)}, bf16[16,16,256]{2,1,0:T(8,128)(2,1)S(1)}, u32[]{:S(2)}, u32[]{:S(2)}) collective-permute-start(bf16[16,16,256]{2,1,0:T(8,128)(2,1)S(1)} %get-tuple-element.38), channel_id=1, source_target_pairs={{0,8},{4,12},{8,0},{12,4},{1,9},{5,13},{9,1},{13,5},{2,10},{6,14},... | collective-permute-start | bytes 393224 | tf_op jit(solution)/shard_map/ppermute | solution.py:413
  17.6 2.8 %collective-permute-start.10 = (bf16[16,16,256]{2,1,0:T(8,128)(2,1)S(1)}, bf16[16,16,256]{2,1,0:T(8,128)(2,1)S(1)}, u32[]{:S(2)}, u32[]{:S(2)}) collective-permute-start(bf16[16,16,256]{2,1,0:T(8,128)(2,1)S(1)} %settle.2.current), channel_id=1, source_target_pairs={{0,4},{4,0},{8,12},{12,8},{1,5},{5,1},{9,13},{13,9},{2,6},{6,2},{1... | collective-permute-start | bytes 393224 | tf_op jit(solution)/shard_map/ppermute | solution.py:410
  18.2 3.8 %collective-permute-start.7 = (bf16[2,16,256]{2,1,0:T(8,128)(2,1)S(1)}, bf16[2,16,256]{2,1,0:T(8,128)(2,1)S(1)}, u32[]{:S(2)}, u32[]{:S(2)}) collective-permute-start(bf16[2,16,256]{2,1,0:T(8,128)(2,1)S(1)} %coeffs.1.refs_0_.others_0_), channel_id=1, source_target_pairs={{0,8},{4,12},{8,0},{12,4},{1,9},{5,13},{9,1},{13,5},{2,10},{6,14},... | collective-permute-start | bytes 49160 | tf_op jit(solution)/shard_map/ppermute | solution.py:413
  20.4 1.5 %collective-permute-start.12 = (bf16[16,16,256]{2,1,0:T(8,128)(2,1)S(1)}, bf16[16,16,256]{2,1,0:T(8,128)(2,1)S(1)}, u32[]{:S(2)}, u32[]{:S(2)}) collective-permute-start(bf16[16,16,256]{2,1,0:T(8,128)(2,1)S(1)} %settle.3.column), channel_id=1, source_target_pairs={{0,4},{4,0},{8,12},{12,8},{1,5},{5,1},{9,13},{13,9},{2,6},{6,2},{1... | collective-permute-start | bytes 393224 | tf_op jit(solution)/shard_map/ppermute | solution.py:410
  22.0 3.3 %collective-permute-start.8 = (bf16[4,16,256]{2,1,0:T(8,128)(2,1)S(1)}, bf16[4,16,256]{2,1,0:T(8,128)(2,1)S(1)}, u32[]{:S(2)}, u32[]{:S(2)}) collective-permute-start(bf16[4,16,256]{2,1,0:T(8,128)(2,1)S(1)} %pad_maximum_fusion), channel_id=1, source_target_pairs={{0,4},{4,0},{8,12},{12,8},{1,5},{5,1},{9,13},{13,9},{2,6},{6,2},{1... | collective-permute-start | bytes 98312 | tf_op jit(solution)/shard_map/ppermute | solution.py:410
  23.0 4.6 %collective-permute-start.13 = (bf16[16,16,128]{2,1,0:T(8,128)(2,1)S(1)}, bf16[16,16,128]{2,1,0:T(8,128)(2,1)S(1)}, u32[]{:S(2)}, u32[]{:S(2)}) collective-permute-start(bf16[16,16,128]{2,1,0:T(8,128)(2,1)S(1)} %get-tuple-element.40), channel_id=1, source_target_pairs={{0,8},{4,12},{8,0},{12,4},{1,9},{5,13},{9,1},{13,5},{2,10},{6,14},... | collective-permute-start | bytes 196616 | tf_op jit(solution)/shard_map/ppermute | solution.py:413
  24.8 2.8 %collective-permute-start.14 = (bf16[16,16,128]{2,1,0:T(8,128)(2,1)S(1)}, bf16[16,16,128]{2,1,0:T(8,128)(2,1)S(1)}, u32[]{:S(2)}, u32[]{:S(2)}) collective-permute-start(bf16[16,16,128]{2,1,0:T(8,128)(2,1)S(1)} %get-tuple-element.41), channel_id=1, source_target_pairs={{0,4},{4,0},{8,12},{12,8},{1,5},{5,1},{9,13},{13,9},{2,6},{6,2},{1... | collective-permute-start | bytes 196616 | tf_op jit(solution)/shard_map/ppermute | solution.py:410
  25.0 4.0 %collective-permute-start.15 = (bf16[16,16,128]{2,1,0:T(8,128)(2,1)S(1)}, bf16[16,16,128]{2,1,0:T(8,128)(2,1)S(1)}, u32[]{:S(2)}, u32[]{:S(2)}) collective-permute-start(bf16[16,16,128]{2,1,0:T(8,128)(2,1)S(1)} %get-tuple-element.42), channel_id=1, source_target_pairs={{0,12},{4,8},{8,4},{12,0},{1,13},{5,9},{9,5},{13,1},{2,14},{6,10},... | collective-permute-start | bytes 196616 | tf_op jit(solution)/shard_map/ppermute | solution.py:564

commit v7 on v6

--- a/solution.py
+++ b/solution.py
@@ -131,20 +131,20 @@
 ):
     copies = load_all(
         sems,
+        (column_basis, basis_held),
+        (vectors, current),
+        (column_transfer, transfer_held),
         (source_home, source),
         (target_home, target),
         (block_local, local),
         (far_source, far),
-        (vectors, current),
-        (column_basis, basis_held),
-        (column_transfer, transfer_held),
-    )
-    for copy in copies[:4]:
+    )
+    for copy in copies[3:]:
         copy.wait()
     place_table(columns, vectors.shape[0], source, target, local, far, values, places)
     placed = pltpu.make_async_copy(values, table, sems.at[7])
     placed.start()
-    for copy in copies[4:]:
+    for copy in copies[:3]:
         copy.wait()
     parent_coeffs(current, basis_held, transfer_held, packed, 0)
     placed.wait()

time: 29.9 us -> 29.9 us (level)
  no operation moved by 1% of the time
where the time goes in v7:
time: 29.9 us; the launch traced here: 29.7 us
  starting transfers between devices  11 us (37%)
  Pallas kernels  9.48 us (32%)
  waiting for transfers between devices  8.93 us (30%)
    ppermute x6, starting transfers between devices, to_column(): lax.ppermute(x, 'loop', [(i, (i + 2 * shift) % count) for i in range(coun...  9.34 us
    ppermute x6, waiting for transfers between devices, to_column(): lax.ppermute(x, 'loop', [(i, (i + 2 * shift) % count) for i in range(coun...  6.1 us
    pallas_call x1, Pallas kernels, on_device(): first_call(*in_hbm(*raw, vectors, column_basis, column_transfer))  1.91 us
    pallas_call x1, Pallas kernels, on_device(): mine, theirs = turn_call(*in_vmem(near_tiles))  1.68 us
    ppermute x9, starting transfers between devices, to_sibling(): return lax.ppermute(x, 'loop', sibling)  1.48 us
    ppermute x1, waiting for transfers between devices, on_device(): lax.ppermute(diagonal, 'loop', [(i, i ^ 3) for i in range(count)])  1.45 us
    ppermute x9, waiting for transfers between devices, to_sibling(): return lax.ppermute(x, 'loop', sibling)  1.39 us
    pallas_call x2, Pallas kernels, far_call(): call(functools.partial(far_kernel, tuple(starts), rows), 'far', panels(cl...  1.12 us
  transfers between devices with their start and end apart: 16, of which 8 were waited for; matrix products, arithmetic and copies ran while one was open for 0% of the time, Pallas kernels for 26%

profile of v7, /device:TPU:0, one launch (start us, length us, event | category | flops | bytes accessed | tf_op | source)
XLA Modules:
  0.0 29.7 jit_solution(16009449398347937068)
XLA Ops:
  0.0 3.0 %collective-permute-start.1 = (bf16[16,16,256]{2,1,0:T(8,128)(2,1)}, bf16[16,16,256]{2,1,0:T(8,128)(2,1)S(1)}, u32[]{:S(2)}, u32[]{:S(2)}) collective-permute-start(bf16[16,16,256]{2,1,0:T(8,128)(2,1)} %vectors.1), channel_id=1, source_target_pairs={{0,8},{4,12},{8,0},{12,4},{1,9},{5,13},{9,1},{13,5},{2,10},{6,14},... | collective-permute-start | bytes 393224 | tf_op jit(solution)/shard_map/ppermute | solution.py:413
  3.0 1.9 %first.1 = (bf16[2,16,256]{2,1,0:T(8,128)(2,1)S(1)}, bf16[16,16,256]{2,1,0:T(8,128)(2,1)S(1)}, s32[8,128]{1,0:T(8,128)S(1)}, s32[16,128]{1,0:T(8,128)S(4)}) custom-call(s32[1,48]{1,0:T(1,128)} %bitcast.4, s32[1,48]{1,0:T(1,128)} %bitcast.5, s32[2,48]{1,0:T(2,128)} %bitcast.3, s32[8,8]{1,0:T(8,128)} %far_source.1, bf16[16,16,256]{2,1,0:T(8,128)(2,1)} %vectors.1, ...), custom_call_target="tpu_custom_call" | custom-call | flops 10000000000 | tf_op jit(solution)/shard_map/first/pallas_call | solution.py:520
  4.9 0.1 collective-permute-start.2
  5.0 0.1 collective-permute-start.4
  5.0 0.4 %collective-permute-start = (bf16[16,16,256]{2,1,0:T(8,128)(2,1)S(1)}, bf16[16,16,256]{2,1,0:T(8,128)(2,1)S(1)}, u32[]{:S(2)}, u32[]{:S(2)}) collective-permute-start(bf16[16,16,256]{2,1,0:T(8,128)(2,1)S(1)} %get-tuple-element.27.refs_0_.current), channel_id=1, source_target_pairs={{0,4},{4,0},{8,12},{12,8},{1,5},{5,1},{9,13},{13,9},{2,6},{6,2},{1... | collective-permute-start | bytes 393224 | tf_op jit(solution)/shard_map/ppermute | solution.py:410
  5.5 1.2 %collective-permute-done.1.refs_2_ = bf16[16,16,256]{2,1,0:T(8,128)(2,1)S(1)} collective-permute-done((bf16[16,16,256]{2,1,0:T(8,128)(2,1)}, bf16[16,16,256]{2,1,0:T(8,128)(2,1)S(1)}, u32[]{:S(2)}, u32[]{:S(2)}) %collective-permute-start.1) | collective-permute-done | bytes 131104 | tf_op jit(solution)/shard_map/ppermute | solution.py:413
  6.7 0.0 collective-permute-done.2.refs_2_.places_beside
  6.7 0.1 collective-permute-start.3
  6.8 1.7 %turn.1 = (bf16[48,256,128]{2,1,0:T(8,128)(2,1)S(1)}, bf16[48,256,128]{2,1,0:T(8,128)(2,1)S(1)}) custom-call(bf16[48,256,256]{2,1,0:T(8,128)(2,1)S(1)} %copy-done.4), custom_call_target="tpu_custom_call" | custom-call | flops 2500000000 | tf_op jit(solution)/shard_map/turn/pallas_call | solution.py:526
  8.5 0.3 collective-permute-done.4.refs_5_.refs_2_
  8.8 0.0 collective-permute-done.refs_1_
  8.8 0.0 collective-permute-done.3.refs_3_
  8.8 1.0 %near.1 = (bf16[36,16,256]{2,1,0:T(8,128)(2,1)S(1)}, f32[16,16,256]{2,1,0:T(8,128)S(1)}, f32[16,16,256]{2,1,0:T(8,128)S(1)}) custom-call(s32[16,128]{1,0:T(8,128)S(4)} %get-tuple-element.24.table, bf16[48,256,128]{2,1,0:T(8,128)(2,1)S(1)} %get-tuple-element.25.mine, bf16[48,256,128]{2,1,0:T(8,128)(2,1)S(1)} %get-tuple-element.26.theirs.refs_0_, ...), custom_call_target="tpu_custom_call" | custom-call | flops 1000000000 | tf_op jit(solution)/shard_map/near/pallas_call | solution.py:452
  9.8 0.3 collective-permute-start.5
  10.1 1.4 %collective-permute-done.5.arrived.refs_1_.refs_3_ = bf16[36,16,256]{2,1,0:T(8,128)(2,1)S(1)} collective-permute-done((bf16[36,16,256]{2,1,0:T(8,128)(2,1)S(1)}, bf16[36,16,256]{2,1,0:T(8,128)(2,1)S(1)}, u32[]{:S(2)}, u32[]{:S(2)}) %collective-permute-start.5) | collective-permute-done | bytes 294944 | tf_op jit(solution)/shard_map/ppermute | solution.py:410
  11.5 0.0 copy-start.1
  11.5 0.0 copy-start.2
  11.5 0.0 copy-start.3
  11.5 0.0 copy-start
  11.6 0.0 copy-start.5
  11.6 0.0 copy-start.6
  11.6 0.3 collective-permute-start.9
  11.9 1.7 %collective-permute-start.6 = (bf16[16,16,256]{2,1,0:T(8,128)(2,1)S(1)}, bf16[16,16,256]{2,1,0:T(8,128)(2,1)S(1)}, u32[]{:S(2)}, u32[]{:S(2)}) collective-permute-start(bf16[16,16,256]{2,1,0:T(8,128)(2,1)S(1)} %get-tuple-element.33.sent_before.refs_1_), channel_id=1, source_target_pairs={{0,8},{4,12},{8,0},{12,4},{1,9},{5,13},{9,1},{13,5},{2,10},{6,14},... | collective-permute-start | bytes 393224 | tf_op jit(solution)/shard_map/ppermute | solution.py:413
  13.6 0.6 %far.2.far_part = f32[16,16,256]{2,1,0:T(8,128)S(1)} custom-call(s32[16,128]{1,0:T(8,128)S(4)} %get-tuple-element.24.table, bf16[16,64,64]{2,1,0:T(8,128)(2,1)S(1)} %copy-done.3, bf16[16,64,256]{2,1,0:T(8,128)(2,1)S(1)} %copy-done.1, bf16[8,64,512]{2,1,0:T(8,128)(2,1)S(1)} %copy-done.2, bf16[2,16,256]{2,1,0:T(8,128)(2,1)S(1)} %get-tuple-element.28.refs_1_.refs_4_.refs_0_, ...), custom_call_target="tpu_custom_call" | custom-call | flops 500000000 | tf_op jit(solution)/shard_map/far/pallas_call | solution.py:497
  14.2 0.0 copy-done
  14.2 0.7 %first_self.1 = (f32[16,16,256]{2,1,0:T(8,128)S(1)}, s32[16,128]{1,0:T(8,128)S(4)}) custom-call(bf16[16,16,256]{2,1,0:T(8,128)(2,1)S(1)} %get-tuple-element.27.refs_0_.current, bf16[16,256,256]{2,1,0:T(8,128)(2,1)S(1)} %copy-done, s32[8,128]{1,0:T(8,128)S(1)} %get-tuple-element.29.places, s32[8,128]{1,0:T(8,128)S(1)} %collective-permute-done.2.refs_2_.places_beside, ...), custom_call_target="tpu_custom_call" | custom-call | flops 600000000 | tf_op jit(solution)/shard_map/first_self/pallas_call | solution.py:540
  14.9 0.1 own.1
  15.0 1.0 %collective-permute-start.11 = (bf16[16,16,256]{2,1,0:T(8,128)(2,1)S(1)}, bf16[16,16,256]{2,1,0:T(8,128)(2,1)S(1)}, u32[]{:S(2)}, u32[]{:S(2)}) collective-permute-start(bf16[16,16,256]{2,1,0:T(8,128)(2,1)S(1)} %get-tuple-element.38), channel_id=1, source_target_pairs={{0,8},{4,12},{8,0},{12,4},{1,9},{5,13},{9,1},{13,5},{2,10},{6,14},... | collective-permute-start | bytes 393224 | tf_op jit(solution)/shard_map/ppermute | solution.py:413
  16.0 1.6 %collective-permute-done.6.message = bf16[16,16,256]{2,1,0:T(8,128)(2,1)S(1)} collective-permute-done((bf16[16,16,256]{2,1,0:T(8,128)(2,1)S(1)}, bf16[16,16,256]{2,1,0:T(8,128)(2,1)S(1)}, u32[]{:S(2)}, u32[]{:S(2)}) %collective-permute-start.6) | collective-permute-done | bytes 131104 | tf_op jit(solution)/shard_map/ppermute | solution.py:413
  17.6 0.1 collective-permute-start.10
  17.7 0.5 %coeffs.1.refs_0_.others_0_ = bf16[2,16,256]{2,1,0:T(8,128)(2,1)S(1)} custom-call(bf16[16,16,256]{2,1,0:T(8,128)(2,1)S(1)} %settle.2.current, bf16[16,64,256]{2,1,0:T(8,128)(2,1)S(1)} %copy-done.5, bf16[16,64,64]{2,1,0:T(8,128)(2,1)S(1)} %copy-done.6), custom_call_target="tpu_custom_call" | custom-call | flops 500000000 | tf_op jit(solution)/shard_map/coeffs/pallas_call | solution.py:557
  18.2 1.8 %collective-permute-start.7 = (bf16[2,16,256]{2,1,0:T(8,128)(2,1)S(1)}, bf16[2,16,256]{2,1,0:T(8,128)(2,1)S(1)}, u32[]{:S(2)}, u32[]{:S(2)}) collective-permute-start(bf16[2,16,256]{2,1,0:T(8,128)(2,1)S(1)} %coeffs.1.refs_0_.others_0_), channel_id=1, source_target_pairs={{0,8},{4,12},{8,0},{12,4},{1,9},{5,13},{9,1},{13,5},{2,10},{6,14},... | collective-permute-start | bytes 49160 | tf_op jit(solution)/shard_map/ppermute | solution.py:413
  19.9 0.4 %collective-permute-done.11.message = bf16[16,16,256]{2,1,0:T(8,128)(2,1)S(1)} collective-permute-done((bf16[16,16,256]{2,1,0:T(8,128)(2,1)S(1)}, bf16[16,16,256]{2,1,0:T(8,128)(2,1)S(1)}, u32[]{:S(2)}, u32[]{:S(2)}) %collective-permute-start.11) | collective-permute-done | bytes 131104 | tf_op jit(solution)/shard_map/ppermute | solution.py:413
  20.4 0.0 collective-permute-done.10.others_1_.current_beside
  20.4 0.1 collective-permute-start.12
  20.5 0.6 %self.1.self_part = f32[16,16,256]{2,1,0:T(8,128)S(1)} custom-call(bf16[16,16,256]{2,1,0:T(8,128)(2,1)S(1)} %settle.2.current, bf16[16,256,256]{2,1,0:T(8,128)(2,1)S(1)} %copy-done), custom_call_target="tpu_custom_call" | custom-call | flops 600000000 | tf_op jit(solution)/shard_map/self/pallas_call | solution.py:447
  21.1 0.8 %collective-permute-done.7.refs_2_ = bf16[2,16,256]{2,1,0:T(8,128)(2,1)S(1)} collective-permute-done((bf16[2,16,256]{2,1,0:T(8,128)(2,1)S(1)}, bf16[2,16,256]{2,1,0:T(8,128)(2,1)S(1)}, u32[]{:S(2)}, u32[]{:S(2)}) %collective-permute-start.7) | collective-permute-done | bytes 16416 | tf_op jit(solution)/shard_map/ppermute | solution.py:413
  21.9 0.0 collective-permute-start.8
  21.9 0.0 collective-permute-done.12.column_beside
  21.9 0.0 collective-permute-done.9.beside
  21.9 1.0 %half.1 = (bf16[16,16,128]{2,1,0:T(8,128)(2,1)S(1)}, bf16[16,16,128]{2,1,0:T(8,128)(2,1)S(1)}, bf16[16,16,128]{2,1,0:T(8,128)(2,1)S(1)}, f32[16,16,128]{2,1,0:T(8,128)S(1)}) custom-call(s32[16,128]{1,0:T(8,128)S(4)} %get-tuple-element.36.table, bf16[48,256,128]{2,1,0:T(8,128)(2,1)S(1)} %get-tuple-element.25.mine, ...), custom_call_target="tpu_custom_call" | custom-call | flops 1000000000 | tf_op jit(solution)/shard_map/half/pallas_call | solution.py:560
  23.0 1.8 %collective-permute-start.13 = (bf16[16,16,128]{2,1,0:T(8,128)(2,1)S(1)}, bf16[16,16,128]{2,1,0:T(8,128)(2,1)S(1)}, u32[]{:S(2)}, u32[]{:S(2)}) collective-permute-start(bf16[16,16,128]{2,1,0:T(8,128)(2,1)S(1)} %get-tuple-element.40), channel_id=1, source_target_pairs={{0,8},{4,12},{8,0},{12,4},{1,9},{5,13},{9,1},{13,5},{2,10},{6,14},... | collective-permute-start | bytes 196616 | tf_op jit(solution)/shard_map/ppermute | solution.py:413
  24.8 0.2 collective-permute-start.14
  25.0 0.2 collective-permute-start.15
  25.2 0.6 %far.3.far_part = f32[16,16,256]{2,1,0:T(8,128)S(1)} custom-call(s32[16,128]{1,0:T(8,128)S(4)} %get-tuple-element.24.table, bf16[16,64,64]{2,1,0:T(8,128)(2,1)S(1)} %copy-done.3, bf16[16,64,256]{2,1,0:T(8,128)(2,1)S(1)} %copy-done.1, bf16[8,64,512]{2,1,0:T(8,128)(2,1)S(1)} %copy-done.2, bf16[2,16,256]{2,1,0:T(8,128)(2,1)S(1)} %coeffs.1.refs_0_.others_0_, ...), custom_call_target="tpu_custom_call" | custom-call | flops 500000000 | tf_op jit(solution)/shard_map/far/pallas_call | solution.py:497
  25.8 1.8 %collective-permute-done.13.crossed = bf16[16,16,128]{2,1,0:T(8,128)(2,1)S(1)} collective-permute-done((bf16[16,16,128]{2,1,0:T(8,128)(2,1)S(1)}, bf16[16,16,128]{2,1,0:T(8,128)(2,1)S(1)}, u32[]{:S(2)}, u32[]{:S(2)}) %collective-permute-start.13) | collective-permute-done | bytes 65568 | tf_op jit(solution)/shard_map/ppermute | solution.py:413
  27.5 1.4 %collective-permute-done.15.diagonal = bf16[16,16,128]{2,1,0:T(8,128)(2,1)S(1)} collective-permute-done((bf16[16,16,128]{2,1,0:T(8,128)(2,1)S(1)}, bf16[16,16,128]{2,1,0:T(8,128)(2,1)S(1)}, u32[]{:S(2)}, u32[]{:S(2)}) %collective-permute-start.15) | collective-permute-done | bytes 65568 | tf_op jit(solution)/shard_map/ppermute | solution.py:564
  29.0 0.7 %last.1 = bf16[16,16,256]{2,1,0:T(8,128)(2,1)} custom-call(f32[16,16,256]{2,1,0:T(8,128)S(1)} %self.1.self_part, f32[16,16,256]{2,1,0:T(8,128)S(1)} %far.3.far_part, f32[16,16,128]{2,1,0:T(8,128)S(1)} %get-tuple-element.39.keep, bf16[16,16,128]{2,1,0:T(8,128)(2,1)S(1)} %collective-permute-done.13.crossed, ...), custom_call_target="tpu_custom_call" | custom-call | flops 100000000 | tf_op jit(solution)/shard_map/last/pallas_call | solution.py:567
  (17 shorter events, 0.1 us)
Async XLA Ops:
  0.0 6.7 %collective-permute-start.1 = (bf16[16,16,256]{2,1,0:T(8,128)(2,1)}, bf16[16,16,256]{2,1,0:T(8,128)(2,1)S(1)}, u32[]{:S(2)}, u32[]{:S(2)}) collective-permute-start(bf16[16,16,256]{2,1,0:T(8,128)(2,1)} %vectors.1), channel_id=1, source_target_pairs={{0,8},{4,12},{8,0},{12,4},{1,9},{5,13},{9,1},{13,5},{2,10},{6,14},... | collective-permute-start | bytes 393224 | tf_op jit(solution)/shard_map/ppermute | solution.py:413
  3.0 3.8 %copy-start.4 = (bf16[48,256,256]{2,1,0:T(8,128)(2,1)S(1)}, bf16[48,256,256]{2,1,0:T(8,128)(2,1)}, u32[]{:S(2)}) copy-start(bf16[48,256,256]{2,1,0:T(8,128)(2,1)} %tiles.1) | copy-start | bytes 18874372
  4.9 1.8 %collective-permute-start.2 = (s32[8,128]{1,0:T(8,128)S(1)}, s32[8,128]{1,0:T(8,128)S(1)}, u32[]{:S(2)}, u32[]{:S(2)}) collective-permute-start(s32[8,128]{1,0:T(8,128)S(1)} %get-tuple-element.29.places), channel_id=1, source_target_pairs={{0,4},{4,0},{8,12},{12,8},{1,5},{5,1},{9,13},{13,9},{2,6},{6,2},{1... | collective-permute-start | bytes 12296 | tf_op jit(solution)/shard_map/ppermute | solution.py:410
  5.0 3.8 %collective-permute-start.4 = (bf16[2,16,256]{2,1,0:T(8,128)(2,1)S(1)}, bf16[2,16,256]{2,1,0:T(8,128)(2,1)S(1)}, u32[]{:S(2)}, u32[]{:S(2)}) collective-permute-start(bf16[2,16,256]{2,1,0:T(8,128)(2,1)S(1)} %get-tuple-element.28.refs_1_.refs_4_.refs_0_), channel_id=1, source_target_pairs={{0,8},{4,12},{8,0},{12,4},{1,9},{5,13},{9,1},{13,5},{2,10},{6,14},... | collective-permute-start | bytes 49160 | tf_op jit(solution)/shard_map/ppermute | solution.py:413
  5.0 3.7 %collective-permute-start = (bf16[16,16,256]{2,1,0:T(8,128)(2,1)S(1)}, bf16[16,16,256]{2,1,0:T(8,128)(2,1)S(1)}, u32[]{:S(2)}, u32[]{:S(2)}) collective-permute-start(bf16[16,16,256]{2,1,0:T(8,128)(2,1)S(1)} %get-tuple-element.27.refs_0_.current), channel_id=1, source_target_pairs={{0,4},{4,0},{8,12},{12,8},{1,5},{5,1},{9,13},{13,9},{2,6},{6,2},{1... | collective-permute-start | bytes 393224 | tf_op jit(solution)/shard_map/ppermute | solution.py:410
  6.7 2.1 %collective-permute-start.3 = (bf16[16,16,256]{2,1,0:T(8,128)(2,1)S(1)}, bf16[16,16,256]{2,1,0:T(8,128)(2,1)S(1)}, u32[]{:S(2)}, u32[]{:S(2)}) collective-permute-start(bf16[16,16,256]{2,1,0:T(8,128)(2,1)S(1)} %tie.2), channel_id=1, source_target_pairs={{0,4},{4,0},{8,12},{12,8},{1,5},{5,1},{9,13},{13,9},{2,6},{6,2},{1... | collective-permute-start | bytes 393224 | tf_op jit(solution)/shard_map/ppermute | solution.py:410
  9.8 1.6 %collective-permute-start.5 = (bf16[36,16,256]{2,1,0:T(8,128)(2,1)S(1)}, bf16[36,16,256]{2,1,0:T(8,128)(2,1)S(1)}, u32[]{:S(2)}, u32[]{:S(2)}) collective-permute-start(bf16[36,16,256]{2,1,0:T(8,128)(2,1)S(1)} %get-tuple-element.31), channel_id=1, source_target_pairs={{0,4},{4,0},{8,12},{12,8},{1,5},{5,1},{9,13},{13,9},{2,6},{6,2},{1... | collective-permute-start | bytes 884744 | tf_op jit(solution)/shard_map/ppermute | solution.py:410
  11.5 2.1 %copy-start.1 = (bf16[16,64,256]{2,1,0:T(8,128)(2,1)S(1)}, bf16[16,64,256]{2,1,0:T(8,128)(2,1)}, u32[]{:S(2)}) copy-start(bf16[16,64,256]{2,1,0:T(8,128)(2,1)} %row_basis.3) | copy-start | bytes 1572868
  11.5 2.1 %copy-start.2 = (bf16[8,64,512]{2,1,0:T(8,128)(2,1)S(1)}, bf16[8,64,512]{2,1,0:T(8,128)(2,1)}, u32[]{:S(2)}) copy-start(bf16[8,64,512]{2,1,0:T(8,128)(2,1)} %coupling.3) | copy-start | bytes 1572868
  11.5 2.1 %copy-start.3 = (bf16[16,64,64]{2,1,0:T(8,128)(2,1)S(1)}, bf16[16,64,64]{2,1,0:T(8,128)(2,1)}, u32[]{:S(2)}) copy-start(bf16[16,64,64]{2,1,0:T(8,128)(2,1)} %row_transfer.3) | copy-start | bytes 393220
  11.5 2.7 %copy-start = (bf16[16,256,256]{2,1,0:T(8,128)(2,1)S(1)}, bf16[16,256,256]{2,1,0:T(8,128)(2,1)}, u32[]{:S(2)}) copy-start(bf16[16,256,256]{2,1,0:T(8,128)(2,1)} %self_tiles.3) | copy-start | bytes 6291460
  11.6 6.1 %copy-start.5 = (bf16[16,64,256]{2,1,0:T(8,128)(2,1)S(1)}, bf16[16,64,256]{2,1,0:T(8,128)(2,1)}, u32[]{:S(2)}) copy-start(bf16[16,64,256]{2,1,0:T(8,128)(2,1)} %column_basis.3) | copy-start | bytes 1572868
  11.6 6.1 %copy-start.6 = (bf16[16,64,64]{2,1,0:T(8,128)(2,1)S(1)}, bf16[16,64,64]{2,1,0:T(8,128)(2,1)}, u32[]{:S(2)}) copy-start(bf16[16,64,64]{2,1,0:T(8,128)(2,1)} %column_transfer.3) | copy-start | bytes 393220
  11.6 10.4 %collective-permute-start.9 = (bf16[48,256,128]{2,1,0:T(8,128)(2,1)S(1)}, bf16[48,256,128]{2,1,0:T(8,128)(2,1)S(1)}, u32[]{:S(2)}, u32[]{:S(2)}) collective-permute-start(bf16[48,256,128]{2,1,0:T(8,128)(2,1)S(1)} %tie.3), channel_id=1, source_target_pairs={{0,4},{4,0},{8,12},{12,8},{1,5},{5,1},{9,13},{13,9},{2,6},{6,2},{1... | collective-permute-start | bytes 9437192 | tf_op jit(solution)/shard_map/ppermute | solution.py:410
  11.9 5.7 %collective-permute-start.6 = (bf16[16,16,256]{2,1,0:T(8,128)(2,1)S(1)}, bf16[16,16,256]{2,1,0:T(8,128)(2,1)S(1)}, u32[]{:S(2)}, u32[]{:S(2)}) collective-permute-start(bf16[16,16,256]{2,1,0:T(8,128)(2,1)S(1)} %get-tuple-element.33.sent_before.refs_1_), channel_id=1, source_target_pairs={{0,8},{4,12},{8,0},{12,4},{1,9},{5,13},{9,1},{13,5},{2,10},{6,14},... | collective-permute-start | bytes 393224 | tf_op jit(solution)/shard_map/ppermute | solution.py:413
  15.0 5.4 %collective-permute-start.11 = (bf16[16,16,256]{2,1,0:T(8,128)(2,1)S(1)}, bf16[16,16,256]{2,1,0:T(8,128)(2,1)S(1)}, u32[]{:S(2)}, u32[]{:S(2)}) collective-permute-start(bf16[16,16,256]{2,1,0:T(8,128)(2,1)S(1)} %get-tuple-element.38), channel_id=1, source_target_pairs={{0,8},{4,12},{8,0},{12,4},{1,9},{5,13},{9,1},{13,5},{2,10},{6,14},... | collective-permute-start | bytes 393224 | tf_op jit(solution)/shard_map/ppermute | solution.py:413
  17.6 2.8 %collective-permute-start.10 = (bf16[16,16,256]{2,1,0:T(8,128)(2,1)S(1)}, bf16[16,16,256]{2,1,0:T(8,128)(2,1)S(1)}, u32[]{:S(2)}, u32[]{:S(2)}) collective-permute-start(bf16[16,16,256]{2,1,0:T(8,128)(2,1)S(1)} %settle.2.current), channel_id=1, source_target_pairs={{0,4},{4,0},{8,12},{12,8},{1,5},{5,1},{9,13},{13,9},{2,6},{6,2},{1... | collective-permute-start | bytes 393224 | tf_op jit(solution)/shard_map/ppermute | solution.py:410
  18.2 3.8 %collective-permute-start.7 = (bf16[2,16,256]{2,1,0:T(8,128)(2,1)S(1)}, bf16[2,16,256]{2,1,0:T(8,128)(2,1)S(1)}, u32[]{:S(2)}, u32[]{:S(2)}) collective-permute-start(bf16[2,16,256]{2,1,0:T(8,128)(2,1)S(1)} %coeffs.1.refs_0_.others_0_), channel_id=1, source_target_pairs={{0,8},{4,12},{8,0},{12,4},{1,9},{5,13},{9,1},{13,5},{2,10},{6,14},... | collective-permute-start | bytes 49160 | tf_op jit(solution)/shard_map/ppermute | solution.py:413
  20.4 1.5 %collective-permute-start.12 = (bf16[16,16,256]{2,1,0:T(8,128)(2,1)S(1)}, bf16[16,16,256]{2,1,0:T(8,128)(2,1)S(1)}, u32[]{:S(2)}, u32[]{:S(2)}) collective-permute-start(bf16[16,16,256]{2,1,0:T(8,128)(2,1)S(1)} %settle.3.column), channel_id=1, source_target_pairs={{0,4},{4,0},{8,12},{12,8},{1,5},{5,1},{9,13},{13,9},{2,6},{6,2},{1... | collective-permute-start | bytes 393224 | tf_op jit(solution)/shard_map/ppermute | solution.py:410
  21.9 3.3 %collective-permute-start.8 = (bf16[4,16,256]{2,1,0:T(8,128)(2,1)S(1)}, bf16[4,16,256]{2,1,0:T(8,128)(2,1)S(1)}, u32[]{:S(2)}, u32[]{:S(2)}) collective-permute-start(bf16[4,16,256]{2,1,0:T(8,128)(2,1)S(1)} %pad_maximum_fusion), channel_id=1, source_target_pairs={{0,4},{4,0},{8,12},{12,8},{1,5},{5,1},{9,13},{13,9},{2,6},{6,2},{1... | collective-permute-start | bytes 98312 | tf_op jit(solution)/shard_map/ppermute | solution.py:410
  23.0 4.6 %collective-permute-start.13 = (bf16[16,16,128]{2,1,0:T(8,128)(2,1)S(1)}, bf16[16,16,128]{2,1,0:T(8,128)(2,1)S(1)}, u32[]{:S(2)}, u32[]{:S(2)}) collective-permute-start(bf16[16,16,128]{2,1,0:T(8,128)(2,1)S(1)} %get-tuple-element.40), channel_id=1, source_target_pairs={{0,8},{4,12},{8,0},{12,4},{1,9},{5,13},{9,1},{13,5},{2,10},{6,14},... | collective-permute-start | bytes 196616 | tf_op jit(solution)/shard_map/ppermute | solution.py:413
  24.8 2.8 %collective-permute-start.14 = (bf16[16,16,128]{2,1,0:T(8,128)(2,1)S(1)}, bf16[16,16,128]{2,1,0:T(8,128)(2,1)S(1)}, u32[]{:S(2)}, u32[]{:S(2)}) collective-permute-start(bf16[16,16,128]{2,1,0:T(8,128)(2,1)S(1)} %get-tuple-element.41), channel_id=1, source_target_pairs={{0,4},{4,0},{8,12},{12,8},{1,5},{5,1},{9,13},{13,9},{2,6},{6,2},{1... | collective-permute-start | bytes 196616 | tf_op jit(solution)/shard_map/ppermute | solution.py:410
  25.0 4.0 %collective-permute-start.15 = (bf16[16,16,128]{2,1,0:T(8,128)(2,1)S(1)}, bf16[16,16,128]{2,1,0:T(8,128)(2,1)S(1)}, u32[]{:S(2)}, u32[]{:S(2)}) collective-permute-start(bf16[16,16,128]{2,1,0:T(8,128)(2,1)S(1)} %get-tuple-element.42), channel_id=1, source_target_pairs={{0,12},{4,8},{8,4},{12,0},{1,13},{5,9},{9,5},{13,1},{2,14},{6,10},... | collective-permute-start | bytes 196616 | tf_op jit(solution)/shard_map/ppermute | solution.py:564
